TPU v7x, 32 devices: a whole 2x2x4 slice. The times are simulated.
32 devices in a mesh: col: 4 (over z), row: 8 (over y, x, core).
Axes of the slice: x: 2, y: 2, z: 4, core: 2. Of those that a mesh axis runs over, the one named last changes fastest.
Arguments:
- inputs: bfloat16 [256, 8192], P('row', 'col'), may hold values from -6 to 6
- grad_out: bfloat16 [256, 8192], P('row', 'col'), may hold values from -6 to 6
- gate_pre: bfloat16 [256, 16384], P('col', 'row'), may hold values from -8 to 8
- up_pre: bfloat16 [256, 16384], P('col', 'row'), may hold values from -6 to 6
- gate_weight: bfloat16 [8192, 16384], P('col', 'row'), may hold values from -0.0625 to 0.0625
- up_weight: bfloat16 [8192, 16384], P('col', 'row'), may hold values from -0.0625 to 0.0625
- down_weight: bfloat16 [16384, 8192], P('row', 'col'), may hold values from -0.046875 to 0.046875
Outputs:
- input_grad: bfloat16 [256, 8192], P('row', 'col')
- gate_grad: bfloat16 [8192, 16384], P('col', 'row')
- up_grad: bfloat16 [8192, 16384], P('col', 'row')
- down_grad: bfloat16 [16384, 8192], P('row', 'col')
All inputs are finite; a program needn't handle non-finite values.
Results may differ from a plain program's by a relative error of at most 0.0049.
Values may be sent and summed in bfloat16 or wider, within the bound.
No kernel may reach another device: no remote copies, remote signals or barrier semaphores. Data moves between devices by JAX's collectives and lax.ppermute only.
A program may use at most 128 MiB of HBM per device.

v0:
```python
import math

import jax
import jax.numpy as jnp
from jax import lax
from jax.sharding import PartitionSpec as P


def swiglu_back(hidden_grad, gate_pre, up_pre):
    gate_val = gate_pre.astype(jnp.float32)
    up_val = up_pre.astype(jnp.float32)
    sigmoid_val = jax.nn.sigmoid(gate_val)
    silu_val = gate_val * sigmoid_val
    hidden = (silu_val * up_val).astype(jnp.bfloat16)
    up_term = (hidden_grad * silu_val).astype(jnp.bfloat16)
    gate_term = (
        hidden_grad * up_val * sigmoid_val * (1.0 + gate_val * (1.0 - sigmoid_val))
    ).astype(jnp.bfloat16)
    return (hidden, gate_term, up_term)


def per_device(inputs, grad_out, gate_pre, up_pre, gate_weight, up_weight, down_weight):
    total_tokens = grad_out.shape[0] * lax.axis_size("row")
    grad_scale = 1.0 / math.sqrt(total_tokens)
    grad_all, input_all = (
        lax.all_gather(grad_out, "row", axis=0, tiled=True),
        lax.all_gather(inputs, "row", axis=0, tiled=True),
    )
    partial_hidden = jnp.einsum(
        "td,fd->tf", grad_all, down_weight, preferred_element_type=jnp.float32
    )
    hidden_grad = lax.psum_scatter(partial_hidden, "col", scatter_dimension=0, tiled=True)
    hidden, gate_term, up_term = swiglu_back(hidden_grad, gate_pre, up_pre)
    hidden_all, gate_all, up_all = (
        lax.all_gather(hidden, "col", axis=0, tiled=True),
        lax.all_gather(gate_term, "col", axis=0, tiled=True),
        lax.all_gather(up_term, "col", axis=0, tiled=True),
    )
    down_grad = (
        jnp.einsum("tf,td->fd", hidden_all, grad_all, preferred_element_type=jnp.float32)
        * grad_scale
    ).astype(jnp.bfloat16)
    gate_sum = jnp.einsum("td,tf->df", input_all, gate_all, preferred_element_type=jnp.float32)
    up_sum = jnp.einsum("td,tf->df", input_all, up_all, preferred_element_type=jnp.float32)
    gate_grad = (gate_sum * grad_scale).astype(jnp.bfloat16)
    up_grad = (up_sum * grad_scale).astype(jnp.bfloat16)
    input_grad = lax.psum_scatter(
        jnp.einsum("tf,df->td", gate_all, gate_weight, preferred_element_type=jnp.float32)
        + jnp.einsum("tf,df->td", up_all, up_weight, preferred_element_type=jnp.float32),
        "row",
        scatter_dimension=0,
        tiled=True,
    ).astype(jnp.bfloat16)
    return (input_grad, gate_grad, up_grad, down_grad)


def solution(mesh):
    return jax.shard_map(
        per_device,
        mesh=mesh,
        in_specs=(
            P("row", "col"),
            P("row", "col"),
            P("col", "row"),
            P("col", "row"),
            P("col", "row"),
            P("col", "row"),
            P("row", "col"),
        ),
        out_specs=(P("row", "col"), P("col", "row"), P("col", "row"), P("row", "col")),
        check_vma=False,
    )
```

profile of v0, /device:TPU:0, one launch (start us, length us, event | category | flops | bytes accessed | tf_op | source)
XLA Modules:
  0.0 253.9 jit_solution(6086308613098054272)
XLA Ops:
  7.2 0.0 all-gather.6.cloned.1.call-start
  7.2 0.7 all-gather.6.cloned.1.call-update
  7.9 0.0 reduce-scatter.3.cloned.1.call-start
  8.0 28.1 %all-gather.6.cloned.1.call-done = bf16[256,2048]{1,0:T(8,128)(2,1)} async-done(((bf16[32,2048]{1,0:T(8,128)(2,1)}), bf16[256,2048]{1,0:T(8,128)(2,1)}) %all-gather.6.cloned.1.call-update) | async-done | bytes 1048592 | tf_op jit(solution)/shard_map/all_gather | solution.py:26
  36.1 7.4 %fusion.10 = f32[256,2048]{1,0:T(8,128)} fusion(bf16[256,2048]{1,0:T(8,128)(2,1)} %all-gather.6.cloned.1.call-done, bf16[2048,2048]{1,0:T(8,128)(2,1)} %param.13), kind=kOutput, calls=%fused_computation.20 | convolution fusion | flops 2147483648 | bytes 11534336 | tf_op jit(solution)/shard_map/td,fd->tf/dot_general | solution.py:29
  43.5 0.0 reduce-scatter.3.cloned.1.call-update
  43.5 0.0 all-gather.8.cloned.1.call-start
  43.6 44.0 %reduce-scatter.3.cloned.1.call-done = f32[64,2048]{1,0:T(8,128)} async-done(((f32[256,2048]{1,0:T(8,128)}), f32[64,2048]{1,0:T(8,128)}) %reduce-scatter.3.cloned.1.call-update) | async-done | bytes 524304 | tf_op jit(solution)/shard_map/reduce_scatter | solution.py:32
  87.6 2.2 multiply_convert_fusion.3
  89.7 0.0 all-gather.8.cloned.1.call-update
  89.7 0.0 all-gather.10.cloned.1.call-start
  89.8 0.5 all-gather.10.cloned.1.call-update
  90.3 0.0 all-gather.12.cloned.1.call-start
  90.4 0.5 all-gather.12.cloned.1.call-update
  90.9 0.0 all-gather.14.cloned.1.call-start
  91.0 0.5 all-gather.14.cloned.1.call-update
  91.5 0.2 reduce-scatter.5.cloned.1.call-start
  91.7 25.4 %all-gather.8.cloned.1.call-done = bf16[256,2048]{1,0:T(8,128)(2,1)} async-done(((bf16[64,2048]{1,0:T(8,128)(2,1)}), bf16[256,2048]{1,0:T(8,128)(2,1)}) %all-gather.8.cloned.1.call-update) | async-done | bytes 1048592 | tf_op jit(solution)/shard_map/all_gather | solution.py:36
  117.2 6.1 %fusion.11 = f32[256,2048]{1,0:T(8,128)S(1)} fusion(bf16[256,2048]{1,0:T(8,128)(2,1)} %all-gather.8.cloned.1.call-done, bf16[2048,2048]{1,0:T(8,128)(2,1)} %param.11), kind=kOutput, calls=%fused_computation.21 | convolution fusion | flops 2147483648 | bytes 11534336 | tf_op jit(solution)/shard_map/tf,df->td/dot_general | solution.py:48
  123.3 23.4 %all-gather.10.cloned.1.call-done = bf16[256,2048]{1,0:T(8,128)(2,1)} async-done(((bf16[64,2048]{1,0:T(8,128)(2,1)}), bf16[256,2048]{1,0:T(8,128)(2,1)}) %all-gather.10.cloned.1.call-update) | async-done | bytes 1048592 | tf_op jit(solution)/shard_map/all_gather | solution.py:37
  146.7 7.4 %convolution_add_fusion = f32[256,2048]{1,0:T(8,128)} fusion(f32[256,2048]{1,0:T(8,128)S(1)} %fusion.11, bf16[256,2048]{1,0:T(8,128)(2,1)} %all-gather.10.cloned.1.call-done, bf16[2048,2048]{1,0:T(8,128)(2,1)} %param.12), kind=kOutput, calls=%fused_computation.5 | convolution fusion | flops 2148007936 | bytes 13631488 | tf_op jit(solution)/shard_map/tf,df->td/dot_general | solution.py:49
  154.1 0.0 reduce-scatter.5.cloned.1.call-update
  154.1 17.5 %all-gather.12.cloned.1.call-done = bf16[256,2048]{1,0:T(8,128)(2,1)} async-done(((bf16[32,2048]{1,0:T(8,128)(2,1)}), bf16[256,2048]{1,0:T(8,128)(2,1)}) %all-gather.12.cloned.1.call-update) | async-done | bytes 1048592 | tf_op jit(solution)/shard_map/all_gather | solution.py:27
  171.6 0.0 copy-done.3
  171.6 7.0 %fusion = bf16[2048,2048]{0,1:T(8,128)(2,1)} fusion(bf16[256,2048]{1,0:T(8,128)(2,1)S(1)} %copy-done.3, bf16[256,2048]{1,0:T(8,128)(2,1)} %all-gather.12.cloned.1.call-done), kind=kOutput, calls=%fused_computation.3 | convolution fusion | flops 2155872256 | bytes 10485760 | tf_op jit(solution)/shard_map/td,tf->df/dot_general | solution.py:43
  178.6 12.4 %copy.11 = bf16[2048,2048]{1,0:T(8,128)(2,1)} copy(bf16[2048,2048]{0,1:T(8,128)(2,1)} %fusion) | data formatting | bytes 16777216
  191.0 5.8 %fusion.1 = bf16[2048,2048]{0,1:T(8,128)(2,1)} fusion(bf16[256,2048]{1,0:T(8,128)(2,1)S(1)} %copy-done.4, bf16[256,2048]{1,0:T(8,128)(2,1)S(1)} %copy-done.5), kind=kOutput, calls=%fused_computation.4 | convolution fusion | flops 2155872256 | bytes 10485760 | tf_op jit(solution)/shard_map/td,tf->df/dot_general | solution.py:44
  196.8 12.3 %copy.12 = bf16[2048,2048]{1,0:T(8,128)(2,1)} copy(bf16[2048,2048]{0,1:T(8,128)(2,1)} %fusion.1) | data formatting | bytes 16777216
  209.1 0.0 copy-done.2
  209.2 7.0 %multiply_convert_fusion = bf16[2048,2048]{1,0:T(8,128)(2,1)} fusion(bf16[256,2048]{1,0:T(8,128)(2,1)} %all-gather.14.cloned.1.call-done, bf16[256,2048]{1,0:T(8,128)(2,1)S(1)} %copy-done.2), kind=kOutput, calls=%fused_computation | convolution fusion | flops 2155872256 | bytes 10485760 | tf_op jit(solution)/shard_map/tf,td->fd/dot_general | solution.py:40
  216.2 29.3 %reduce-scatter.5.cloned.1.call-done = f32[32,2048]{1,0:T(8,128)} async-done(((f32[256,2048]{1,0:T(8,128)}), f32[32,2048]{1,0:T(8,128)}) %reduce-scatter.5.cloned.1.call-update) | async-done | bytes 262160 | tf_op jit(solution)/shard_map/reduce_scatter | solution.py:47
  245.5 1.6 convert_element_type.37
  (11 shorter events, 0.0 us)
Async XLA Ops:
  7.2 28.9 %all-gather.6.cloned.1.call-start = ((), (), s32[]{:S(2)}) async-start(), calls=%async_computation.2 | async-start | bytes 1179648 | tf_op jit(solution)/shard_map/all_gather | solution.py:26
  7.9 79.6 %copy-start = (bf16[64,2048]{1,0:T(8,128)(2,1)S(1)}, bf16[64,2048]{1,0:T(8,128)(2,1)}, u32[]{:S(2)}) copy-start(bf16[64,2048]{1,0:T(8,128)(2,1)} %param.9) | copy-start | bytes 786436
  7.9 79.6 %copy-start.1 = (bf16[64,2048]{1,0:T(8,128)(2,1)S(1)}, bf16[64,2048]{1,0:T(8,128)(2,1)}, u32[]{:S(2)}) copy-start(bf16[64,2048]{1,0:T(8,128)(2,1)} %param.10) | copy-start | bytes 786436
  7.9 79.6 %reduce-scatter.3.cloned.1.call-start = ((), (), s32[]{:S(2)}) async-start(), calls=%async_computation.3 | async-start | bytes 2621440 | tf_op jit(solution)/shard_map/reduce_scatter | solution.py:32
  43.5 73.6 %all-gather.8.cloned.1.call-start = ((), (), s32[]{:S(2)}) async-start(), calls=%async_computation.4 | async-start | bytes 1310720 | tf_op jit(solution)/shard_map/all_gather | solution.py:36
  89.7 56.9 %all-gather.10.cloned.1.call-start = ((), (), s32[]{:S(2)}) async-start(), calls=%async_computation.5 | async-start | bytes 1310720 | tf_op jit(solution)/shard_map/all_gather | solution.py:37
  90.3 81.3 %all-gather.12.cloned.1.call-start = ((), (), s32[]{:S(2)}) async-start(), calls=%async_computation.7 | async-start | bytes 1179648 | tf_op jit(solution)/shard_map/all_gather | solution.py:27
  90.9 118.2 %all-gather.14.cloned.1.call-start = ((), (), s32[]{:S(2)}) async-start(), calls=%async_computation.8 | async-start | bytes 1310720 | tf_op jit(solution)/shard_map/all_gather | solution.py:35
  91.5 154.0 %reduce-scatter.5.cloned.1.call-start = ((), (), s32[]{:S(2)}) async-start(), calls=%async_computation.6 | async-start | bytes 2359296 | tf_op jit(solution)/shard_map/reduce_scatter | solution.py:47
  123.2 48.4 %copy-start.3 = (bf16[256,2048]{1,0:T(8,128)(2,1)S(1)}, bf16[256,2048]{1,0:T(8,128)(2,1)}, u32[]{:S(2)}) copy-start(bf16[256,2048]{1,0:T(8,128)(2,1)} %all-gather.8.cloned.1.call-done) | copy-start | bytes 3145732
  178.6 12.4 %copy-start.4 = (bf16[256,2048]{1,0:T(8,128)(2,1)S(1)}, bf16[256,2048]{1,0:T(8,128)(2,1)}, u32[]{:S(2)}) copy-start(bf16[256,2048]{1,0:T(8,128)(2,1)} %all-gather.10.cloned.1.call-done) | copy-start | bytes 3145732
  178.6 12.4 %copy-start.5 = (bf16[256,2048]{1,0:T(8,128)(2,1)S(1)}, bf16[256,2048]{1,0:T(8,128)(2,1)}, u32[]{:S(2)}) copy-start(bf16[256,2048]{1,0:T(8,128)(2,1)} %all-gather.12.cloned.1.call-done) | copy-start | bytes 3145732
  196.8 12.3 %copy-start.2 = (bf16[256,2048]{1,0:T(8,128)(2,1)S(1)}, bf16[256,2048]{1,0:T(8,128)(2,1)}, u32[]{:S(2)}) copy-start(bf16[256,2048]{1,0:T(8,128)(2,1)} %all-gather.6.cloned.1.call-done) | copy-start | bytes 3145732
Sparse Core Ops, SparseCore 0:
  9.9 26.1 all-gather.5
  43.7 43.8 reduce-scatter.2
  89.9 27.2 all-gather.7
  119.2 27.4 all-gather.9
  148.6 22.9 all-gather.11
  173.1 27.9 all-gather.13
  204.7 40.7 reduce-scatter.4
where the time goes:
time: 255 us; the launch traced here: 254 us
  waiting for transfers between devices  170 us (67%)
  matrix products  40.7 us (16%)
  local copies, waits for them, and re-layouts  24.8 us (10%)
  between operations  14.2 us (6%)
  other arithmetic  3.79 us (1%)
    reduce_scatter x1, waiting for transfers between devices, per_device(): lax.psum_scatter(partial_hidden, 'col', scatter_dimension=0, tiled=True)  44 us
    reduce_scatter x1, waiting for transfers between devices, per_device(): lax.psum_scatter(jnp.einsum('tf,df->td', gate_all, gate_weight, preferred...  29.3 us
    all_gather x1, waiting for transfers between devices, per_device(): lax.all_gather(grad_out, 'row', axis=0, tiled=True)  28.1 us
    all_gather x1, waiting for transfers between devices, per_device(): lax.all_gather(gate_term, 'col', axis=0, tiled=True)  25.4 us
    unnamed x14, local copies, waits for them, and re-layouts  24.8 us
    all_gather x1, waiting for transfers between devices, per_device(): lax.all_gather(up_term, 'col', axis=0, tiled=True)  23.4 us
    all_gather x1, waiting for transfers between devices, per_device(): lax.all_gather(inputs, 'row', axis=0, tiled=True)  17.5 us
    dot_general x1, matrix products, per_device(): jnp.einsum('tf,df->td', up_all, up_weight, preferred_element_type=jnp.flo...  7.41 us
  transfers between devices with their start and end apart: 7, of which 6 were waited for; matrix products, arithmetic and copies ran while one was open for 23% of the time, Pallas kernels for 0%

commit v1 on v0

v1 whole, which is shorter than its diff:
```python
import functools
import math

import jax
import jax.numpy as jnp
from jax import lax
from jax.experimental import pallas as pl
from jax.experimental.pallas import tpu as pltpu
from jax.sharding import PartitionSpec as P

F32, BF16 = jnp.float32, jnp.bfloat16
VMEM_LIMIT = 40 * 1024 * 1024
STRIPE = 256


def stripe(extent):
    return math.gcd(extent, STRIPE)


def whole(shape):
    return pl.BlockSpec(shape, lambda i, *_: (0,) * len(shape))


def params():
    return pltpu.CompilerParams(vmem_limit_bytes=VMEM_LIMIT, dimension_semantics=("arbitrary",))


def flip(count, mask):
    return [(i, i ^ mask) for i in range(count)]


def turn(count, shift):
    return [(i, (i + shift) % count) for i in range(count)]


def gather_row(own, n_row):
    pieces = [own] + [None] * (n_row - 1)
    for mask in range(2, n_row, 2):
        pieces[mask] = lax.ppermute(own, "row", flip(n_row, mask))
    for mask in range(0, n_row, 2):
        pieces[mask ^ 1] = lax.ppermute(pieces[mask], "row", flip(n_row, 1))
    return pieces


def relay_col(own, n_col):
    from_low, from_high = [own], [own]
    for step in range(1, n_col):
        up = [(i, i + 1) for i in range(step - 1, n_col - 1)]
        down = [(i, i - 1) for i in range(1, n_col - step + 1)]
        from_low.append(lax.ppermute(from_low[-1], "col", up))
        from_high.append(lax.ppermute(from_high[-1], "col", down))
    return from_low, from_high


def hidden_kernel(n_row, n_col, offsets, *refs):
    pieces, weight = refs[:n_row], refs[n_row]
    grad_all, own, sends = refs[n_row + 1], refs[n_row + 2], refs[n_row + 3 :]
    rows = pieces[0].shape[0]

    @pl.when(pl.program_id(0) == 0)
    def _():
        for x in range(n_row):
            grad_all[pl.ds(pl.multiple_of(offsets[x], rows), rows), :] = pieces[x][...]

    total = lax.dot_general(
        grad_all[...], weight[...], (((1,), (1,)), ((), ())), preferred_element_type=F32
    )
    part = own.shape[0]
    own[...] = total[:part]
    for j in range(1, n_col):
        sends[j - 1][...] = total[j * part : (j + 1) * part].astype(BF16)


def partial_hidden(pieces, weight, offsets, n_col):
    n_row = len(pieces)
    rows, width = pieces[0].shape
    units = weight.shape[0]
    tokens = rows * n_row
    part = tokens // n_col
    step = stripe(units)
    return pl.pallas_call(
        functools.partial(hidden_kernel, n_row, n_col),
        grid_spec=pltpu.PrefetchScalarGridSpec(
            num_scalar_prefetch=1,
            grid=(units // step,),
            in_specs=[whole((rows, width))] * n_row + [pl.BlockSpec((step, width), lambda i, *_: (i, 0))],
            out_specs=[whole((tokens, width))] + [pl.BlockSpec((part, step), lambda i, *_: (0, i))] * n_col,
        ),
        out_shape=[jax.ShapeDtypeStruct((tokens, width), BF16), jax.ShapeDtypeStruct((part, units), F32)]
        + [jax.ShapeDtypeStruct((part, units), BF16)] * (n_col - 1),
        compiler_params=params(),
        cost_estimate=pl.CostEstimate(
            flops=2 * tokens * width * units, bytes_accessed=2 * units * width, transcendentals=0
        ),
        name="partial_hidden",
    )(offsets, *pieces, weight)


def down_kernel(n_col, scale, place, *refs):
    gate, up, grad_all = refs[:3]
    from_low, from_high = refs[3 : 2 + n_col], refs[2 + n_col : 1 + 2 * n_col]
    down_grad, up_factor, gate_factor = refs[1 + 2 * n_col :]
    part = gate.shape[0]
    hidden = []
    for j in range(n_col):
        if j == 0:
            g, u = gate[...], up[...]
        else:
            low = place[0] >= j
            g = jnp.where(low, from_low[j - 1][0], from_high[n_col - j - 1][0])
            u = jnp.where(low, from_low[j - 1][1], from_high[n_col - j - 1][1])
        g, u = g.astype(F32), u.astype(F32)
        s = 1.0 / (1.0 + jnp.exp(-g))
        silu = g * s
        hidden.append((silu * u).astype(BF16))
        up_factor[j * part : (j + 1) * part, :] = silu
        gate_factor[j * part : (j + 1) * part, :] = u * s * (1.0 + g * (1.0 - s))
    product = lax.dot_general(
        jnp.concatenate(hidden, axis=0), grad_all[...], (((0,), (0,)), ((), ())), preferred_element_type=F32
    )
    down_grad[...] = (product * scale).astype(BF16)


def down_gradient(gate, up, grad_all, from_low, from_high, place, scale):
    n_col = len(from_low)
    part, units = gate.shape
    tokens, width = grad_all.shape
    step = stripe(units)
    flat = pl.BlockSpec((part, step), lambda i, *_: (0, i))
    pair = pl.BlockSpec((2, part, step), lambda i, *_: (0, 0, i))
    tall = pl.BlockSpec((tokens, step), lambda i, *_: (0, i))
    return pl.pallas_call(
        functools.partial(down_kernel, n_col, scale),
        grid_spec=pltpu.PrefetchScalarGridSpec(
            num_scalar_prefetch=1,
            grid=(units // step,),
            in_specs=[flat, flat, whole((tokens, width))] + [pair] * (2 * n_col - 2),
            out_specs=[pl.BlockSpec((step, width), lambda i, *_: (i, 0)), tall, tall],
        ),
        out_shape=[jax.ShapeDtypeStruct((units, width), BF16)] + [jax.ShapeDtypeStruct((tokens, units), F32)] * 2,
        compiler_params=params(),
        cost_estimate=pl.CostEstimate(
            flops=2 * tokens * width * units,
            bytes_accessed=2 * units * width + 12 * tokens * units,
            transcendentals=tokens * units,
        ),
        name="down_gradient",
    )(place, gate, up, grad_all, *from_low[1:], *from_high[1:])


def input_kernel(n_row, n_col, offsets, *refs):
    hidden_grad, refs = refs[:n_col], refs[n_col:]
    up_factor, gate_factor, gate_weight, up_weight, gate_term, up_term, own, other = refs
    part = hidden_grad[0].shape[0]
    rows = part * n_col // n_row

    @pl.when(pl.program_id(0) == 0)
    def _():
        for j in range(n_col):
            h = hidden_grad[j][...].astype(F32)
            at = slice(j * part, (j + 1) * part)
            terms = ((gate_term, (h * gate_factor[at, :]).astype(BF16)), (up_term, (h * up_factor[at, :]).astype(BF16)))
            for c in range(part // rows):
                to = pl.ds(pl.multiple_of(offsets[j * (part // rows) + c], rows), rows)
                for ref, term in terms:
                    ref[to, :] = term[c * rows : (c + 1) * rows]

    contract = (((1,), (1,)), ((), ()))
    total = lax.dot_general(gate_term[...], gate_weight[...], contract, preferred_element_type=F32)
    total += lax.dot_general(up_term[...], up_weight[...], contract, preferred_element_type=F32)
    half = own.shape[0]
    own[...] = total[:half]
    other[...] = total[half:].astype(BF16)


def partial_input(hidden_grad, up_factor, gate_factor, gate_weight, up_weight, offsets, n_row):
    n_col = len(hidden_grad)
    part, units = hidden_grad[0].shape
    tokens = part * n_col
    width = gate_weight.shape[0]
    step = stripe(width)
    weight = pl.BlockSpec((step, units), lambda i, *_: (i, 0))
    half = pl.BlockSpec((tokens // 2, step), lambda i, *_: (0, i))
    return pl.pallas_call(
        functools.partial(input_kernel, n_row, n_col),
        grid_spec=pltpu.PrefetchScalarGridSpec(
            num_scalar_prefetch=1,
            grid=(width // step,),
            in_specs=[whole((part, units))] * n_col + [whole((tokens, units))] * 2 + [weight, weight],
            out_specs=[whole((tokens, units))] * 2 + [half, half],
        ),
        out_shape=[jax.ShapeDtypeStruct((tokens, units), BF16)] * 2
        + [jax.ShapeDtypeStruct((tokens // 2, width), F32), jax.ShapeDtypeStruct((tokens // 2, width), BF16)],
        compiler_params=params(),
        cost_estimate=pl.CostEstimate(
            flops=4 * tokens * width * units, bytes_accessed=4 * units * width, transcendentals=0
        ),
        name="partial_input",
    )(offsets, *hidden_grad, up_factor, gate_factor, gate_weight, up_weight)


def weight_kernel(n_row, scale, *refs):
    pieces = refs[:n_row]
    gate_term, up_term, gate_grad, up_grad = refs[n_row:]
    order = list(range(0, n_row, 2)) + list(range(1, n_row, 2))
    left = jnp.concatenate([pieces[x][...] for x in order], axis=0)
    for term, out in ((gate_term, gate_grad), (up_term, up_grad)):
        product = lax.dot_general(left, term[...], (((0,), (0,)), ((), ())), preferred_element_type=F32)
        out[...] = (product * scale).astype(BF16)


def weight_gradients(pieces, gate_term, up_term, scale):
    n_row = len(pieces)
    rows, width = pieces[0].shape
    tokens, units = gate_term.shape
    step = stripe(width)
    out = pl.BlockSpec((step, units), lambda i: (i, 0))
    return pl.pallas_call(
        functools.partial(weight_kernel, n_row, scale),
        grid=(width // step,),
        in_specs=[pl.BlockSpec((rows, step), lambda i: (0, i))] * n_row + [whole((tokens, units))] * 2,
        out_specs=[out, out],
        out_shape=[jax.ShapeDtypeStruct((width, units), BF16)] * 2,
        compiler_params=params(),
        cost_estimate=pl.CostEstimate(
            flops=4 * tokens * width * units, bytes_accessed=4 * units * width, transcendentals=0
        ),
        name="weight_gradients",
    )(*pieces, gate_term, up_term)


def per_device(inputs, grad_out, gate_pre, up_pre, gate_weight, up_weight, down_weight):
    n_row, n_col = lax.axis_size("row"), lax.axis_size("col")
    row, col = lax.axis_index("row"), lax.axis_index("col")
    rows = grad_out.shape[0]
    tokens = rows * n_row
    share = n_row // n_col
    scale = 1.0 / math.sqrt(tokens)

    block = row ^ jnp.arange(n_row, dtype=jnp.int32)
    part_offsets = (jnp.mod(col - block // share, n_col) * share + block % share) * rows
    block = (jnp.mod(col - jnp.arange(n_col, dtype=jnp.int32), n_col)[:, None] * share + jnp.arange(share)).reshape(-1)
    seen = block ^ row
    block_offsets = ((seen % 2) * (n_row // 2) + seen // 2) * rows

    grad_pieces = gather_row(grad_out, n_row)
    from_low, from_high = relay_col(jnp.stack([gate_pre, up_pre]), n_col)
    grad_all, own, *sends = partial_hidden(grad_pieces, down_weight, part_offsets.astype(jnp.int32), n_col)
    for j, send in enumerate(sends, 1):
        own = own + lax.ppermute(send, "col", turn(n_col, -j)).astype(F32)
    own = own.astype(BF16)
    hidden_grad = [own] + [lax.ppermute(own, "col", turn(n_col, j)) for j in range(1, n_col)]

    down_grad, up_factor, gate_factor = down_gradient(
        gate_pre, up_pre, grad_all, from_low, from_high, col[None].astype(jnp.int32), scale
    )
    gate_term, up_term, mine, other = partial_input(
        hidden_grad, up_factor, gate_factor, gate_weight, up_weight, block_offsets.astype(jnp.int32), n_row
    )
    mine = mine + lax.ppermute(other, "row", flip(n_row, 1)).astype(F32)
    input_pieces = gather_row(inputs, n_row)
    input_grad = mine[:rows]
    for k in range(1, n_row // 2):
        away = mine[k * rows : (k + 1) * rows].astype(BF16)
        input_grad = input_grad + lax.ppermute(away, "row", flip(n_row, 2 * k)).astype(F32)
    gate_grad, up_grad = weight_gradients(input_pieces, gate_term, up_term, scale)
    return (input_grad.astype(BF16), gate_grad, up_grad, down_grad)


def solution(mesh):
    return jax.shard_map(
        per_device,
        mesh=mesh,
        in_specs=(
            P("row", "col"),
            P("row", "col"),
            P("col", "row"),
            P("col", "row"),
            P("col", "row"),
            P("col", "row"),
            P("row", "col"),
        ),
        out_specs=(P("row", "col"), P("col", "row"), P("col", "row"), P("row", "col")),
        check_vma=False,
    )
```

time: 255 us -> 122 us (0.48)
  waiting for transfers between devices: 170 us -> 43.8 us
  matrix products: 40.7 us -> 0 us
  starting transfers between devices: 0.45 us -> 36.7 us
  Pallas kernels: 0 us -> 33.7 us
  local copies, waits for them, and re-layouts: 24.8 us -> 4.41 us
  between operations: 14.2 us -> 0.81 us
    all_gather x5 -> x0, waiting for transfers between devices: 94.5 us -> none  [the longest x1 28.1 us: per_device(): lax.all_gather(grad_out, 'row', axis=0, tiled=True)]
    reduce_scatter x2 -> x0, waiting for transfers between devices: 73.3 us -> none  [the longest x1 44 us: per_device(): lax.psum_scatter(partial_hidden, 'col', scatter_dimension=0, tiled=True)]
    ppermute x0 -> x30, waiting for transfers between devices: none -> 43.8 us  [the longest x3 21.1 us: per_device(): own = own + lax.ppermute(send, 'col', turn(n_col, -j)).astype(F32)]
    dot_general x6 -> x0, matrix products: 40.7 us -> none  [the longest x1 7.41 us: per_device(): jnp.einsum('tf,df->td', up_all, up_weight, preferred_element_type=jnp.flo...]
    ppermute x0 -> x30, starting transfers between devices: none -> 36.7 us  [the longest x6 9.89 us: gather_row(): pieces[mask] = lax.ppermute(own, 'row', flip(n_row, mask))]
    pallas_call x0 -> x4, Pallas kernels: none -> 33.7 us  [the longest x1 11.3 us: partial_input(): pl.pallas_call(functools.partial(input_kernel, n_row, n_col), grid_spec=p...]
    unnamed x14 -> x10, local copies, waits for them, and re-layouts: 24.8 us -> 4.29 us
    convert_element_type x2, other arithmetic: 3.79 us -> 0.83 us  [the longest x1 0.72 us: per_device(): return (input_grad.astype(BF16), gate_grad, up_grad, down_grad)]
  transfers between devices with their start and end apart: 7 -> 30, of which waited for: 6 -> 9; matrix products, arithmetic and copies ran while one was open for 23% -> 0% of each run, Pallas kernels for 0% -> 18%
where the time goes in v1:
time: 122 us
  waiting for transfers between devices  43.8 us (36%)
  starting transfers between devices  36.7 us (30%)
  Pallas kernels  33.7 us (28%)
  local copies, waits for them, and re-layouts  4.41 us (4%)
  other arithmetic  2.24 us (2%)
    ppermute x3, waiting for transfers between devices, per_device(): own = own + lax.ppermute(send, 'col', turn(n_col, -j)).astype(F32)  21.1 us
    pallas_call x1, Pallas kernels, partial_input(): pl.pallas_call(functools.partial(input_kernel, n_row, n_col), grid_spec=p...  11.3 us
    ppermute x6, waiting for transfers between devices, gather_row(): pieces[mask] = lax.ppermute(own, 'row', flip(n_row, mask))  10.7 us
    ppermute x6, starting transfers between devices, gather_row(): pieces[mask] = lax.ppermute(own, 'row', flip(n_row, mask))  9.89 us
    ppermute x3, waiting for transfers between devices, per_device(): lax.ppermute(own, 'col', turn(n_col, j))  9.81 us
    pallas_call x1, Pallas kernels, down_gradient(): pl.pallas_call(functools.partial(down_kernel, n_col, scale), grid_spec=pl...  8.79 us
    ppermute x3, starting transfers between devices, relay_col(): from_low.append(lax.ppermute(from_low[-1], 'col', up))  8.54 us
    pallas_call x1, Pallas kernels, weight_gradients(): pl.pallas_call(functools.partial(weight_kernel, n_row, scale), grid=(widt...  8.04 us
  transfers between devices with their start and end apart: 30, of which 9 were waited for; matrix products, arithmetic and copies ran while one was open for 0% of the time, Pallas kernels for 18%

profile of v1, /device:TPU:0, one launch (start us, length us, event | category | flops | bytes accessed | tf_op | source)
XLA Modules:
  0.0 121.6 jit_solution(11789861503972543240)
XLA Ops:
  0.7 1.1 pad_maximum_fusion
  1.8 1.3 %collective-permute-start.16 = (bf16[2,64,2048]{2,1,0:T(8,128)(2,1)S(1)}, bf16[2,64,2048]{2,1,0:T(8,128)(2,1)S(1)}, u32[]{:S(2)}, u32[]{:S(2)}) collective-permute-start(bf16[2,64,2048]{2,1,0:T(8,128)(2,1)S(1)} %pad_maximum_fusion), channel_id=1, source_target_pairs={{8,0},{16,8},{24,16},{9,1},{17,9},{25,17},{10,2},{18,10},{26,18},{... | collective-permute-start | bytes 1572872 | tf_op jit(solution)/shard_map/ppermute | solution.py:51
  3.1 6.4 %collective-permute-start.13 = (bf16[2,64,2048]{2,1,0:T(8,128)(2,1)S(1)}, bf16[2,64,2048]{2,1,0:T(8,128)(2,1)}, u32[]{:S(2)}, u32[]{:S(2)}) collective-permute-start(bf16[2,64,2048]{2,1,0:T(8,128)(2,1)S(1)} %pad_maximum_fusion), channel_id=1, source_target_pairs={{0,8},{8,16},{16,24},{1,9},{9,17},{17,25},{2,10},{10,18},{18,26},{... | collective-permute-start | bytes 1572872 | tf_op jit(solution)/shard_map/ppermute | solution.py:50
  9.5 2.0 %collective-permute-start.3 = (bf16[32,2048]{1,0:T(8,128)(2,1)}, bf16[32,2048]{1,0:T(8,128)(2,1)S(1)}, u32[]{:S(2)}, u32[]{:S(2)}) collective-permute-start(bf16[32,2048]{1,0:T(8,128)(2,1)} %refs_0_.3), channel_id=1, source_target_pairs={{0,4},{1,5},{2,6},{3,7},{4,0},{5,1},{6,2},{7,3},{8,12},{9,13},{10,... | collective-permute-start | bytes 393224 | tf_op jit(solution)/shard_map/ppermute | solution.py:39
  11.4 1.5 %collective-permute-start.1 = (bf16[32,2048]{1,0:T(8,128)(2,1)}, bf16[32,2048]{1,0:T(8,128)(2,1)S(1)}, u32[]{:S(2)}, u32[]{:S(2)}) collective-permute-start(bf16[32,2048]{1,0:T(8,128)(2,1)} %refs_0_.3), channel_id=1, source_target_pairs={{0,2},{1,3},{2,0},{3,1},{4,6},{5,7},{6,4},{7,5},{8,10},{9,11},{10,... | collective-permute-start | bytes 393224 | tf_op jit(solution)/shard_map/ppermute | solution.py:39
  12.9 1.7 %collective-permute-done.3.refs_4_ = bf16[32,2048]{1,0:T(8,128)(2,1)S(1)} collective-permute-done((bf16[32,2048]{1,0:T(8,128)(2,1)}, bf16[32,2048]{1,0:T(8,128)(2,1)S(1)}, u32[]{:S(2)}, u32[]{:S(2)}) %collective-permute-start.3) | collective-permute-done | bytes 131104 | tf_op jit(solution)/shard_map/ppermute | solution.py:39
  14.6 2.9 %collective-permute-start.5 = (bf16[32,2048]{1,0:T(8,128)(2,1)}, bf16[32,2048]{1,0:T(8,128)(2,1)S(1)}, u32[]{:S(2)}, u32[]{:S(2)}) collective-permute-start(bf16[32,2048]{1,0:T(8,128)(2,1)} %refs_0_.3), channel_id=1, source_target_pairs={{0,6},{1,7},{2,4},{3,5},{4,2},{5,3},{6,0},{7,1},{8,14},{9,15},{10,... | collective-permute-start | bytes 393224 | tf_op jit(solution)/shard_map/ppermute | solution.py:39
  18.0 2.7 %collective-permute-done.5.refs_6_ = bf16[32,2048]{1,0:T(8,128)(2,1)S(1)} collective-permute-done((bf16[32,2048]{1,0:T(8,128)(2,1)}, bf16[32,2048]{1,0:T(8,128)(2,1)S(1)}, u32[]{:S(2)}, u32[]{:S(2)}) %collective-permute-start.5) | collective-permute-done | bytes 131104 | tf_op jit(solution)/shard_map/ppermute | solution.py:39
  20.7 1.3 %collective-permute-start.17 = (bf16[2,64,2048]{2,1,0:T(8,128)(2,1)S(1)}, bf16[2,64,2048]{2,1,0:T(8,128)(2,1)}, u32[]{:S(2)}, u32[]{:S(2)}) collective-permute-start(bf16[2,64,2048]{2,1,0:T(8,128)(2,1)S(1)} %collective-permute-done.16.refs_6_), channel_id=1, source_target_pairs={{8,0},{16,8},{9,1},{17,9},{10,2},{18,10},{11,3},{19,11},{12,4},{20... | collective-permute-start | bytes 1572872 | tf_op jit(solution)/shard_map/ppermute | solution.py:51
  22.1 1.5 %collective-permute-start.14 = (bf16[2,64,2048]{2,1,0:T(8,128)(2,1)}, bf16[2,64,2048]{2,1,0:T(8,128)(2,1)}, u32[]{:S(2)}, u32[]{:S(2)}) collective-permute-start(bf16[2,64,2048]{2,1,0:T(8,128)(2,1)} %collective-permute-done.13.refs_3_), channel_id=1, source_target_pairs={{8,16},{16,24},{9,17},{17,25},{10,18},{18,26},{11,19},{19,27},{12,... | collective-permute-start | bytes 1572872 | tf_op jit(solution)/shard_map/ppermute | solution.py:50
  23.6 3.4 %copy-done = bf16[2048,2048]{1,0:T(8,128)(2,1)S(1)} copy-done((bf16[2048,2048]{1,0:T(8,128)(2,1)S(1)}, bf16[2048,2048]{1,0:T(8,128)(2,1)}, u32[]{:S(2)}) %copy-start) | copy-done | bytes 8388632
  26.9 0.9 copy-done.3
  27.8 5.6 %partial_hidden.1 = (bf16[256,2048]{1,0:T(8,128)(2,1)S(1)}, f32[64,2048]{1,0:T(8,128)S(1)}, bf16[64,2048]{1,0:T(8,128)(2,1)}, bf16[64,2048]{1,0:T(8,128)(2,1)}, bf16[64,2048]{1,0:T(8,128)(2,1)}) custom-call(s32[8]{0:T(128)S(1)} %fusion.10.offsets, bf16[32,2048]{1,0:T(8,128)(2,1)S(1)} %copy-done.3, bf16[32,2048]{1,0:T(8,128)(2,1)S(1)} %collective-permute-done.refs_1_, ...), custom_call_target="tpu_custom_call" | custom-call | flops 2147483648 | bytes 8388608 | tf_op jit(solution)/shard_map/partial_hidden/pallas_call | solution.py:81
  33.4 2.4 %collective-permute-start.7 = (bf16[64,2048]{1,0:T(8,128)(2,1)}, bf16[64,2048]{1,0:T(8,128)(2,1)S(1)}, u32[]{:S(2)}, u32[]{:S(2)}) collective-permute-start(bf16[64,2048]{1,0:T(8,128)(2,1)} %get-tuple-element.19), channel_id=1, source_target_pairs={{0,24},{8,0},{16,8},{24,16},{1,25},{9,1},{17,9},{25,17},{2,26},{10... | collective-permute-start | bytes 786440 | tf_op jit(solution)/shard_map/ppermute | solution.py:250
  35.8 5.0 %collective-permute-start.8 = (bf16[64,2048]{1,0:T(8,128)(2,1)}, bf16[64,2048]{1,0:T(8,128)(2,1)S(1)}, u32[]{:S(2)}, u32[]{:S(2)}) collective-permute-start(bf16[64,2048]{1,0:T(8,128)(2,1)} %get-tuple-element.20), channel_id=1, source_target_pairs={{0,16},{8,24},{16,0},{24,8},{1,17},{9,25},{17,1},{25,9},{2,18},{10... | collective-permute-start | bytes 786440 | tf_op jit(solution)/shard_map/ppermute | solution.py:250
  41.0 1.3 %collective-permute-start.18 = (bf16[2,64,2048]{2,1,0:T(8,128)(2,1)}, bf16[2,64,2048]{2,1,0:T(8,128)(2,1)S(1)}, u32[]{:S(2)}, u32[]{:S(2)}) collective-permute-start(bf16[2,64,2048]{2,1,0:T(8,128)(2,1)} %collective-permute-done.17.refs_7_), channel_id=1, source_target_pairs={{8,0},{9,1},{10,2},{11,3},{12,4},{13,5},{14,6},{15,7}} | collective-permute-start | bytes 1572872 | tf_op jit(solution)/shard_map/ppermute | solution.py:51
  43.0 3.7 %collective-permute-done.7 = bf16[64,2048]{1,0:T(8,128)(2,1)S(1)} collective-permute-done((bf16[64,2048]{1,0:T(8,128)(2,1)}, bf16[64,2048]{1,0:T(8,128)(2,1)S(1)}, u32[]{:S(2)}, u32[]{:S(2)}) %collective-permute-start.7) | collective-permute-done | bytes 262176 | tf_op jit(solution)/shard_map/ppermute | solution.py:250
  46.7 17.4 %collective-permute-done.8 = bf16[64,2048]{1,0:T(8,128)(2,1)S(1)} collective-permute-done((bf16[64,2048]{1,0:T(8,128)(2,1)}, bf16[64,2048]{1,0:T(8,128)(2,1)S(1)}, u32[]{:S(2)}, u32[]{:S(2)}) %collective-permute-start.8) | collective-permute-done | bytes 262176 | tf_op jit(solution)/shard_map/ppermute | solution.py:250
  64.3 0.8 collective-permute-start.11
  65.1 1.9 %collective-permute-start.10 = (bf16[64,2048]{1,0:T(8,128)(2,1)S(1)}, bf16[64,2048]{1,0:T(8,128)(2,1)S(1)}, u32[]{:S(2)}, u32[]{:S(2)}) collective-permute-start(bf16[64,2048]{1,0:T(8,128)(2,1)S(1)} %add_convert_fusion.refs_0_), channel_id=1, source_target_pairs={{0,8},{8,16},{16,24},{24,0},{1,9},{9,17},{17,25},{25,1},{2,10},{10... | collective-permute-start | bytes 786440 | tf_op jit(solution)/shard_map/ppermute | solution.py:252
  67.1 2.1 %collective-permute-done.18.refs_8_ = bf16[2,64,2048]{2,1,0:T(8,128)(2,1)S(1)} collective-permute-done((bf16[2,64,2048]{2,1,0:T(8,128)(2,1)}, bf16[2,64,2048]{2,1,0:T(8,128)(2,1)S(1)}, u32[]{:S(2)}, u32[]{:S(2)}) %collective-permute-start.18) | collective-permute-done | bytes 524320 | tf_op jit(solution)/shard_map/ppermute | solution.py:51
  69.2 8.8 %down_gradient.1 = (bf16[2048,2048]{1,0:T(8,128)(2,1)}, f32[256,2048]{1,0:T(8,128)S(1)}, f32[256,2048]{1,0:T(8,128)S(1)}) custom-call(s32[1]{0:T(128)} %bitcast.place, bf16[64,2048]{1,0:T(8,128)(2,1)S(1)} %copy-done.1, bf16[64,2048]{1,0:T(8,128)(2,1)S(1)} %copy-done.2, bf16[256,2048]{1,0:T(8,128)(2,1)S(1)} %get-tuple-element.22.refs_2_, ...), custom_call_target="tpu_custom_call" | custom-call | flops 2147483648 | bytes 14680064 | tf_op jit(solution)/shard_map/down_gradient/pallas_call | solution.py:132
  78.0 9.8 %collective-permute-done.11.refs_2_ = bf16[64,2048]{1,0:T(8,128)(2,1)S(1)} collective-permute-done((bf16[64,2048]{1,0:T(8,128)(2,1)S(1)}, bf16[64,2048]{1,0:T(8,128)(2,1)S(1)}, u32[]{:S(2)}, u32[]{:S(2)}) %collective-permute-start.11) | collective-permute-done | bytes 262176 | tf_op jit(solution)/shard_map/ppermute | solution.py:252
  87.8 11.3 %partial_input.1 = (bf16[256,2048]{1,0:T(8,128)(2,1)S(1)}, bf16[256,2048]{1,0:T(8,128)(2,1)S(1)}, f32[128,2048]{1,0:T(8,128)S(1)}, bf16[128,2048]{1,0:T(8,128)(2,1)S(1)}) custom-call(s32[8]{0:T(128)S(1)} %fusion.11.offsets, bf16[64,2048]{1,0:T(8,128)(2,1)S(1)} %add_convert_fusion.refs_0_, bf16[64,2048]{1,0:T(8,128)(2,1)S(1)} %collective-permute-done.10.refs_1_, ...), custom_call_target="tpu_custom_call" | custom-call | flops 4294967296 | bytes 16777216 | tf_op jit(solution)/shard_map/partial_input/pallas_call | solution.py:184
  99.2 1.6 %collective-permute-start.26 = (bf16[32,2048]{1,0:T(8,128)(2,1)S(1)}, bf16[32,2048]{1,0:T(8,128)(2,1)S(1)}, u32[]{:S(2)}, u32[]{:S(2)}) collective-permute-start(bf16[32,2048]{1,0:T(8,128)(2,1)S(1)} %copy-done.4), channel_id=1, source_target_pairs={{0,4},{1,5},{2,6},{3,7},{4,0},{5,1},{6,2},{7,3},{8,12},{9,13},{10,... | collective-permute-start | bytes 393224 | tf_op jit(solution)/shard_map/ppermute | solution.py:39
  100.8 1.5 %collective-permute-start.24 = (bf16[32,2048]{1,0:T(8,128)(2,1)S(1)}, bf16[32,2048]{1,0:T(8,128)(2,1)S(1)}, u32[]{:S(2)}, u32[]{:S(2)}) collective-permute-start(bf16[32,2048]{1,0:T(8,128)(2,1)S(1)} %copy-done.4), channel_id=1, source_target_pairs={{0,2},{1,3},{2,0},{3,1},{4,6},{5,7},{6,4},{7,5},{8,10},{9,11},{10,... | collective-permute-start | bytes 393224 | tf_op jit(solution)/shard_map/ppermute | solution.py:39
  102.8 2.3 %collective-permute-done.26.refs_4_ = bf16[32,2048]{1,0:T(8,128)(2,1)S(1)} collective-permute-done((bf16[32,2048]{1,0:T(8,128)(2,1)S(1)}, bf16[32,2048]{1,0:T(8,128)(2,1)S(1)}, u32[]{:S(2)}, u32[]{:S(2)}) %collective-permute-start.26) | collective-permute-done | bytes 131104 | tf_op jit(solution)/shard_map/ppermute | solution.py:39
  105.1 2.0 %collective-permute-done.24.refs_2_ = bf16[32,2048]{1,0:T(8,128)(2,1)S(1)} collective-permute-done((bf16[32,2048]{1,0:T(8,128)(2,1)S(1)}, bf16[32,2048]{1,0:T(8,128)(2,1)S(1)}, u32[]{:S(2)}, u32[]{:S(2)}) %collective-permute-start.24) | collective-permute-done | bytes 131104 | tf_op jit(solution)/shard_map/ppermute | solution.py:39
  107.1 2.0 %collective-permute-done.28.refs_6_ = bf16[32,2048]{1,0:T(8,128)(2,1)S(1)} collective-permute-done((bf16[32,2048]{1,0:T(8,128)(2,1)S(1)}, bf16[32,2048]{1,0:T(8,128)(2,1)S(1)}, u32[]{:S(2)}, u32[]{:S(2)}) %collective-permute-start.28) | collective-permute-done | bytes 131104 | tf_op jit(solution)/shard_map/ppermute | solution.py:39
  109.3 1.6 %collective-permute-start.20 = (bf16[32,2048]{1,0:T(8,128)(2,1)S(1)}, bf16[32,2048]{1,0:T(8,128)(2,1)S(1)}, u32[]{:S(2)}, u32[]{:S(2)}) collective-permute-start(bf16[32,2048]{1,0:T(8,128)(2,1)S(1)} %get-tuple-element.34), channel_id=1, source_target_pairs={{0,2},{1,3},{2,0},{3,1},{4,6},{5,7},{6,4},{7,5},{8,10},{9,11},{10,... | collective-permute-start | bytes 393224 | tf_op jit(solution)/shard_map/ppermute | solution.py:265
  110.9 1.5 %collective-permute-start.22 = (bf16[32,2048]{1,0:T(8,128)(2,1)S(1)}, bf16[32,2048]{1,0:T(8,128)(2,1)S(1)}, u32[]{:S(2)}, u32[]{:S(2)}) collective-permute-start(bf16[32,2048]{1,0:T(8,128)(2,1)S(1)} %get-tuple-element.35), channel_id=1, source_target_pairs={{0,6},{1,7},{2,4},{3,5},{4,2},{5,3},{6,0},{7,1},{8,14},{9,15},{10,... | collective-permute-start | bytes 393224 | tf_op jit(solution)/shard_map/ppermute | solution.py:265
  112.9 8.0 %weight_gradients.1 = (bf16[2048,2048]{1,0:T(8,128)(2,1)}, bf16[2048,2048]{1,0:T(8,128)(2,1)}) custom-call(bf16[32,2048]{1,0:T(8,128)(2,1)S(1)} %copy-done.4, bf16[32,2048]{1,0:T(8,128)(2,1)S(1)} %collective-permute-done.23.refs_1_, bf16[32,2048]{1,0:T(8,128)(2,1)S(1)} %collective-permute-done.24.refs_2_, ...), custom_call_target="tpu_custom_call" | custom-call | flops 4294967296 | bytes 16777216 | tf_op jit(solution)/shard_map/weight_gradients/pallas_call | solution.py:218
  (52 shorter events, 3.6 us)
Async XLA Ops:
  0.6 68.5 %copy-start.1 = (bf16[64,2048]{1,0:T(8,128)(2,1)S(1)}, bf16[64,2048]{1,0:T(8,128)(2,1)}, u32[]{:S(2)}) copy-start(bf16[64,2048]{1,0:T(8,128)(2,1)} %refs_0_.4) | copy-start | bytes 786436
  0.6 68.5 %copy-start.2 = (bf16[64,2048]{1,0:T(8,128)(2,1)S(1)}, bf16[64,2048]{1,0:T(8,128)(2,1)}, u32[]{:S(2)}) copy-start(bf16[64,2048]{1,0:T(8,128)(2,1)} %refs_1_.1) | copy-start | bytes 786436
  1.8 19.0 %collective-permute-start.16 = (bf16[2,64,2048]{2,1,0:T(8,128)(2,1)S(1)}, bf16[2,64,2048]{2,1,0:T(8,128)(2,1)S(1)}, u32[]{:S(2)}, u32[]{:S(2)}) collective-permute-start(bf16[2,64,2048]{2,1,0:T(8,128)(2,1)S(1)} %pad_maximum_fusion), channel_id=1, source_target_pairs={{8,0},{16,8},{24,16},{9,1},{17,9},{25,17},{10,2},{18,10},{26,18},{... | collective-permute-start | bytes 1572872 | tf_op jit(solution)/shard_map/ppermute | solution.py:51
  3.1 19.0 %collective-permute-start.13 = (bf16[2,64,2048]{2,1,0:T(8,128)(2,1)S(1)}, bf16[2,64,2048]{2,1,0:T(8,128)(2,1)}, u32[]{:S(2)}, u32[]{:S(2)}) collective-permute-start(bf16[2,64,2048]{2,1,0:T(8,128)(2,1)S(1)} %pad_maximum_fusion), channel_id=1, source_target_pairs={{0,8},{8,16},{16,24},{1,9},{9,17},{17,25},{2,10},{10,18},{18,26},{... | collective-permute-start | bytes 1572872 | tf_op jit(solution)/shard_map/ppermute | solution.py:50
  9.5 5.2 %collective-permute-start.3 = (bf16[32,2048]{1,0:T(8,128)(2,1)}, bf16[32,2048]{1,0:T(8,128)(2,1)S(1)}, u32[]{:S(2)}, u32[]{:S(2)}) collective-permute-start(bf16[32,2048]{1,0:T(8,128)(2,1)} %refs_0_.3), channel_id=1, source_target_pairs={{0,4},{1,5},{2,6},{3,7},{4,0},{5,1},{6,2},{7,3},{8,12},{9,13},{10,... | collective-permute-start | bytes 393224 | tf_op jit(solution)/shard_map/ppermute | solution.py:39
  11.4 6.1 %collective-permute-start.1 = (bf16[32,2048]{1,0:T(8,128)(2,1)}, bf16[32,2048]{1,0:T(8,128)(2,1)S(1)}, u32[]{:S(2)}, u32[]{:S(2)}) collective-permute-start(bf16[32,2048]{1,0:T(8,128)(2,1)} %refs_0_.3), channel_id=1, source_target_pairs={{0,2},{1,3},{2,0},{3,1},{4,6},{5,7},{6,4},{7,5},{8,10},{9,11},{10,... | collective-permute-start | bytes 393224 | tf_op jit(solution)/shard_map/ppermute | solution.py:39
  12.9 4.6 %collective-permute-start = (bf16[32,2048]{1,0:T(8,128)(2,1)}, bf16[32,2048]{1,0:T(8,128)(2,1)S(1)}, u32[]{:S(2)}, u32[]{:S(2)}) collective-permute-start(bf16[32,2048]{1,0:T(8,128)(2,1)} %refs_0_.3), channel_id=1, source_target_pairs={{0,1},{1,0},{2,3},{3,2},{4,5},{5,4},{6,7},{7,6},{8,9},{9,8},{10,11... | collective-permute-start | bytes 393224 | tf_op jit(solution)/shard_map/ppermute | solution.py:41
  14.6 6.1 %collective-permute-start.5 = (bf16[32,2048]{1,0:T(8,128)(2,1)}, bf16[32,2048]{1,0:T(8,128)(2,1)S(1)}, u32[]{:S(2)}, u32[]{:S(2)}) collective-permute-start(bf16[32,2048]{1,0:T(8,128)(2,1)} %refs_0_.3), channel_id=1, source_target_pairs={{0,6},{1,7},{2,4},{3,5},{4,2},{5,3},{6,0},{7,1},{8,14},{9,15},{10,... | collective-permute-start | bytes 393224 | tf_op jit(solution)/shard_map/ppermute | solution.py:39
  17.5 6.0 %collective-permute-start.4 = (bf16[32,2048]{1,0:T(8,128)(2,1)S(1)}, bf16[32,2048]{1,0:T(8,128)(2,1)S(1)}, u32[]{:S(2)}, u32[]{:S(2)}) collective-permute-start(bf16[32,2048]{1,0:T(8,128)(2,1)S(1)} %collective-permute-done.3.refs_4_), channel_id=1, source_target_pairs={{0,1},{1,0},{2,3},{3,2},{4,5},{5,4},{6,7},{7,6},{8,9},{9,8},{10,11... | collective-permute-start | bytes 393224 | tf_op jit(solution)/shard_map/ppermute | solution.py:41
  17.5 6.0 %collective-permute-start.2 = (bf16[32,2048]{1,0:T(8,128)(2,1)S(1)}, bf16[32,2048]{1,0:T(8,128)(2,1)S(1)}, u32[]{:S(2)}, u32[]{:S(2)}) collective-permute-start(bf16[32,2048]{1,0:T(8,128)(2,1)S(1)} %collective-permute-done.1.refs_2_), channel_id=1, source_target_pairs={{0,1},{1,0},{2,3},{3,2},{4,5},{5,4},{6,7},{7,6},{8,9},{9,8},{10,11... | collective-permute-start | bytes 393224 | tf_op jit(solution)/shard_map/ppermute | solution.py:41
  20.7 2.8 %collective-permute-start.6 = (bf16[32,2048]{1,0:T(8,128)(2,1)S(1)}, bf16[32,2048]{1,0:T(8,128)(2,1)S(1)}, u32[]{:S(2)}, u32[]{:S(2)}) collective-permute-start(bf16[32,2048]{1,0:T(8,128)(2,1)S(1)} %collective-permute-done.5.refs_6_), channel_id=1, source_target_pairs={{0,1},{1,0},{2,3},{3,2},{4,5},{5,4},{6,7},{7,6},{8,9},{9,8},{10,11... | collective-permute-start | bytes 393224 | tf_op jit(solution)/shard_map/ppermute | solution.py:41
  20.7 20.3 %collective-permute-start.17 = (bf16[2,64,2048]{2,1,0:T(8,128)(2,1)S(1)}, bf16[2,64,2048]{2,1,0:T(8,128)(2,1)}, u32[]{:S(2)}, u32[]{:S(2)}) collective-permute-start(bf16[2,64,2048]{2,1,0:T(8,128)(2,1)S(1)} %collective-permute-done.16.refs_6_), channel_id=1, source_target_pairs={{8,0},{16,8},{9,1},{17,9},{10,2},{18,10},{11,3},{19,11},{12,4},{20... | collective-permute-start | bytes 1572872 | tf_op jit(solution)/shard_map/ppermute | solution.py:51
  22.1 20.2 %collective-permute-start.14 = (bf16[2,64,2048]{2,1,0:T(8,128)(2,1)}, bf16[2,64,2048]{2,1,0:T(8,128)(2,1)}, u32[]{:S(2)}, u32[]{:S(2)}) collective-permute-start(bf16[2,64,2048]{2,1,0:T(8,128)(2,1)} %collective-permute-done.13.refs_3_), channel_id=1, source_target_pairs={{8,16},{16,24},{9,17},{17,25},{10,18},{18,26},{11,19},{19,27},{12,... | collective-permute-start | bytes 1572872 | tf_op jit(solution)/shard_map/ppermute | solution.py:50
  33.4 13.3 %collective-permute-start.7 = (bf16[64,2048]{1,0:T(8,128)(2,1)}, bf16[64,2048]{1,0:T(8,128)(2,1)S(1)}, u32[]{:S(2)}, u32[]{:S(2)}) collective-permute-start(bf16[64,2048]{1,0:T(8,128)(2,1)} %get-tuple-element.19), channel_id=1, source_target_pairs={{0,24},{8,0},{16,8},{24,16},{1,25},{9,1},{17,9},{25,17},{2,26},{10... | collective-permute-start | bytes 786440 | tf_op jit(solution)/shard_map/ppermute | solution.py:250
  35.8 28.3 %collective-permute-start.8 = (bf16[64,2048]{1,0:T(8,128)(2,1)}, bf16[64,2048]{1,0:T(8,128)(2,1)S(1)}, u32[]{:S(2)}, u32[]{:S(2)}) collective-permute-start(bf16[64,2048]{1,0:T(8,128)(2,1)} %get-tuple-element.20), channel_id=1, source_target_pairs={{0,16},{8,24},{16,0},{24,8},{1,17},{9,25},{17,1},{25,9},{2,18},{10... | collective-permute-start | bytes 786440 | tf_op jit(solution)/shard_map/ppermute | solution.py:250
  40.8 23.3 %collective-permute-start.9 = (bf16[64,2048]{1,0:T(8,128)(2,1)}, bf16[64,2048]{1,0:T(8,128)(2,1)S(1)}, u32[]{:S(2)}, u32[]{:S(2)}) collective-permute-start(bf16[64,2048]{1,0:T(8,128)(2,1)} %get-tuple-element.21), channel_id=1, source_target_pairs={{0,8},{8,16},{16,24},{24,0},{1,9},{9,17},{17,25},{25,1},{2,10},{10... | collective-permute-start | bytes 786440 | tf_op jit(solution)/shard_map/ppermute | solution.py:250
  41.0 28.2 %collective-permute-start.18 = (bf16[2,64,2048]{2,1,0:T(8,128)(2,1)}, bf16[2,64,2048]{2,1,0:T(8,128)(2,1)S(1)}, u32[]{:S(2)}, u32[]{:S(2)}) collective-permute-start(bf16[2,64,2048]{2,1,0:T(8,128)(2,1)} %collective-permute-done.17.refs_7_), channel_id=1, source_target_pairs={{8,0},{9,1},{10,2},{11,3},{12,4},{13,5},{14,6},{15,7}} | collective-permute-start | bytes 1572872 | tf_op jit(solution)/shard_map/ppermute | solution.py:51
  42.3 26.9 %collective-permute-start.15 = (bf16[2,64,2048]{2,1,0:T(8,128)(2,1)}, bf16[2,64,2048]{2,1,0:T(8,128)(2,1)S(1)}, u32[]{:S(2)}, u32[]{:S(2)}) collective-permute-start(bf16[2,64,2048]{2,1,0:T(8,128)(2,1)} %collective-permute-done.14.refs_4_), channel_id=1, source_target_pairs={{16,24},{17,25},{18,26},{19,27},{20,28},{21,29},{22,30},{23,31}} | collective-permute-start | bytes 1572872 | tf_op jit(solution)/shard_map/ppermute | solution.py:50
  64.2 13.7 %collective-permute-start.12 = (bf16[64,2048]{1,0:T(8,128)(2,1)S(1)}, bf16[64,2048]{1,0:T(8,128)(2,1)S(1)}, u32[]{:S(2)}, u32[]{:S(2)}) collective-permute-start(bf16[64,2048]{1,0:T(8,128)(2,1)S(1)} %add_convert_fusion.refs_0_), channel_id=1, source_target_pairs={{0,24},{8,0},{16,8},{24,16},{1,25},{9,1},{17,9},{25,17},{2,26},{10... | collective-permute-start | bytes 786440 | tf_op jit(solution)/shard_map/ppermute | solution.py:252
  64.3 23.5 %collective-permute-start.11 = (bf16[64,2048]{1,0:T(8,128)(2,1)S(1)}, bf16[64,2048]{1,0:T(8,128)(2,1)S(1)}, u32[]{:S(2)}, u32[]{:S(2)}) collective-permute-start(bf16[64,2048]{1,0:T(8,128)(2,1)S(1)} %add_convert_fusion.refs_0_), channel_id=1, source_target_pairs={{0,16},{8,24},{16,0},{24,8},{1,17},{9,25},{17,1},{25,9},{2,18},{10... | collective-permute-start | bytes 786440 | tf_op jit(solution)/shard_map/ppermute | solution.py:252
  65.1 22.7 %collective-permute-start.10 = (bf16[64,2048]{1,0:T(8,128)(2,1)S(1)}, bf16[64,2048]{1,0:T(8,128)(2,1)S(1)}, u32[]{:S(2)}, u32[]{:S(2)}) collective-permute-start(bf16[64,2048]{1,0:T(8,128)(2,1)S(1)} %add_convert_fusion.refs_0_), channel_id=1, source_target_pairs={{0,8},{8,16},{16,24},{24,0},{1,9},{9,17},{17,25},{25,1},{2,10},{10... | collective-permute-start | bytes 786440 | tf_op jit(solution)/shard_map/ppermute | solution.py:252
  99.1 10.0 %collective-permute-start.19 = (bf16[128,2048]{1,0:T(8,128)(2,1)S(1)}, bf16[128,2048]{1,0:T(8,128)(2,1)S(1)}, u32[]{:S(2)}, u32[]{:S(2)}) collective-permute-start(bf16[128,2048]{1,0:T(8,128)(2,1)S(1)} %get-tuple-element.26), channel_id=1, source_target_pairs={{0,1},{1,0},{2,3},{3,2},{4,5},{5,4},{6,7},{7,6},{8,9},{9,8},{10,11... | collective-permute-start | bytes 1572872 | tf_op jit(solution)/shard_map/ppermute | solution.py:260
  99.2 5.9 %collective-permute-start.26 = (bf16[32,2048]{1,0:T(8,128)(2,1)S(1)}, bf16[32,2048]{1,0:T(8,128)(2,1)S(1)}, u32[]{:S(2)}, u32[]{:S(2)}) collective-permute-start(bf16[32,2048]{1,0:T(8,128)(2,1)S(1)} %copy-done.4), channel_id=1, source_target_pairs={{0,4},{1,5},{2,6},{3,7},{4,0},{5,1},{6,2},{7,3},{8,12},{9,13},{10,... | collective-permute-start | bytes 393224 | tf_op jit(solution)/shard_map/ppermute | solution.py:39
  100.8 6.3 %collective-permute-start.24 = (bf16[32,2048]{1,0:T(8,128)(2,1)S(1)}, bf16[32,2048]{1,0:T(8,128)(2,1)S(1)}, u32[]{:S(2)}, u32[]{:S(2)}) collective-permute-start(bf16[32,2048]{1,0:T(8,128)(2,1)S(1)} %copy-done.4), channel_id=1, source_target_pairs={{0,2},{1,3},{2,0},{3,1},{4,6},{5,7},{6,4},{7,5},{8,10},{9,11},{10,... | collective-permute-start | bytes 393224 | tf_op jit(solution)/shard_map/ppermute | solution.py:39
  102.3 6.8 %collective-permute-start.28 = (bf16[32,2048]{1,0:T(8,128)(2,1)S(1)}, bf16[32,2048]{1,0:T(8,128)(2,1)S(1)}, u32[]{:S(2)}, u32[]{:S(2)}) collective-permute-start(bf16[32,2048]{1,0:T(8,128)(2,1)S(1)} %copy-done.4), channel_id=1, source_target_pairs={{0,6},{1,7},{2,4},{3,5},{4,2},{5,3},{6,0},{7,1},{8,14},{9,15},{10,... | collective-permute-start | bytes 393224 | tf_op jit(solution)/shard_map/ppermute | solution.py:39
  102.8 8.1 %collective-permute-start.23 = (bf16[32,2048]{1,0:T(8,128)(2,1)S(1)}, bf16[32,2048]{1,0:T(8,128)(2,1)S(1)}, u32[]{:S(2)}, u32[]{:S(2)}) collective-permute-start(bf16[32,2048]{1,0:T(8,128)(2,1)S(1)} %copy-done.4), channel_id=1, source_target_pairs={{0,1},{1,0},{2,3},{3,2},{4,5},{5,4},{6,7},{7,6},{8,9},{9,8},{10,11... | collective-permute-start | bytes 393224 | tf_op jit(solution)/shard_map/ppermute | solution.py:41
  105.1 7.2 %collective-permute-start.27 = (bf16[32,2048]{1,0:T(8,128)(2,1)S(1)}, bf16[32,2048]{1,0:T(8,128)(2,1)S(1)}, u32[]{:S(2)}, u32[]{:S(2)}) collective-permute-start(bf16[32,2048]{1,0:T(8,128)(2,1)S(1)} %collective-permute-done.26.refs_4_), channel_id=1, source_target_pairs={{0,1},{1,0},{2,3},{3,2},{4,5},{5,4},{6,7},{7,6},{8,9},{9,8},{10,11... | collective-permute-start | bytes 393224 | tf_op jit(solution)/shard_map/ppermute | solution.py:41
  107.1 5.7 %collective-permute-start.25 = (bf16[32,2048]{1,0:T(8,128)(2,1)S(1)}, bf16[32,2048]{1,0:T(8,128)(2,1)S(1)}, u32[]{:S(2)}, u32[]{:S(2)}) collective-permute-start(bf16[32,2048]{1,0:T(8,128)(2,1)S(1)} %collective-permute-done.24.refs_2_), channel_id=1, source_target_pairs={{0,1},{1,0},{2,3},{3,2},{4,5},{5,4},{6,7},{7,6},{8,9},{9,8},{10,11... | collective-permute-start | bytes 393224 | tf_op jit(solution)/shard_map/ppermute | solution.py:41
  109.1 3.8 %collective-permute-start.29 = (bf16[32,2048]{1,0:T(8,128)(2,1)S(1)}, bf16[32,2048]{1,0:T(8,128)(2,1)S(1)}, u32[]{:S(2)}, u32[]{:S(2)}) collective-permute-start(bf16[32,2048]{1,0:T(8,128)(2,1)S(1)} %collective-permute-done.28.refs_6_), channel_id=1, source_target_pairs={{0,1},{1,0},{2,3},{3,2},{4,5},{5,4},{6,7},{7,6},{8,9},{9,8},{10,11... | collective-permute-start | bytes 393224 | tf_op jit(solution)/shard_map/ppermute | solution.py:41
  109.3 11.6 %collective-permute-start.20 = (bf16[32,2048]{1,0:T(8,128)(2,1)S(1)}, bf16[32,2048]{1,0:T(8,128)(2,1)S(1)}, u32[]{:S(2)}, u32[]{:S(2)}) collective-permute-start(bf16[32,2048]{1,0:T(8,128)(2,1)S(1)} %get-tuple-element.34), channel_id=1, source_target_pairs={{0,2},{1,3},{2,0},{3,1},{4,6},{5,7},{6,4},{7,5},{8,10},{9,11},{10,... | collective-permute-start | bytes 393224 | tf_op jit(solution)/shard_map/ppermute | solution.py:265
  110.9 10.1 %collective-permute-start.22 = (bf16[32,2048]{1,0:T(8,128)(2,1)S(1)}, bf16[32,2048]{1,0:T(8,128)(2,1)S(1)}, u32[]{:S(2)}, u32[]{:S(2)}) collective-permute-start(bf16[32,2048]{1,0:T(8,128)(2,1)S(1)} %get-tuple-element.35), channel_id=1, source_target_pairs={{0,6},{1,7},{2,4},{3,5},{4,2},{5,3},{6,0},{7,1},{8,14},{9,15},{10,... | collective-permute-start | bytes 393224 | tf_op jit(solution)/shard_map/ppermute | solution.py:265
  112.4 8.6 %collective-permute-start.21 = (bf16[32,2048]{1,0:T(8,128)(2,1)S(1)}, bf16[32,2048]{1,0:T(8,128)(2,1)S(1)}, u32[]{:S(2)}, u32[]{:S(2)}) collective-permute-start(bf16[32,2048]{1,0:T(8,128)(2,1)S(1)} %get-tuple-element.36), channel_id=1, source_target_pairs={{0,4},{1,5},{2,6},{3,7},{4,0},{5,1},{6,2},{7,3},{8,12},{9,13},{10,... | collective-permute-start | bytes 393224 | tf_op jit(solution)/shard_map/ppermute | solution.py:265
  (3 other events, 15.7 us)

commit v2 on v1

v2 whole, which is shorter than its diff:
```python
import functools
import math

import jax
import jax.numpy as jnp
from jax import lax
from jax.experimental import pallas as pl
from jax.experimental.pallas import tpu as pltpu
from jax.sharding import PartitionSpec as P

F32, BF16 = jnp.float32, jnp.bfloat16
MIB = 1024 * 1024
STRIPE = 256


def stripe(extent):
    return math.gcd(extent, STRIPE)


def params(mib):
    return pltpu.CompilerParams(vmem_limit_bytes=mib * MIB)


def flip(count, mask):
    return [(i, i ^ mask) for i in range(count)]


def turn(count, shift):
    return [(i, (i + shift) % count) for i in range(count)]


def gather_row(own, n_row):
    mine = jnp.stack([own] + [lax.ppermute(own, "row", flip(n_row, mask)) for mask in range(2, n_row, 2)])
    return mine, lax.ppermute(mine, "row", flip(n_row, 1))


def relay_col(own, n_col):
    from_low, from_high = [own], [own]
    for step in range(1, n_col):
        up = [(i, i + 1) for i in range(step - 1, n_col - 1)]
        down = [(i, i - 1) for i in range(1, n_col - step + 1)]
        from_low.append(lax.ppermute(from_low[-1], "col", up))
        from_high.append(lax.ppermute(from_high[-1], "col", down))
    return from_low, from_high


def fetch_kernel(count, *refs):
    sources, targets, arrived = refs[:count], refs[-1 - count : -1], refs[-1]
    copies = []
    for k in range(count):
        rows = sources[k].shape[0] // arrived.shape[1]
        for i in range(arrived.shape[1]):
            at = pl.ds(i * rows, rows)
            copies.append(pltpu.make_async_copy(sources[k].at[at, :], targets[k].at[at, :], arrived.at[k, i]))
            copies[-1].start()
    for copy in copies:
        copy.wait()


def fetch(weights, after=()):
    size = sum(w.size * 2 for w in weights)
    return pl.pallas_call(
        functools.partial(fetch_kernel, len(weights)),
        in_specs=[IN_HBM] * len(weights) + [IN_ANY] * len(after),
        out_specs=[IN_VMEM] * len(weights),
        out_shape=[jax.ShapeDtypeStruct(w.shape, w.dtype) for w in weights],
        scratch_shapes=[pltpu.SemaphoreType.DMA((len(weights), 4))],
        compiler_params=params(1),
        cost_estimate=pl.CostEstimate(flops=0, bytes_accessed=size, transcendentals=0),
        name="fetch",
    )(*weights, *after)


def store(buffer, hbm, semaphores, i):
    rows = buffer.shape[0] // semaphores.shape[0]
    at = pl.ds(i * rows, rows)
    copy = pltpu.make_async_copy(buffer.at[at, :], hbm.at[at, :], semaphores.at[i])
    copy.start()
    return copy


IN_VMEM = pl.BlockSpec(memory_space=pltpu.VMEM)
IN_SMEM = pl.BlockSpec(memory_space=pltpu.SMEM)
IN_HBM = pl.BlockSpec(memory_space=pltpu.HBM)
IN_ANY = pl.BlockSpec(memory_space=pl.ANY)
NT = (((1,), (1,)), ((), ()))
TN = (((0,), (0,)), ((), ()))


def hidden_kernel(n_row, n_col, offsets, mine, theirs, weight, grad_all, own, *sends):
    rows, part = mine.shape[1], own.shape[0]
    for x in range(n_row):
        grad_all[pl.ds(pl.multiple_of(offsets[x], rows), rows), :] = (theirs if x % 2 else mine)[x // 2]
    step = stripe(weight.shape[0])
    for i in range(weight.shape[0] // step):
        at = slice(i * step, (i + 1) * step)
        total = lax.dot_general(grad_all[...], weight[at, :], NT, preferred_element_type=F32)
        own[:, at] = total[:part]
        for j in range(1, n_col):
            sends[j - 1][:, at] = total[j * part : (j + 1) * part].astype(BF16)


def partial_hidden(mine, theirs, weight, offsets, n_col):
    n_row, rows, width = 2 * mine.shape[0], mine.shape[1], mine.shape[2]
    units = weight.shape[0]
    tokens = rows * n_row
    part = tokens // n_col
    return pl.pallas_call(
        functools.partial(hidden_kernel, n_row, n_col),
        in_specs=[IN_SMEM] + [IN_VMEM] * 3,
        out_specs=[IN_VMEM] * (1 + n_col),
        out_shape=[jax.ShapeDtypeStruct((tokens, width), BF16), jax.ShapeDtypeStruct((part, units), F32)]
        + [jax.ShapeDtypeStruct((part, units), BF16)] * (n_col - 1),
        compiler_params=params(8),
        cost_estimate=pl.CostEstimate(
            flops=2 * tokens * width * units, bytes_accessed=2 * units * width, transcendentals=0
        ),
        name="partial_hidden",
    )(offsets, mine, theirs, weight)


def down_kernel(n_col, scale, place, *refs):
    gate, up, grad_all, mine, theirs = refs[:5]
    from_low, from_high = refs[5 : 4 + n_col], refs[4 + n_col : 3 + 2 * n_col]
    down_grad, up_factor, gate_factor, input_all, buffer, left = refs[3 + 2 * n_col :]
    blocks, rows = mine.shape[:2]
    for k in range(blocks):
        input_all[k * rows : (k + 1) * rows, :] = mine[k]
        input_all[(blocks + k) * rows : (blocks + k + 1) * rows, :] = theirs[k]
    part, units = gate.shape
    step = units // left.shape[0]
    copies = []
    for i in range(left.shape[0]):
        at = slice(i * step, (i + 1) * step)
        hidden = []
        for j in range(n_col):
            if j == 0:
                g, u = gate[:, at], up[:, at]
            else:
                low = place[0] >= j
                g = jnp.where(low, from_low[j - 1][0, :, at], from_high[n_col - j - 1][0, :, at])
                u = jnp.where(low, from_low[j - 1][1, :, at], from_high[n_col - j - 1][1, :, at])
            g, u = g.astype(F32), u.astype(F32)
            s = 1.0 / (1.0 + jnp.exp(-g))
            silu = g * s
            hidden.append((silu * u).astype(BF16))
            up_factor[j * part : (j + 1) * part, at] = silu
            gate_factor[j * part : (j + 1) * part, at] = u * s * (1.0 + g * (1.0 - s))
        product = lax.dot_general(
            jnp.concatenate(hidden, axis=0), grad_all[...], TN, preferred_element_type=F32
        )
        buffer[at, :] = (product * scale).astype(BF16)
        copies.append(store(buffer, down_grad, left, i))
    for copy in copies:
        copy.wait()


def down_gradient(gate, up, grad_all, mine, theirs, from_low, from_high, place, scale):
    n_col = len(from_low)
    part, units = gate.shape
    tokens, width = grad_all.shape
    return pl.pallas_call(
        functools.partial(down_kernel, n_col, scale),
        in_specs=[IN_SMEM] + [IN_VMEM] * (2 * n_col + 3),
        out_specs=[IN_HBM] + [IN_VMEM] * 3,
        out_shape=[jax.ShapeDtypeStruct((units, width), BF16)]
        + [jax.ShapeDtypeStruct((tokens, units), F32)] * 2
        + [jax.ShapeDtypeStruct((tokens, width), BF16)],
        scratch_shapes=[pltpu.VMEM((units, width), BF16), pltpu.SemaphoreType.DMA((units // stripe(units),))],
        compiler_params=params(16),
        cost_estimate=pl.CostEstimate(
            flops=2 * tokens * width * units,
            bytes_accessed=2 * units * width + 12 * tokens * units,
            transcendentals=tokens * units,
        ),
        name="down_gradient",
    )(place, gate, up, grad_all, mine, theirs, *from_low[1:], *from_high[1:])


def input_kernel(n_row, n_col, offsets, *refs):
    hidden_grad, refs = refs[:n_col], refs[n_col:]
    up_factor, gate_factor, gate_weight, up_weight, gate_term, up_term, own, other = refs
    part = hidden_grad[0].shape[0]
    rows = part * n_col // n_row
    half = own.shape[0]
    for j in range(n_col):
        h = hidden_grad[j][...].astype(F32)
        at = slice(j * part, (j + 1) * part)
        terms = ((gate_term, (h * gate_factor[at, :]).astype(BF16)), (up_term, (h * up_factor[at, :]).astype(BF16)))
        for c in range(part // rows):
            to = pl.ds(pl.multiple_of(offsets[j * (part // rows) + c], rows), rows)
            for ref, term in terms:
                ref[to, :] = term[c * rows : (c + 1) * rows]
    step = stripe(own.shape[1])
    for i in range(own.shape[1] // step):
        at = slice(i * step, (i + 1) * step)
        total = lax.dot_general(gate_term[...], gate_weight[at, :], NT, preferred_element_type=F32)
        total += lax.dot_general(up_term[...], up_weight[at, :], NT, preferred_element_type=F32)
        own[:, at] = total[:half]
        other[:, at] = total[half:]


def partial_input(hidden_grad, up_factor, gate_factor, gate_weight, up_weight, offsets, n_row):
    n_col = len(hidden_grad)
    part, units = hidden_grad[0].shape
    tokens = part * n_col
    width = gate_weight.shape[0]
    return pl.pallas_call(
        functools.partial(input_kernel, n_row, n_col),
        in_specs=[IN_SMEM] + [IN_VMEM] * (n_col + 4),
        out_specs=[IN_VMEM] * 4,
        out_shape=[jax.ShapeDtypeStruct((tokens, units), BF16)] * 2
        + [jax.ShapeDtypeStruct((tokens // 2, width), F32)] * 2,
        compiler_params=params(8),
        cost_estimate=pl.CostEstimate(
            flops=4 * tokens * width * units, bytes_accessed=4 * units * width, transcendentals=0
        ),
        name="partial_input",
    )(offsets, *hidden_grad, up_factor, gate_factor, gate_weight, up_weight)


def weight_kernel(scale, input_all, gate_term, up_term, gate_grad, up_grad, buffers, left):
    step = buffers.shape[1] // left.shape[1]
    copies = []
    for i in range(left.shape[1]):
        at = slice(i * step, (i + 1) * step)
        for k, (term, out) in enumerate(((gate_term, gate_grad), (up_term, up_grad))):
            product = lax.dot_general(input_all[:, at], term[...], TN, preferred_element_type=F32)
            buffers[k, at, :] = (product * scale).astype(BF16)
            copies.append(store(buffers.at[k], out, left.at[k], i))
    for copy in copies:
        copy.wait()


def weight_gradients(input_all, gate_term, up_term, scale):
    tokens, width = input_all.shape
    units = gate_term.shape[1]
    return pl.pallas_call(
        functools.partial(weight_kernel, scale),
        in_specs=[IN_VMEM] * 3,
        out_specs=[IN_HBM] * 2,
        out_shape=[jax.ShapeDtypeStruct((width, units), BF16)] * 2,
        scratch_shapes=[
            pltpu.VMEM((2, width, units), BF16),
            pltpu.SemaphoreType.DMA((2, width // stripe(width))),
        ],
        compiler_params=params(24),
        cost_estimate=pl.CostEstimate(
            flops=4 * tokens * width * units, bytes_accessed=4 * units * width, transcendentals=0
        ),
        name="weight_gradients",
    )(input_all, gate_term, up_term)


def per_device(inputs, grad_out, gate_pre, up_pre, gate_weight, up_weight, down_weight):
    n_row, n_col = lax.axis_size("row"), lax.axis_size("col")
    row, col = lax.axis_index("row"), lax.axis_index("col")
    rows = grad_out.shape[0]
    tokens = rows * n_row
    share = n_row // n_col
    scale = 1.0 / math.sqrt(tokens)

    block = row ^ jnp.arange(n_row, dtype=jnp.int32)
    part_offsets = (jnp.mod(col - block // share, n_col) * share + block % share) * rows
    block = (jnp.mod(col - jnp.arange(n_col, dtype=jnp.int32), n_col)[:, None] * share + jnp.arange(share)).reshape(-1)
    seen = block ^ row
    block_offsets = ((seen % 2) * (n_row // 2) + seen // 2) * rows

    (fetched,) = fetch([down_weight])
    grad_mine, grad_theirs = gather_row(grad_out, n_row)
    from_low, from_high = relay_col(jnp.stack([gate_pre, up_pre]), n_col)
    grad_all, own, *sends = partial_hidden(
        grad_mine, grad_theirs, fetched, part_offsets.astype(jnp.int32), n_col
    )
    for j, send in enumerate(sends, 1):
        own = own + lax.ppermute(send, "col", turn(n_col, -j)).astype(F32)
    own = own.astype(BF16)
    hidden_grad = [own] + [lax.ppermute(own, "col", turn(n_col, j)) for j in range(1, n_col)]

    input_mine, input_theirs = gather_row(inputs, n_row)
    down_grad, up_factor, gate_factor, input_all = down_gradient(
        gate_pre, up_pre, grad_all, input_mine, input_theirs, from_low, from_high, col[None].astype(jnp.int32), scale
    )
    gate_fetched, up_fetched = fetch([gate_weight, up_weight], after=[own])
    gate_term, up_term, mine, other = partial_input(
        hidden_grad, up_factor, gate_factor, gate_fetched, up_fetched, block_offsets.astype(jnp.int32), n_row
    )
    mine = mine + lax.ppermute(other, "row", flip(n_row, 1))
    input_grad = mine[:rows]
    for k in range(1, n_row // 2):
        away = mine[k * rows : (k + 1) * rows].astype(BF16)
        input_grad = input_grad + lax.ppermute(away, "row", flip(n_row, 2 * k)).astype(F32)
    gate_grad, up_grad = weight_gradients(input_all, gate_term, up_term, scale)
    return (input_grad.astype(BF16), gate_grad, up_grad, down_grad)


def solution(mesh):
    return jax.shard_map(
        per_device,
        mesh=mesh,
        in_specs=(
            P("row", "col"),
            P("row", "col"),
            P("col", "row"),
            P("col", "row"),
            P("col", "row"),
            P("col", "row"),
            P("row", "col"),
        ),
        out_specs=(P("row", "col"), P("col", "row"), P("col", "row"), P("row", "col")),
        check_vma=False,
    )
```

time: 122 us -> 113 us (0.926)
  waiting for transfers between devices: 43.8 us -> 23.9 us
  starting transfers between devices: 36.7 us -> 48.4 us
  Pallas kernels: 33.7 us -> 23.7 us
  local copies, waits for them, and re-layouts: 4.41 us -> 10.5 us
  other arithmetic: 2.24 us -> 5.23 us
    ppermute x3, starting transfers between devices: 2.82 us -> 15.9 us  [per_device(): lax.ppermute(own, 'col', turn(n_col, j))]
    pallas_call x4 -> x6, Pallas kernels: 33.7 us -> 23.7 us  [the longest x1 6.43 us: weight_gradients(): pl.pallas_call(functools.partial(weight_kernel, scale), in_specs=[IN_VMEM...]
    ppermute x3, waiting for transfers between devices: 9.81 us -> 0.01 us  [per_device(): lax.ppermute(own, 'col', turn(n_col, j))]
    ppermute x15 -> x9, waiting for transfers between devices: 10.8 us -> 2.67 us  [the longest x1 2.65 us: per_device(): mine = mine + lax.ppermute(other, 'row', flip(n_row, 1))]
    unnamed x10 -> x12, local copies, waits for them, and re-layouts: 4.29 us -> 10.4 us
    ppermute x3, waiting for transfers between devices: 2.09 us -> 0.01 us  [relay_col(): from_high.append(lax.ppermute(from_high[-1], 'col', down))]
    another operation x1 -> x3, other arithmetic: 0.15 us -> 2.1 us  [the longest x2 1.95 us: gather_row(): jnp.stack([own] + [lax.ppermute(own, 'row', flip(n_row, mask)) for mask i...]
    ppermute x15 -> x9, starting transfers between devices: 10.5 us -> 9.36 us  [the longest x6 9.21 us: gather_row(): lax.ppermute(own, 'row', flip(n_row, mask))]
  transfers between devices with their start and end apart: 30 -> 24, of which waited for: 9 -> 4; matrix products, arithmetic and copies ran while one was open for 0% -> 4% of each run, Pallas kernels for 18% -> 16%
where the time goes in v2:
time: 113 us
  starting transfers between devices  48.4 us (43%)
  waiting for transfers between devices  23.9 us (21%)
  Pallas kernels  23.7 us (21%)
  local copies, waits for them, and re-layouts  10.5 us (9%)
  other arithmetic  5.23 us (5%)
    ppermute x3, waiting for transfers between devices, per_device(): own = own + lax.ppermute(send, 'col', turn(n_col, -j)).astype(F32)  20.1 us
    ppermute x3, starting transfers between devices, per_device(): lax.ppermute(own, 'col', turn(n_col, j))  15.9 us
    unnamed x12, local copies, waits for them, and re-layouts  10.4 us
    ppermute x6, starting transfers between devices, gather_row(): lax.ppermute(own, 'row', flip(n_row, mask))  9.21 us
    ppermute x3, starting transfers between devices, per_device(): own = own + lax.ppermute(send, 'col', turn(n_col, -j)).astype(F32)  8.26 us
    ppermute x3, starting transfers between devices, relay_col(): from_low.append(lax.ppermute(from_low[-1], 'col', up))  7.54 us
    pallas_call x1, Pallas kernels, weight_gradients(): pl.pallas_call(functools.partial(weight_kernel, scale), in_specs=[IN_VMEM...  6.43 us
    pallas_call x1, Pallas kernels, down_gradient(): pl.pallas_call(functools.partial(down_kernel, n_col, scale), in_specs=[IN...  5.91 us
  transfers between devices with their start and end apart: 24, of which 4 were waited for; matrix products, arithmetic and copies ran while one was open for 4% of the time, Pallas kernels for 16%

profile of v2, /device:TPU:0, one launch (start us, length us, event | category | flops | bytes accessed | tf_op | source)
XLA Modules:
  0.0 112.7 jit_solution(8972711137824870120)
XLA Ops:
  0.6 3.0 %collective-permute-start = (bf16[32,2048]{1,0:T(8,128)(2,1)}, bf16[32,2048]{1,0:T(8,128)(2,1)S(1)}, u32[]{:S(2)}, u32[]{:S(2)}) collective-permute-start(bf16[32,2048]{1,0:T(8,128)(2,1)} %param.8), channel_id=1, source_target_pairs={{0,2},{1,3},{2,0},{3,1},{4,6},{5,7},{6,4},{7,5},{8,10},{9,11},{10,... | collective-permute-start | bytes 393224 | tf_op jit(solution)/shard_map/ppermute | solution.py:33
  3.6 1.5 %collective-permute-start.2 = (bf16[32,2048]{1,0:T(8,128)(2,1)}, bf16[32,2048]{1,0:T(8,128)(2,1)S(1)}, u32[]{:S(2)}, u32[]{:S(2)}) collective-permute-start(bf16[32,2048]{1,0:T(8,128)(2,1)} %param.8), channel_id=1, source_target_pairs={{0,6},{1,7},{2,4},{3,5},{4,2},{5,3},{6,0},{7,1},{8,14},{9,15},{10,... | collective-permute-start | bytes 393224 | tf_op jit(solution)/shard_map/ppermute | solution.py:33
  5.2 1.1 pad_maximum_fusion.2
  6.3 1.3 %collective-permute-start.17 = (bf16[2,64,2048]{2,1,0:T(8,128)(2,1)S(1)}, bf16[2,64,2048]{2,1,0:T(8,128)(2,1)S(1)}, u32[]{:S(2)}, u32[]{:S(2)}) collective-permute-start(bf16[2,64,2048]{2,1,0:T(8,128)(2,1)S(1)} %pad_maximum_fusion.2), channel_id=1, source_target_pairs={{8,0},{16,8},{24,16},{9,1},{17,9},{25,17},{10,2},{18,10},{26,18},{... | collective-permute-start | bytes 1572872 | tf_op jit(solution)/shard_map/ppermute | solution.py:43
  7.6 5.4 %collective-permute-start.14 = (bf16[2,64,2048]{2,1,0:T(8,128)(2,1)S(1)}, bf16[2,64,2048]{2,1,0:T(8,128)(2,1)}, u32[]{:S(2)}, u32[]{:S(2)}) collective-permute-start(bf16[2,64,2048]{2,1,0:T(8,128)(2,1)S(1)} %pad_maximum_fusion.2), channel_id=1, source_target_pairs={{0,8},{8,16},{16,24},{1,9},{9,17},{17,25},{2,10},{10,18},{18,26},{... | collective-permute-start | bytes 1572872 | tf_op jit(solution)/shard_map/ppermute | solution.py:42
  12.9 1.0 pad_maximum_fusion.mine
  14.0 2.0 %collective-permute-start.10 = (bf16[32,2048]{1,0:T(8,128)(2,1)}, bf16[32,2048]{1,0:T(8,128)(2,1)S(1)}, u32[]{:S(2)}, u32[]{:S(2)}) collective-permute-start(bf16[32,2048]{1,0:T(8,128)(2,1)} %param.7), channel_id=1, source_target_pairs={{0,2},{1,3},{2,0},{3,1},{4,6},{5,7},{6,4},{7,5},{8,10},{9,11},{10,... | collective-permute-start | bytes 393224 | tf_op jit(solution)/shard_map/ppermute | solution.py:33
  16.0 1.5 %collective-permute-start.12 = (bf16[32,2048]{1,0:T(8,128)(2,1)}, bf16[32,2048]{1,0:T(8,128)(2,1)}, u32[]{:S(2)}, u32[]{:S(2)}) collective-permute-start(bf16[32,2048]{1,0:T(8,128)(2,1)} %param.7), channel_id=1, source_target_pairs={{0,6},{1,7},{2,4},{3,5},{4,2},{5,3},{6,0},{7,1},{8,14},{9,15},{10,... | collective-permute-start | bytes 393224 | tf_op jit(solution)/shard_map/ppermute | solution.py:33
  17.5 3.4 %copy-done = bf16[2048,2048]{1,0:T(8,128)(2,1)S(1)} copy-done((bf16[2048,2048]{1,0:T(8,128)(2,1)S(1)}, bf16[2048,2048]{1,0:T(8,128)(2,1)}, u32[]{:S(2)}) %copy-start) | copy-done | bytes 8388632
  21.8 1.2 %collective-permute-start.11 = (bf16[32,2048]{1,0:T(8,128)(2,1)S(1)}, bf16[32,2048]{1,0:T(8,128)(2,1)S(1)}, u32[]{:S(2)}, u32[]{:S(2)}) collective-permute-start(bf16[32,2048]{1,0:T(8,128)(2,1)S(1)} %copy-done.5), channel_id=1, source_target_pairs={{0,4},{1,5},{2,6},{3,7},{4,0},{5,1},{6,2},{7,3},{8,12},{9,13},{10,... | collective-permute-start | bytes 393224 | tf_op jit(solution)/shard_map/ppermute | solution.py:33
  23.0 1.3 %collective-permute-start.18 = (bf16[2,64,2048]{2,1,0:T(8,128)(2,1)S(1)}, bf16[2,64,2048]{2,1,0:T(8,128)(2,1)}, u32[]{:S(2)}, u32[]{:S(2)}) collective-permute-start(bf16[2,64,2048]{2,1,0:T(8,128)(2,1)S(1)} %collective-permute-done.17.refs_8_), channel_id=1, source_target_pairs={{8,0},{16,8},{9,1},{17,9},{10,2},{18,10},{11,3},{19,11},{12,4},{20... | collective-permute-start | bytes 1572872 | tf_op jit(solution)/shard_map/ppermute | solution.py:43
  24.3 1.5 %collective-permute-start.15 = (bf16[2,64,2048]{2,1,0:T(8,128)(2,1)}, bf16[2,64,2048]{2,1,0:T(8,128)(2,1)}, u32[]{:S(2)}, u32[]{:S(2)}) collective-permute-start(bf16[2,64,2048]{2,1,0:T(8,128)(2,1)} %collective-permute-done.14.refs_5_), channel_id=1, source_target_pairs={{8,16},{16,24},{9,17},{17,25},{10,18},{18,26},{11,19},{19,27},{12,... | collective-permute-start | bytes 1572872 | tf_op jit(solution)/shard_map/ppermute | solution.py:42
  25.7 3.6 %partial_hidden.1 = (bf16[256,2048]{1,0:T(8,128)(2,1)S(1)}, f32[64,2048]{1,0:T(8,128)S(1)}, bf16[64,2048]{1,0:T(8,128)(2,1)S(1)}, bf16[64,2048]{1,0:T(8,128)(2,1)}, bf16[64,2048]{1,0:T(8,128)(2,1)S(1)}) custom-call(s32[8]{0:T(128)S(1)} %fusion.10.offsets, bf16[4,32,2048]{2,1,0:T(8,128)(2,1)S(1)} %pad_maximum_fusion.mine, ...), custom_call_target="tpu_custom_call" | custom-call | flops 2147483648 | bytes 8388608 | tf_op jit(solution)/shard_map/partial_hidden/pallas_call | solution.py:108
  29.4 4.3 %collective-permute-start.4 = (bf16[64,2048]{1,0:T(8,128)(2,1)S(1)}, bf16[64,2048]{1,0:T(8,128)(2,1)}, u32[]{:S(2)}, u32[]{:S(2)}) collective-permute-start(bf16[64,2048]{1,0:T(8,128)(2,1)S(1)} %get-tuple-element.22), channel_id=1, source_target_pairs={{0,24},{8,0},{16,8},{24,16},{1,25},{9,1},{17,9},{25,17},{2,26},{10... | collective-permute-start | bytes 786440 | tf_op jit(solution)/shard_map/ppermute | solution.py:276
  33.6 4.0 %collective-permute-start.5 = (bf16[64,2048]{1,0:T(8,128)(2,1)}, bf16[64,2048]{1,0:T(8,128)(2,1)}, u32[]{:S(2)}, u32[]{:S(2)}) collective-permute-start(bf16[64,2048]{1,0:T(8,128)(2,1)} %get-tuple-element.23), channel_id=1, source_target_pairs={{0,16},{8,24},{16,0},{24,8},{1,17},{9,25},{17,1},{25,9},{2,18},{10... | collective-permute-start | bytes 786440 | tf_op jit(solution)/shard_map/ppermute | solution.py:276
  38.6 5.0 %collective-permute-done.4 = bf16[64,2048]{1,0:T(8,128)(2,1)} collective-permute-done((bf16[64,2048]{1,0:T(8,128)(2,1)S(1)}, bf16[64,2048]{1,0:T(8,128)(2,1)}, u32[]{:S(2)}, u32[]{:S(2)}) %collective-permute-start.4) | collective-permute-done | bytes 262176 | tf_op jit(solution)/shard_map/ppermute | solution.py:276
  43.8 1.3 %collective-permute-start.19 = (bf16[2,64,2048]{2,1,0:T(8,128)(2,1)}, bf16[2,64,2048]{2,1,0:T(8,128)(2,1)S(1)}, u32[]{:S(2)}, u32[]{:S(2)}) collective-permute-start(bf16[2,64,2048]{2,1,0:T(8,128)(2,1)} %collective-permute-done.18.refs_9_), channel_id=1, source_target_pairs={{8,0},{9,1},{10,2},{11,3},{12,4},{13,5},{14,6},{15,7}} | collective-permute-start | bytes 1572872 | tf_op jit(solution)/shard_map/ppermute | solution.py:43
  45.8 15.0 %collective-permute-done.5 = bf16[64,2048]{1,0:T(8,128)(2,1)} collective-permute-done((bf16[64,2048]{1,0:T(8,128)(2,1)}, bf16[64,2048]{1,0:T(8,128)(2,1)}, u32[]{:S(2)}, u32[]{:S(2)}) %collective-permute-start.5) | collective-permute-done | bytes 262176 | tf_op jit(solution)/shard_map/ppermute | solution.py:276
  60.8 1.2 %add_convert_fusion.refs_2_.refs_0_ = bf16[64,2048]{1,0:T(8,128)(2,1)S(1)} fusion(bf16[64,2048]{1,0:T(8,128)(2,1)} %collective-permute-done.6, bf16[64,2048]{1,0:T(8,128)(2,1)} %collective-permute-done.5, f32[64,2048]{1,0:T(8,128)S(1)} %get-tuple-element.21, bf16[64,2048]{1,0:T(8,128)(2,1)} %collective-permute-done.4), kind=kLoop, calls=%fused_computation.3 | loop fusion | flops 917504 | bytes 1572864 | tf_op jit(solution)/shard_map/convert_element_type | solution.py:277
  62.1 2.9 %collective-permute-start.9 = (bf16[64,2048]{1,0:T(8,128)(2,1)S(1)}, bf16[64,2048]{1,0:T(8,128)(2,1)S(1)}, u32[]{:S(2)}, u32[]{:S(2)}) collective-permute-start(bf16[64,2048]{1,0:T(8,128)(2,1)S(1)} %add_convert_fusion.refs_2_.refs_0_), channel_id=1, source_target_pairs={{0,24},{8,0},{16,8},{24,16},{1,25},{9,1},{17,9},{25,17},{2,26},{10... | collective-permute-start | bytes 786440 | tf_op jit(solution)/shard_map/ppermute | solution.py:278
  65.0 11.0 %collective-permute-start.8 = (bf16[64,2048]{1,0:T(8,128)(2,1)S(1)}, bf16[64,2048]{1,0:T(8,128)(2,1)S(1)}, u32[]{:S(2)}, u32[]{:S(2)}) collective-permute-start(bf16[64,2048]{1,0:T(8,128)(2,1)S(1)} %add_convert_fusion.refs_2_.refs_0_), channel_id=1, source_target_pairs={{0,16},{8,24},{16,0},{24,8},{1,17},{9,25},{17,1},{25,9},{2,18},{10... | collective-permute-start | bytes 786440 | tf_op jit(solution)/shard_map/ppermute | solution.py:278
  76.0 1.9 %collective-permute-start.7 = (bf16[64,2048]{1,0:T(8,128)(2,1)S(1)}, bf16[64,2048]{1,0:T(8,128)(2,1)S(1)}, u32[]{:S(2)}, u32[]{:S(2)}) collective-permute-start(bf16[64,2048]{1,0:T(8,128)(2,1)S(1)} %add_convert_fusion.refs_2_.refs_0_), channel_id=1, source_target_pairs={{0,8},{8,16},{16,24},{24,0},{1,9},{9,17},{17,25},{25,1},{2,10},{10... | collective-permute-start | bytes 786440 | tf_op jit(solution)/shard_map/ppermute | solution.py:278
  78.0 3.4 %copy-done.1 = bf16[2048,2048]{1,0:T(8,128)(2,1)S(1)} copy-done((bf16[2048,2048]{1,0:T(8,128)(2,1)S(1)}, bf16[2048,2048]{1,0:T(8,128)(2,1)}, u32[]{:S(2)}) %copy-start.1) | copy-done | bytes 8388632
  81.3 3.4 %copy-done.2 = bf16[2048,2048]{1,0:T(8,128)(2,1)S(1)} copy-done((bf16[2048,2048]{1,0:T(8,128)(2,1)S(1)}, bf16[2048,2048]{1,0:T(8,128)(2,1)}, u32[]{:S(2)}) %copy-start.2) | copy-done | bytes 8388632
  84.7 1.4 %fetch.3 = (bf16[2048,2048]{1,0:T(8,128)(2,1)S(1)}, bf16[2048,2048]{1,0:T(8,128)(2,1)S(1)}) custom-call(bf16[2048,2048]{1,0:T(8,128)(2,1)S(1)} %copy-done.1, bf16[2048,2048]{1,0:T(8,128)(2,1)S(1)} %copy-done.2, bf16[64,2048]{1,0:T(8,128)(2,1)S(1)} %add_convert_fusion.refs_2_.refs_0_), custom_call_target="tpu_custom_call" | custom-call | bytes 16777216 | tf_op jit(solution)/shard_map/fetch/pallas_call | solution.py:62
  86.2 5.9 %down_gradient.1 = (bf16[2048,2048]{1,0:T(8,128)(2,1)}, f32[256,2048]{1,0:T(8,128)S(1)}, f32[256,2048]{1,0:T(8,128)S(1)}, bf16[256,2048]{1,0:T(8,128)(2,1)S(1)}) custom-call(s32[1]{0:T(128)} %bitcast.4.place, bf16[64,2048]{1,0:T(8,128)(2,1)S(1)} %copy-done.3, bf16[64,2048]{1,0:T(8,128)(2,1)S(1)} %copy-done.4, ...), custom_call_target="tpu_custom_call" | custom-call | flops 2147483648 | bytes 14680064 | tf_op jit(solution)/shard_map/down_gradient/pallas_call | solution.py:162
  92.1 5.8 %partial_input.1 = (bf16[256,2048]{1,0:T(8,128)(2,1)S(1)}, bf16[256,2048]{1,0:T(8,128)(2,1)S(1)}, f32[128,2048]{1,0:T(8,128)S(1)}, f32[128,2048]{1,0:T(8,128)S(1)}) custom-call(s32[8]{0:T(128)S(1)} %fusion.11.offsets, bf16[64,2048]{1,0:T(8,128)(2,1)S(1)} %add_convert_fusion.refs_2_.refs_0_, bf16[64,2048]{1,0:T(8,128)(2,1)S(1)} %collective-permute-done.7.refs_1_, ...), custom_call_target="tpu_custom_call" | custom-call | flops 4294967296 | bytes 16777216 | tf_op jit(solution)/shard_map/partial_input/pallas_call | solution.py:208
  98.0 2.6 %collective-permute-done.20 = f32[128,2048]{1,0:T(8,128)S(1)} collective-permute-done((f32[128,2048]{1,0:T(8,128)S(1)}, f32[128,2048]{1,0:T(8,128)S(1)}, u32[]{:S(2)}, u32[]{:S(2)}) %collective-permute-start.20) | collective-permute-done | bytes 1048608 | tf_op jit(solution)/shard_map/ppermute | solution.py:288
  100.8 1.9 %collective-permute-start.21 = (bf16[32,2048]{1,0:T(8,128)(2,1)S(1)}, bf16[32,2048]{1,0:T(8,128)(2,1)S(1)}, u32[]{:S(2)}, u32[]{:S(2)}) collective-permute-start(bf16[32,2048]{1,0:T(8,128)(2,1)S(1)} %get-tuple-element.40), channel_id=1, source_target_pairs={{0,2},{1,3},{2,0},{3,1},{4,6},{5,7},{6,4},{7,5},{8,10},{9,11},{10,... | collective-permute-start | bytes 393224 | tf_op jit(solution)/shard_map/ppermute | solution.py:292
  102.7 1.5 %collective-permute-start.23 = (bf16[32,2048]{1,0:T(8,128)(2,1)S(1)}, bf16[32,2048]{1,0:T(8,128)(2,1)S(1)}, u32[]{:S(2)}, u32[]{:S(2)}) collective-permute-start(bf16[32,2048]{1,0:T(8,128)(2,1)S(1)} %get-tuple-element.41), channel_id=1, source_target_pairs={{0,6},{1,7},{2,4},{3,5},{4,2},{5,3},{6,0},{7,1},{8,14},{9,15},{10,... | collective-permute-start | bytes 393224 | tf_op jit(solution)/shard_map/ppermute | solution.py:292
  104.3 6.4 %weight_gradients.1 = (bf16[2048,2048]{1,0:T(8,128)(2,1)}, bf16[2048,2048]{1,0:T(8,128)(2,1)}) custom-call(bf16[256,2048]{1,0:T(8,128)(2,1)S(1)} %get-tuple-element.32.input_all, bf16[256,2048]{1,0:T(8,128)(2,1)S(1)} %get-tuple-element.33.gate_term, bf16[256,2048]{1,0:T(8,128)(2,1)S(1)} %get-tuple-element.34.up_term), custom_call_target="tpu_custom_call" | custom-call | flops 4294967296 | bytes 16777216 | tf_op jit(solution)/shard_map/weight_gradients/pallas_call | solution.py:238
  110.8 1.2 %collective-permute-done.22 = bf16[32,2048]{1,0:T(8,128)(2,1)S(1)} collective-permute-done((bf16[32,2048]{1,0:T(8,128)(2,1)S(1)}, bf16[32,2048]{1,0:T(8,128)(2,1)S(1)}, u32[]{:S(2)}, u32[]{:S(2)}) %collective-permute-start.22) | collective-permute-done | bytes 131104 | tf_op jit(solution)/shard_map/ppermute | solution.py:292
  (46 shorter events, 4.0 us)
Async XLA Ops:
  0.6 12.3 %collective-permute-start = (bf16[32,2048]{1,0:T(8,128)(2,1)}, bf16[32,2048]{1,0:T(8,128)(2,1)S(1)}, u32[]{:S(2)}, u32[]{:S(2)}) collective-permute-start(bf16[32,2048]{1,0:T(8,128)(2,1)} %param.8), channel_id=1, source_target_pairs={{0,2},{1,3},{2,0},{3,1},{4,6},{5,7},{6,4},{7,5},{8,10},{9,11},{10,... | collective-permute-start | bytes 393224 | tf_op jit(solution)/shard_map/ppermute | solution.py:33
  3.6 9.3 %collective-permute-start.2 = (bf16[32,2048]{1,0:T(8,128)(2,1)}, bf16[32,2048]{1,0:T(8,128)(2,1)S(1)}, u32[]{:S(2)}, u32[]{:S(2)}) collective-permute-start(bf16[32,2048]{1,0:T(8,128)(2,1)} %param.8), channel_id=1, source_target_pairs={{0,6},{1,7},{2,4},{3,5},{4,2},{5,3},{6,0},{7,1},{8,14},{9,15},{10,... | collective-permute-start | bytes 393224 | tf_op jit(solution)/shard_map/ppermute | solution.py:33
  5.1 7.8 %collective-permute-start.1 = (bf16[32,2048]{1,0:T(8,128)(2,1)}, bf16[32,2048]{1,0:T(8,128)(2,1)S(1)}, u32[]{:S(2)}, u32[]{:S(2)}) collective-permute-start(bf16[32,2048]{1,0:T(8,128)(2,1)} %param.8), channel_id=1, source_target_pairs={{0,4},{1,5},{2,6},{3,7},{4,0},{5,1},{6,2},{7,3},{8,12},{9,13},{10,... | collective-permute-start | bytes 393224 | tf_op jit(solution)/shard_map/ppermute | solution.py:33
  6.3 15.2 %collective-permute-start.17 = (bf16[2,64,2048]{2,1,0:T(8,128)(2,1)S(1)}, bf16[2,64,2048]{2,1,0:T(8,128)(2,1)S(1)}, u32[]{:S(2)}, u32[]{:S(2)}) collective-permute-start(bf16[2,64,2048]{2,1,0:T(8,128)(2,1)S(1)} %pad_maximum_fusion.2), channel_id=1, source_target_pairs={{8,0},{16,8},{24,16},{9,1},{17,9},{25,17},{10,2},{18,10},{26,18},{... | collective-permute-start | bytes 1572872 | tf_op jit(solution)/shard_map/ppermute | solution.py:43
  7.6 15.4 %collective-permute-start.14 = (bf16[2,64,2048]{2,1,0:T(8,128)(2,1)S(1)}, bf16[2,64,2048]{2,1,0:T(8,128)(2,1)}, u32[]{:S(2)}, u32[]{:S(2)}) collective-permute-start(bf16[2,64,2048]{2,1,0:T(8,128)(2,1)S(1)} %pad_maximum_fusion.2), channel_id=1, source_target_pairs={{0,8},{8,16},{16,24},{1,9},{9,17},{17,25},{2,10},{10,18},{18,26},{... | collective-permute-start | bytes 1572872 | tf_op jit(solution)/shard_map/ppermute | solution.py:42
  13.9 10.3 %collective-permute-start.3 = (bf16[4,32,2048]{2,1,0:T(8,128)(2,1)S(1)}, bf16[4,32,2048]{2,1,0:T(8,128)(2,1)S(1)}, u32[]{:S(2)}, u32[]{:S(2)}) collective-permute-start(bf16[4,32,2048]{2,1,0:T(8,128)(2,1)S(1)} %pad_maximum_fusion.mine), channel_id=1, source_target_pairs={{0,1},{1,0},{2,3},{3,2},{4,5},{5,4},{6,7},{7,6},{8,9},{9,8},{10,11... | collective-permute-start | bytes 1572872 | tf_op jit(solution)/shard_map/ppermute | solution.py:34
  14.0 15.4 %collective-permute-start.10 = (bf16[32,2048]{1,0:T(8,128)(2,1)}, bf16[32,2048]{1,0:T(8,128)(2,1)S(1)}, u32[]{:S(2)}, u32[]{:S(2)}) collective-permute-start(bf16[32,2048]{1,0:T(8,128)(2,1)} %param.7), channel_id=1, source_target_pairs={{0,2},{1,3},{2,0},{3,1},{4,6},{5,7},{6,4},{7,5},{8,10},{9,11},{10,... | collective-permute-start | bytes 393224 | tf_op jit(solution)/shard_map/ppermute | solution.py:33
  16.0 17.6 %collective-permute-start.12 = (bf16[32,2048]{1,0:T(8,128)(2,1)}, bf16[32,2048]{1,0:T(8,128)(2,1)}, u32[]{:S(2)}, u32[]{:S(2)}) collective-permute-start(bf16[32,2048]{1,0:T(8,128)(2,1)} %param.7), channel_id=1, source_target_pairs={{0,6},{1,7},{2,4},{3,5},{4,2},{5,3},{6,0},{7,1},{8,14},{9,15},{10,... | collective-permute-start | bytes 393224 | tf_op jit(solution)/shard_map/ppermute | solution.py:33
  17.5 3.4 %copy-start = (bf16[2048,2048]{1,0:T(8,128)(2,1)S(1)}, bf16[2048,2048]{1,0:T(8,128)(2,1)}, u32[]{:S(2)}) copy-start(bf16[2048,2048]{1,0:T(8,128)(2,1)} %refs_0_.3) | copy-start | bytes 25165828
  20.9 0.9 copy-start.5
  21.8 15.9 %collective-permute-start.11 = (bf16[32,2048]{1,0:T(8,128)(2,1)S(1)}, bf16[32,2048]{1,0:T(8,128)(2,1)S(1)}, u32[]{:S(2)}, u32[]{:S(2)}) collective-permute-start(bf16[32,2048]{1,0:T(8,128)(2,1)S(1)} %copy-done.5), channel_id=1, source_target_pairs={{0,4},{1,5},{2,6},{3,7},{4,0},{5,1},{6,2},{7,3},{8,12},{9,13},{10,... | collective-permute-start | bytes 393224 | tf_op jit(solution)/shard_map/ppermute | solution.py:33
  23.0 20.9 %collective-permute-start.18 = (bf16[2,64,2048]{2,1,0:T(8,128)(2,1)S(1)}, bf16[2,64,2048]{2,1,0:T(8,128)(2,1)}, u32[]{:S(2)}, u32[]{:S(2)}) collective-permute-start(bf16[2,64,2048]{2,1,0:T(8,128)(2,1)S(1)} %collective-permute-done.17.refs_8_), channel_id=1, source_target_pairs={{8,0},{16,8},{9,1},{17,9},{10,2},{18,10},{11,3},{19,11},{12,4},{20... | collective-permute-start | bytes 1572872 | tf_op jit(solution)/shard_map/ppermute | solution.py:43
  24.3 20.9 %collective-permute-start.15 = (bf16[2,64,2048]{2,1,0:T(8,128)(2,1)}, bf16[2,64,2048]{2,1,0:T(8,128)(2,1)}, u32[]{:S(2)}, u32[]{:S(2)}) collective-permute-start(bf16[2,64,2048]{2,1,0:T(8,128)(2,1)} %collective-permute-done.14.refs_5_), channel_id=1, source_target_pairs={{8,16},{16,24},{9,17},{17,25},{10,18},{18,26},{11,19},{19,27},{12,... | collective-permute-start | bytes 1572872 | tf_op jit(solution)/shard_map/ppermute | solution.py:42
  29.4 14.3 %collective-permute-start.4 = (bf16[64,2048]{1,0:T(8,128)(2,1)S(1)}, bf16[64,2048]{1,0:T(8,128)(2,1)}, u32[]{:S(2)}, u32[]{:S(2)}) collective-permute-start(bf16[64,2048]{1,0:T(8,128)(2,1)S(1)} %get-tuple-element.22), channel_id=1, source_target_pairs={{0,24},{8,0},{16,8},{24,16},{1,25},{9,1},{17,9},{25,17},{2,26},{10... | collective-permute-start | bytes 786440 | tf_op jit(solution)/shard_map/ppermute | solution.py:276
  33.6 27.2 %collective-permute-start.5 = (bf16[64,2048]{1,0:T(8,128)(2,1)}, bf16[64,2048]{1,0:T(8,128)(2,1)}, u32[]{:S(2)}, u32[]{:S(2)}) collective-permute-start(bf16[64,2048]{1,0:T(8,128)(2,1)} %get-tuple-element.23), channel_id=1, source_target_pairs={{0,16},{8,24},{16,0},{24,8},{1,17},{9,25},{17,1},{25,9},{2,18},{10... | collective-permute-start | bytes 786440 | tf_op jit(solution)/shard_map/ppermute | solution.py:276
  37.6 23.2 %collective-permute-start.6 = (bf16[64,2048]{1,0:T(8,128)(2,1)S(1)}, bf16[64,2048]{1,0:T(8,128)(2,1)}, u32[]{:S(2)}, u32[]{:S(2)}) collective-permute-start(bf16[64,2048]{1,0:T(8,128)(2,1)S(1)} %get-tuple-element.24), channel_id=1, source_target_pairs={{0,8},{8,16},{16,24},{24,0},{1,9},{9,17},{17,25},{25,1},{2,10},{10... | collective-permute-start | bytes 786440 | tf_op jit(solution)/shard_map/ppermute | solution.py:276
  43.7 32.3 %collective-permute-start.13 = (bf16[4,32,2048]{2,1,0:T(8,128)(2,1)S(1)}, bf16[4,32,2048]{2,1,0:T(8,128)(2,1)S(1)}, u32[]{:S(2)}, u32[]{:S(2)}) collective-permute-start(bf16[4,32,2048]{2,1,0:T(8,128)(2,1)S(1)} %pad_maximum_fusion.1.refs_3_), channel_id=1, source_target_pairs={{0,1},{1,0},{2,3},{3,2},{4,5},{5,4},{6,7},{7,6},{8,9},{9,8},{10,11... | collective-permute-start | bytes 1572872 | tf_op jit(solution)/shard_map/ppermute | solution.py:34
  43.8 42.3 %collective-permute-start.19 = (bf16[2,64,2048]{2,1,0:T(8,128)(2,1)}, bf16[2,64,2048]{2,1,0:T(8,128)(2,1)S(1)}, u32[]{:S(2)}, u32[]{:S(2)}) collective-permute-start(bf16[2,64,2048]{2,1,0:T(8,128)(2,1)} %collective-permute-done.18.refs_9_), channel_id=1, source_target_pairs={{8,0},{9,1},{10,2},{11,3},{12,4},{13,5},{14,6},{15,7}} | collective-permute-start | bytes 1572872 | tf_op jit(solution)/shard_map/ppermute | solution.py:43
  45.1 41.0 %collective-permute-start.16 = (bf16[2,64,2048]{2,1,0:T(8,128)(2,1)}, bf16[2,64,2048]{2,1,0:T(8,128)(2,1)S(1)}, u32[]{:S(2)}, u32[]{:S(2)}) collective-permute-start(bf16[2,64,2048]{2,1,0:T(8,128)(2,1)} %collective-permute-done.15.refs_6_), channel_id=1, source_target_pairs={{16,24},{17,25},{18,26},{19,27},{20,28},{21,29},{22,30},{23,31}} | collective-permute-start | bytes 1572872 | tf_op jit(solution)/shard_map/ppermute | solution.py:42
  62.1 30.0 %collective-permute-start.9 = (bf16[64,2048]{1,0:T(8,128)(2,1)S(1)}, bf16[64,2048]{1,0:T(8,128)(2,1)S(1)}, u32[]{:S(2)}, u32[]{:S(2)}) collective-permute-start(bf16[64,2048]{1,0:T(8,128)(2,1)S(1)} %add_convert_fusion.refs_2_.refs_0_), channel_id=1, source_target_pairs={{0,24},{8,0},{16,8},{24,16},{1,25},{9,1},{17,9},{25,17},{2,26},{10... | collective-permute-start | bytes 786440 | tf_op jit(solution)/shard_map/ppermute | solution.py:278
  65.0 27.1 %collective-permute-start.8 = (bf16[64,2048]{1,0:T(8,128)(2,1)S(1)}, bf16[64,2048]{1,0:T(8,128)(2,1)S(1)}, u32[]{:S(2)}, u32[]{:S(2)}) collective-permute-start(bf16[64,2048]{1,0:T(8,128)(2,1)S(1)} %add_convert_fusion.refs_2_.refs_0_), channel_id=1, source_target_pairs={{0,16},{8,24},{16,0},{24,8},{1,17},{9,25},{17,1},{25,9},{2,18},{10... | collective-permute-start | bytes 786440 | tf_op jit(solution)/shard_map/ppermute | solution.py:278
  76.0 16.1 %collective-permute-start.7 = (bf16[64,2048]{1,0:T(8,128)(2,1)S(1)}, bf16[64,2048]{1,0:T(8,128)(2,1)S(1)}, u32[]{:S(2)}, u32[]{:S(2)}) collective-permute-start(bf16[64,2048]{1,0:T(8,128)(2,1)S(1)} %add_convert_fusion.refs_2_.refs_0_), channel_id=1, source_target_pairs={{0,8},{8,16},{16,24},{24,0},{1,9},{9,17},{17,25},{25,1},{2,10},{10... | collective-permute-start | bytes 786440 | tf_op jit(solution)/shard_map/ppermute | solution.py:278
  78.0 3.4 %copy-start.1 = (bf16[2048,2048]{1,0:T(8,128)(2,1)S(1)}, bf16[2048,2048]{1,0:T(8,128)(2,1)}, u32[]{:S(2)}) copy-start(bf16[2048,2048]{1,0:T(8,128)(2,1)} %refs_0_.5) | copy-start | bytes 25165828
  81.3 3.4 %copy-start.2 = (bf16[2048,2048]{1,0:T(8,128)(2,1)S(1)}, bf16[2048,2048]{1,0:T(8,128)(2,1)}, u32[]{:S(2)}) copy-start(bf16[2048,2048]{1,0:T(8,128)(2,1)} %refs_1_.3) | copy-start | bytes 25165828
  84.7 1.4 %copy-start.3 = (bf16[64,2048]{1,0:T(8,128)(2,1)S(1)}, bf16[64,2048]{1,0:T(8,128)(2,1)}, u32[]{:S(2)}) copy-start(bf16[64,2048]{1,0:T(8,128)(2,1)} %refs_0_.4) | copy-start | bytes 786436
  84.7 1.4 %copy-start.4 = (bf16[64,2048]{1,0:T(8,128)(2,1)S(1)}, bf16[64,2048]{1,0:T(8,128)(2,1)}, u32[]{:S(2)}) copy-start(bf16[64,2048]{1,0:T(8,128)(2,1)} %refs_1_.2) | copy-start | bytes 786436
  97.9 2.7 %collective-permute-start.20 = (f32[128,2048]{1,0:T(8,128)S(1)}, f32[128,2048]{1,0:T(8,128)S(1)}, u32[]{:S(2)}, u32[]{:S(2)}) collective-permute-start(f32[128,2048]{1,0:T(8,128)S(1)} %get-tuple-element.31), channel_id=1, source_target_pairs={{0,1},{1,0},{2,3},{3,2},{4,5},{5,4},{6,7},{7,6},{8,9},{9,8},{10,11... | collective-permute-start | bytes 3145736 | tf_op jit(solution)/shard_map/ppermute | solution.py:288
  100.8 10.0 %collective-permute-start.21 = (bf16[32,2048]{1,0:T(8,128)(2,1)S(1)}, bf16[32,2048]{1,0:T(8,128)(2,1)S(1)}, u32[]{:S(2)}, u32[]{:S(2)}) collective-permute-start(bf16[32,2048]{1,0:T(8,128)(2,1)S(1)} %get-tuple-element.40), channel_id=1, source_target_pairs={{0,2},{1,3},{2,0},{3,1},{4,6},{5,7},{6,4},{7,5},{8,10},{9,11},{10,... | collective-permute-start | bytes 393224 | tf_op jit(solution)/shard_map/ppermute | solution.py:292
  102.7 8.1 %collective-permute-start.23 = (bf16[32,2048]{1,0:T(8,128)(2,1)S(1)}, bf16[32,2048]{1,0:T(8,128)(2,1)S(1)}, u32[]{:S(2)}, u32[]{:S(2)}) collective-permute-start(bf16[32,2048]{1,0:T(8,128)(2,1)S(1)} %get-tuple-element.41), channel_id=1, source_target_pairs={{0,6},{1,7},{2,4},{3,5},{4,2},{5,3},{6,0},{7,1},{8,14},{9,15},{10,... | collective-permute-start | bytes 393224 | tf_op jit(solution)/shard_map/ppermute | solution.py:292
  104.2 7.8 %collective-permute-start.22 = (bf16[32,2048]{1,0:T(8,128)(2,1)S(1)}, bf16[32,2048]{1,0:T(8,128)(2,1)S(1)}, u32[]{:S(2)}, u32[]{:S(2)}) collective-permute-start(bf16[32,2048]{1,0:T(8,128)(2,1)S(1)} %get-tuple-element.42), channel_id=1, source_target_pairs={{0,4},{1,5},{2,6},{3,7},{4,0},{5,1},{6,2},{7,3},{8,12},{9,13},{10,... | collective-permute-start | bytes 393224 | tf_op jit(solution)/shard_map/ppermute | solution.py:292

commit v3 on v2

v3 whole, which is shorter than its diff:
```python
import functools
import math

import jax
import jax.numpy as jnp
from jax import lax
from jax.experimental import pallas as pl
from jax.experimental.pallas import tpu as pltpu
from jax.sharding import PartitionSpec as P

F32, BF16 = jnp.float32, jnp.bfloat16
MIB = 1024 * 1024
STRIPE = 256


def pinned(*arrays):
    return [pltpu.with_memory_space_constraint(array, pltpu.HBM) for array in arrays]


def stripe(extent):
    return math.gcd(extent, STRIPE)


def params(mib):
    return pltpu.CompilerParams(vmem_limit_bytes=mib * MIB)


def flip(count, mask):
    return [(i, i ^ mask) for i in range(count)]


def swap(block, axis, mask):
    return lax.ppermute(block, axis, flip(lax.axis_size(axis), mask))


def after(later, earlier):
    return lax.optimization_barrier((later, earlier))


def spread_col(own, token, n_col):
    parts = {0: own}
    mask = n_col // 2
    while mask:
        for p in list(parts):
            block = parts[p]
            if p:
                block, token = after(block, token)
            parts[p | mask] = swap(block, "col", mask)
        mask //= 2
    return [parts[p] for p in range(n_col)]


def reduce_halves(parts, sends, n_col):
    parts, arrived, onward = {**parts, **sends}, [], None
    mask = 1
    while mask < n_col:
        blocks = {p: swap(parts.pop(p).astype(BF16), "col", mask) for p in list(parts) if p & mask}
        arrived.append(blocks.pop(mask))
        for p, block in blocks.items():
            onward = parts[p ^ mask] = parts[p ^ mask] + block.astype(F32)
        mask *= 2
    return arrived, onward


def reduce_line(parts, sends, col):
    right = lax.ppermute(sends[2], "col", [(0, 1), (1, 2)]).astype(F32)
    left = lax.ppermute(sends[2], "col", [(3, 2), (2, 1)]).astype(F32)
    over = lax.ppermute(sends[3], "col", [(0, 2), (3, 1)]).astype(F32)
    right = right + jnp.where(col == 1, parts[3], parts[1]) + jnp.where(col == 2, over, 0.0)
    left = left + jnp.where(col == 2, parts[3], parts[1]) + jnp.where(col == 1, over, 0.0)
    right, left = right.astype(BF16), left.astype(BF16)
    arrived = [
        lax.ppermute(right, "col", [(0, 1), (1, 2), (2, 3)]),
        lax.ppermute(left, "col", [(3, 2), (2, 1), (1, 0)]),
    ]
    return arrived, right


def relay_col(low, high, n_col, step):
    up = [(i, i + 1) for i in range(step - 1, n_col - 1)]
    down = [(i, i - 1) for i in range(1, n_col - step + 1)]
    return lax.ppermute(low, "col", up), lax.ppermute(high, "col", down)


def spread_row(own, n_row):
    mine = own[None]
    mask = 2
    while mask < n_row:
        mine = jnp.concatenate([mine, swap(mine, "row", mask)])
        mask *= 2
    return mine


def fetch_kernel(count, *refs):
    sources, (*targets, token, arrived) = refs[:count], refs[-2 - count :]
    token[...] = jnp.zeros_like(token)
    copies = []
    for k in range(count):
        rows = sources[k].shape[0] // arrived.shape[1]
        for i in range(arrived.shape[1]):
            at = pl.ds(i * rows, rows)
            copies.append(pltpu.make_async_copy(sources[k].at[at, :], targets[k].at[at, :], arrived.at[k, i]))
            copies[-1].start()
    for copy in copies:
        copy.wait()


def fetch(weights, behind=()):
    size = sum(w.size * 2 for w in weights)
    return pl.pallas_call(
        functools.partial(fetch_kernel, len(weights)),
        in_specs=[IN_HBM] * len(weights) + [IN_ANY] * len(behind),
        out_specs=[IN_VMEM] * (len(weights) + 1),
        out_shape=[jax.ShapeDtypeStruct(w.shape, w.dtype) for w in weights] + [jax.ShapeDtypeStruct((8, 128), F32)],
        scratch_shapes=[pltpu.SemaphoreType.DMA((len(weights), 4))],
        compiler_params=params(1),
        cost_estimate=pl.CostEstimate(flops=0, bytes_accessed=1024, transcendentals=0),
        name="fetch",
    )(*pinned(*weights), *behind)


def store(buffer, hbm, semaphores, i):
    rows = buffer.shape[0] // semaphores.shape[0]
    at = pl.ds(i * rows, rows)
    copy = pltpu.make_async_copy(buffer.at[at, :], hbm.at[at, :], semaphores.at[i])
    copy.start()
    return copy


IN_VMEM = pl.BlockSpec(memory_space=pltpu.VMEM)
IN_SMEM = pl.BlockSpec(memory_space=pltpu.SMEM)
IN_HBM = pl.BlockSpec(memory_space=pltpu.HBM)
IN_ANY = pl.BlockSpec(memory_space=pl.ANY)
NT = (((1,), (1,)), ((), ()))
TN = (((0,), (0,)), ((), ()))


def stack_kernel(count, *refs):
    for k in range(count):
        refs[-1][k] = refs[k][...]


def stacked(blocks, behind):
    return pl.pallas_call(
        functools.partial(stack_kernel, len(blocks)),
        in_specs=[IN_VMEM] * len(blocks) + [IN_ANY] * len(behind),
        out_specs=IN_VMEM,
        out_shape=jax.ShapeDtypeStruct((len(blocks),) + blocks[0].shape, blocks[0].dtype),
        compiler_params=params(2),
        name="stacked",
    )(*blocks, *behind)


def hidden_kernel(n_row, n_col, kept, early, offsets, mine, theirs, weight, *refs):
    grad_all, token, *parts = refs[-2 - len(kept) - len(early) :]
    token[...] = jnp.zeros_like(token)
    rows, part = mine.shape[1], parts[0].shape[0]
    kinds = [(p, F32) for p in kept] + [(p, BF16) for p in early]
    for x in range(n_row):
        grad_all[pl.ds(pl.multiple_of(offsets[x], rows), rows), :] = (theirs if x % 2 else mine)[x // 2]
    step = stripe(weight.shape[0])
    for i in range(weight.shape[0] // step):
        at = slice(i * step, (i + 1) * step)
        total = lax.dot_general(grad_all[...], weight[at, :], NT, preferred_element_type=F32)
        for ref, (p, kind) in zip(parts, kinds):
            ref[:, at] = total[p * part : (p + 1) * part].astype(kind)


def partial_hidden(mine, theirs, weight, behind, offsets, n_col, kept, early):
    n_row, rows, width = 2 * mine.shape[0], mine.shape[1], mine.shape[2]
    units = weight.shape[0]
    tokens = rows * n_row
    part = tokens // n_col
    grad_all, token, *parts = pl.pallas_call(
        functools.partial(hidden_kernel, n_row, n_col, kept, early),
        in_specs=[IN_SMEM] + [IN_VMEM] * 3 + [IN_HBM] * len(behind),
        out_specs=[IN_VMEM] * (2 + len(kept) + len(early)),
        out_shape=[jax.ShapeDtypeStruct((tokens, width), BF16), jax.ShapeDtypeStruct((8, 128), F32)]
        + [jax.ShapeDtypeStruct((part, units), F32)] * len(kept)
        + [jax.ShapeDtypeStruct((part, units), BF16)] * len(early),
        compiler_params=params(2),
        cost_estimate=pl.CostEstimate(
            flops=2 * tokens * width * units, bytes_accessed=2 * units * width, transcendentals=0
        ),
        name="partial_hidden",
    )(offsets, mine, theirs, weight, *pinned(*behind))
    return grad_all, token, dict(zip(kept, parts)), dict(zip(early, parts[len(kept) :]))


def sum_kernel(count, *refs):
    total = refs[0][...]
    for ref in refs[1:count]:
        total = total + ref[...].astype(F32)
    refs[-1][...] = total.astype(BF16)


def summed(own, arrived, behind):
    return pl.pallas_call(
        functools.partial(sum_kernel, 1 + len(arrived)),
        in_specs=[IN_VMEM] * (1 + len(arrived)) + [IN_ANY] * len(behind),
        out_specs=IN_VMEM,
        out_shape=jax.ShapeDtypeStruct(own.shape, BF16),
        compiler_params=params(2),
        cost_estimate=pl.CostEstimate(flops=own.size, bytes_accessed=8 * own.size, transcendentals=0),
        name="summed",
    )(own, *arrived, *behind)


def pick(from_low, from_high, p, col, which, at):
    n_col = len(from_low)
    value, known = from_low[0][which, :, at], set()
    for c in range(n_col):
        below, distance = (c ^ p) < c, abs((c ^ p) - c)
        if p and (below, distance) not in known:
            known.add((below, distance))
            block = (from_low if below else from_high)[distance][which, :, at]
            match = jnp.logical_and(((col ^ p) < col) == below, jnp.abs((col ^ p) - col) == distance)
            value = block if len(known) == 1 else jnp.where(match, block, value)
    return value.astype(F32)


def down_kernel(n_col, scale, place, *refs):
    moved, grad_all = refs[: 2 * n_col - 1], refs[2 * n_col - 1]
    down_grad, up_factor, gate_factor, saved, arrived, buffer, left = refs[-7:]
    loads = [pltpu.make_async_copy(block, saved.at[k], arrived.at[k]) for k, block in enumerate(moved)]
    for copy in loads:
        copy.start()
    for copy in loads:
        copy.wait()
    blocks = [saved.at[k] for k in range(len(moved))]
    from_low, from_high = blocks[:n_col], blocks[:1] + blocks[n_col:]
    _, part, units = from_low[0].shape
    col = place[0]
    step = units // left.shape[0]
    copies = []
    for i in range(left.shape[0]):
        at = slice(i * step, (i + 1) * step)
        hidden = []
        for p in range(n_col):
            g, u = (pick(from_low, from_high, p, col, which, at) for which in range(2))
            s = 1.0 / (1.0 + jnp.exp(-g))
            silu = g * s
            hidden.append((silu * u).astype(BF16))
            up_factor[p * part : (p + 1) * part, at] = silu
            gate_factor[p * part : (p + 1) * part, at] = u * s * (1.0 + g * (1.0 - s))
        product = lax.dot_general(
            jnp.concatenate(hidden, axis=0), grad_all[...], TN, preferred_element_type=F32
        )
        buffer[at, :] = (product * scale).astype(BF16)
        copies.append(store(buffer, down_grad, left, i))
    for copy in copies:
        copy.wait()


def down_gradient(from_low, from_high, grad_all, behind, place, scale):
    n_col = len(from_low)
    units = from_low[0].shape[2]
    tokens, width = grad_all.shape
    return pl.pallas_call(
        functools.partial(down_kernel, n_col, scale),
        in_specs=[IN_SMEM] + [IN_HBM] * (2 * n_col - 1) + [IN_VMEM] + [IN_ANY] * len(behind),
        out_specs=[IN_HBM] + [IN_VMEM] * 2,
        out_shape=[jax.ShapeDtypeStruct((units, width), BF16)] + [jax.ShapeDtypeStruct((tokens, units), F32)] * 2,
        scratch_shapes=[
            pltpu.VMEM((2 * n_col - 1,) + from_low[0].shape, BF16),
            pltpu.SemaphoreType.DMA((2 * n_col - 1,)),
            pltpu.VMEM((units, width), BF16),
            pltpu.SemaphoreType.DMA((units // stripe(units),)),
        ],
        compiler_params=params(14),
        cost_estimate=pl.CostEstimate(
            flops=1 * 2 * tokens * width * units,
            bytes_accessed=2 * units * width + 12 * tokens * units,
            transcendentals=tokens * units,
        ),
        name="down_gradient",
    )(place, *pinned(*from_low, *from_high[1:]), grad_all, *behind)


def input_kernel(n_row, n_col, offsets, *refs):
    hidden_grad, refs = refs[:n_col], refs[n_col:]
    up_factor, gate_factor, gate_weight, up_weight, _, gate_term, up_term, own, other, token = refs
    token[...] = jnp.zeros_like(token)
    part = hidden_grad[0].shape[0]
    rows = part * n_col // n_row
    half = own.shape[0]
    for j in range(n_col):
        h = hidden_grad[j][...].astype(F32)
        at = slice(j * part, (j + 1) * part)
        terms = ((gate_term, (h * gate_factor[at, :]).astype(BF16)), (up_term, (h * up_factor[at, :]).astype(BF16)))
        for c in range(part // rows):
            to = pl.ds(pl.multiple_of(offsets[j * (part // rows) + c], rows), rows)
            for ref, term in terms:
                ref[to, :] = term[c * rows : (c + 1) * rows]
    step = stripe(own.shape[1])
    for i in range(own.shape[1] // step):
        at = slice(i * step, (i + 1) * step)
        total = lax.dot_general(gate_term[...], gate_weight[at, :], NT, preferred_element_type=F32)
        total += lax.dot_general(up_term[...], up_weight[at, :], NT, preferred_element_type=F32)
        own[:, at] = total[:half]
        other[:, at] = total[half:]


def partial_input(hidden_grad, up_factor, gate_factor, gate_weight, up_weight, behind, offsets, n_row):
    n_col = len(hidden_grad)
    part, units = hidden_grad[0].shape
    tokens = part * n_col
    width = gate_weight.shape[0]
    return pl.pallas_call(
        functools.partial(input_kernel, n_row, n_col),
        in_specs=[IN_SMEM] + [IN_VMEM] * (n_col + 4) + [IN_ANY],
        out_specs=[IN_VMEM] * 5,
        out_shape=[jax.ShapeDtypeStruct((tokens, units), BF16)] * 2
        + [jax.ShapeDtypeStruct((tokens // 2, width), F32)] * 2
        + [jax.ShapeDtypeStruct((8, 128), F32)],
        compiler_params=params(2),
        cost_estimate=pl.CostEstimate(
            flops=4 * tokens * width * units, bytes_accessed=4 * units * width, transcendentals=0
        ),
        name="partial_input",
    )(offsets, *hidden_grad, up_factor, gate_factor, gate_weight, up_weight, behind)


def weight_kernel(scale, mine, theirs, gate_term, up_term, _, gate_grad, up_grad, buffers, left):
    blocks = mine.shape[0]
    step = buffers.shape[1] // left.shape[1]
    copies = []
    for i in range(left.shape[1]):
        at = slice(i * step, (i + 1) * step)
        left_side = jnp.concatenate([ref[k, :, at] for ref in (mine, theirs) for k in range(blocks)], axis=0)
        for k, (term, out) in enumerate(((gate_term, gate_grad), (up_term, up_grad))):
            product = lax.dot_general(left_side, term[...], TN, preferred_element_type=F32)
            buffers[k, at, :] = (product * scale).astype(BF16)
            copies.append(store(buffers.at[k], out, left.at[k], i))
    for copy in copies:
        copy.wait()


def weight_gradients(mine, theirs, gate_term, up_term, behind, scale):
    width = mine.shape[2]
    tokens, units = gate_term.shape
    return pl.pallas_call(
        functools.partial(weight_kernel, scale),
        in_specs=[IN_VMEM] * 4 + [IN_ANY],
        out_specs=[IN_HBM] * 2,
        out_shape=[jax.ShapeDtypeStruct((width, units), BF16)] * 2,
        scratch_shapes=[
            pltpu.VMEM((2, width, units), BF16),
            pltpu.SemaphoreType.DMA((2, width // stripe(width))),
        ],
        compiler_params=params(18),
        cost_estimate=pl.CostEstimate(
            flops=4 * tokens * width * units, bytes_accessed=4 * units * width, transcendentals=0
        ),
        name="weight_gradients",
    )(mine, theirs, gate_term, up_term, behind)


def per_device(inputs, grad_out, gate_pre, up_pre, gate_weight, up_weight, down_weight):
    n_row, n_col = lax.axis_size("row"), lax.axis_size("col")
    row, col = lax.axis_index("row"), lax.axis_index("col")
    rows = grad_out.shape[0]
    tokens = rows * n_row
    share = n_row // n_col
    scale = 1.0 / math.sqrt(tokens)

    block = row ^ jnp.arange(n_row, dtype=jnp.int32)
    to_parts = (((block // share) ^ col) * share + block % share) * rows
    part = col ^ jnp.arange(n_col, dtype=jnp.int32)
    seen = (part[:, None] * share + jnp.arange(share, dtype=jnp.int32)).reshape(-1) ^ row
    to_blocks = ((seen % 2) * (n_row // 2) + seen // 2) * rows

    near = [swap(grad_out, "row", mask) for mask in range(2, n_row, 2)]
    saved = jnp.stack([gate_pre, up_pre])
    low, high = relay_col(saved, saved, n_col, 1)
    from_low, from_high = [saved, low], [saved, high]
    grad_mine = stacked([grad_out] + near, [])
    fetched, _ = fetch([down_weight], [grad_mine])
    grad_theirs = swap(grad_mine, "row", 1)
    kept, early = ((0, 1, 3), (2, 3)) if n_col == 4 else (tuple(range(0, n_col, 2)), tuple(range(1, n_col, 2)))
    grad_all, token, parts, sends = partial_hidden(
        grad_mine, grad_theirs, fetched, [from_low[1], from_high[1]], to_parts.astype(jnp.int32), n_col, kept, early
    )

    (low, high), token = after((low, high), token)
    for step in range(2, n_col):
        low, high = relay_col(low, high, n_col, step)
        from_low.append(low)
        from_high.append(high)
    if n_col == 4:
        arrived, onward = reduce_line(parts, sends, col)
    else:
        arrived, onward = reduce_halves(parts, sends, n_col)
    (inputs, onward), token = after((inputs, onward[:8, :128]), token)
    input_mine = spread_row(inputs, n_row)
    own = summed(parts[0], arrived, [token, onward])
    gate_fetched, up_fetched, token = fetch([gate_weight, up_weight], [own])
    hidden_grad = spread_col(own, token, n_col)

    down_grad, up_factor, gate_factor = down_gradient(
        from_low, from_high, grad_all, [hidden_grad[n_col // 2]], col[None].astype(jnp.int32), scale
    )
    gate_term, up_term, mine, other, token = partial_input(
        hidden_grad, up_factor, gate_factor, gate_fetched, up_fetched, input_mine, to_blocks.astype(jnp.int32), n_row
    )

    mine = mine + swap(other, "row", 1)
    input_grad = mine[:rows]
    for k in range(1, n_row // 2):
        away = mine[k * rows : (k + 1) * rows].astype(BF16)
        input_grad = input_grad + swap(away, "row", 2 * k).astype(F32)
    input_mine, token = after(input_mine, token)
    input_theirs = swap(input_mine, "row", 1)
    gate_grad, up_grad = weight_gradients(input_mine, input_theirs, gate_term, up_term, token, scale)
    return (input_grad.astype(BF16), gate_grad, up_grad, down_grad)


def solution(mesh):
    return jax.shard_map(
        per_device,
        mesh=mesh,
        in_specs=(
            P("row", "col"),
            P("row", "col"),
            P("col", "row"),
            P("col", "row"),
            P("col", "row"),
            P("col", "row"),
            P("row", "col"),
        ),
        out_specs=(P("row", "col"), P("col", "row"), P("col", "row"), P("row", "col")),
        check_vma=False,
    )
```

time: 113 us -> 106 us (0.938)
  Pallas kernels: 23.7 us -> 32.4 us
  starting transfers between devices: 48.4 us -> 41.4 us
  local copies, waits for them, and re-layouts: 10.5 us -> 3.59 us
  other arithmetic: 5.23 us -> 2.37 us
    pallas_call x2, Pallas kernels: 1.98 us -> 10.7 us  [fetch(): pl.pallas_call(functools.partial(fetch_kernel, len(weights)), in_specs=[I...]
    ppermute x24 -> x25, starting transfers between devices: 48.4 us -> 41.4 us  [the longest x14 16.5 us: swap(): return lax.ppermute(block, axis, flip(lax.axis_size(axis), mask))]
    unnamed x12 -> x18, local copies, waits for them, and re-layouts: 10.4 us -> 3.47 us
    another operation x4 -> x2, other arithmetic: 3.17 us -> 1.25 us  [the longest x1 1.08 us: per_device(): saved = jnp.stack([gate_pre, up_pre])]
    ppermute x24 -> x25, waiting for transfers between devices: 23.9 us -> 25 us  [the longest x6 9.27 us: relay_col(): return (lax.ppermute(low, 'col', up), lax.ppermute(high, 'col', down))]
    pallas_call x1 -> x3, Pallas kernels: 3.62 us -> 3.06 us  [the longest x1 2.93 us: partial_hidden(): pl.pallas_call(functools.partial(hidden_kernel, n_row, n_col, kept, early...]
  transfers between devices with their start and end apart: 24 -> 25, of which waited for: 4 -> 10; matrix products, arithmetic and copies ran while one was open for 4% -> 2% of each run, Pallas kernels for 16% -> 22%
where the time goes in v3:
time: 106 us
  starting transfers between devices  41.4 us (39%)
  Pallas kernels  32.4 us (31%)
  waiting for transfers between devices  25 us (24%)
  local copies, waits for them, and re-layouts  3.59 us (3%)
  other arithmetic  2.37 us (2%)
    ppermute x14, starting transfers between devices, swap(): return lax.ppermute(block, axis, flip(lax.axis_size(axis), mask))  16.5 us
    ppermute x6, starting transfers between devices, relay_col(): return (lax.ppermute(low, 'col', up), lax.ppermute(high, 'col', down))  10.8 us
    pallas_call x2, Pallas kernels, fetch(): pl.pallas_call(functools.partial(fetch_kernel, len(weights)), in_specs=[I...  10.7 us
    ppermute x6, waiting for transfers between devices, relay_col(): return (lax.ppermute(low, 'col', up), lax.ppermute(high, 'col', down))  9.27 us
    ppermute x14, waiting for transfers between devices, swap(): return lax.ppermute(block, axis, flip(lax.axis_size(axis), mask))  7.83 us
    pallas_call x1, Pallas kernels, down_gradient(): pl.pallas_call(functools.partial(down_kernel, n_col, scale), in_specs=[IN...  6.53 us
    pallas_call x1, Pallas kernels, weight_gradients(): pl.pallas_call(functools.partial(weight_kernel, scale), in_specs=[IN_VMEM...  6.43 us
    pallas_call x1, Pallas kernels, partial_input(): pl.pallas_call(functools.partial(input_kernel, n_row, n_col), in_specs=[I...  5.75 us
  transfers between devices with their start and end apart: 25, of which 10 were waited for; matrix products, arithmetic and copies ran while one was open for 2% of the time, Pallas kernels for 22%

profile of v3, /device:TPU:0, one launch (start us, length us, event | category | flops | bytes accessed | tf_op | source)
XLA Modules:
  0.0 105.8 jit_solution(16342942012781854428)
XLA Ops:
  0.6 3.0 %collective-permute-start.1 = (bf16[32,2048]{1,0:T(8,128)(2,1)}, bf16[32,2048]{1,0:T(8,128)(2,1)S(1)}, u32[]{:S(2)}, u32[]{:S(2)}) collective-permute-start(bf16[32,2048]{1,0:T(8,128)(2,1)} %refs_0_.3), channel_id=1, source_target_pairs={{0,4},{1,5},{2,6},{3,7},{4,0},{5,1},{6,2},{7,3},{8,12},{9,13},{10,... | collective-permute-start | bytes 393224 | tf_op jit(solution)/shard_map/ppermute | solution.py:33
  3.7 1.5 %collective-permute-start = (bf16[32,2048]{1,0:T(8,128)(2,1)}, bf16[32,2048]{1,0:T(8,128)(2,1)S(1)}, u32[]{:S(2)}, u32[]{:S(2)}) collective-permute-start(bf16[32,2048]{1,0:T(8,128)(2,1)} %refs_0_.3), channel_id=1, source_target_pairs={{0,2},{1,3},{2,0},{3,1},{4,6},{5,7},{6,4},{7,5},{8,10},{9,11},{10,... | collective-permute-start | bytes 393224 | tf_op jit(solution)/shard_map/ppermute | solution.py:33
  5.2 1.1 %pad_maximum_fusion.refs_0_ = bf16[2,64,2048]{2,1,0:T(8,128)(2,1)S(1)} fusion(bf16[1,64,2048]{2,1,0:T(8,128)(2,1)} %bitcast.7, bf16[1,64,2048]{2,1,0:T(8,128)(2,1)} %bitcast.8), kind=kLoop, calls=%fused_computation.6 | loop fusion | flops 262144 | bytes 1048576 | tf_op jit(solution)/shard_map/stack | solution.py:374
  6.3 1.3 %collective-permute-start.5 = (bf16[2,64,2048]{2,1,0:T(8,128)(2,1)S(1)}, bf16[2,64,2048]{2,1,0:T(8,128)(2,1)S(1)}, u32[]{:S(2)}, u32[]{:S(2)}) collective-permute-start(bf16[2,64,2048]{2,1,0:T(8,128)(2,1)S(1)} %pad_maximum_fusion.refs_0_), channel_id=1, source_target_pairs={{8,0},{16,8},{24,16},{9,1},{17,9},{25,17},{10,2},{18,10},{26,18},{... | collective-permute-start | bytes 1572872 | tf_op jit(solution)/shard_map/ppermute | solution.py:82
  7.6 4.6 %collective-permute-start.4 = (bf16[2,64,2048]{2,1,0:T(8,128)(2,1)S(1)}, bf16[2,64,2048]{2,1,0:T(8,128)(2,1)S(1)}, u32[]{:S(2)}, u32[]{:S(2)}) collective-permute-start(bf16[2,64,2048]{2,1,0:T(8,128)(2,1)S(1)} %pad_maximum_fusion.refs_0_), channel_id=1, source_target_pairs={{0,8},{8,16},{16,24},{1,9},{9,17},{17,25},{2,10},{10,18},{18,26},{... | collective-permute-start | bytes 1572872 | tf_op jit(solution)/shard_map/ppermute | solution.py:82
  13.3 4.1 %fetch.2 = (bf16[2048,2048]{1,0:T(8,128)(2,1)S(1)}, f32[8,128]{1,0:T(8,128)}) custom-call(bf16[2048,2048]{1,0:T(8,128)(2,1)} %refs_0_.4, bf16[4,32,2048]{2,1,0:T(8,128)(2,1)S(1)} %stacked.1.refs_1_.mine), custom_call_target="tpu_custom_call" | custom-call | bytes 1024 | tf_op jit(solution)/shard_map/fetch/pallas_call | solution.py:110
  17.4 3.9 %collective-permute-done.5.refs_1_.refs_4_ = bf16[2,64,2048]{2,1,0:T(8,128)(2,1)S(1)} collective-permute-done((bf16[2,64,2048]{2,1,0:T(8,128)(2,1)S(1)}, bf16[2,64,2048]{2,1,0:T(8,128)(2,1)S(1)}, u32[]{:S(2)}, u32[]{:S(2)}) %collective-permute-start.5) | collective-permute-done | bytes 524320 | tf_op jit(solution)/shard_map/ppermute | solution.py:82
  21.3 1.2 %collective-permute-done.4.refs_0_.refs_1_ = bf16[2,64,2048]{2,1,0:T(8,128)(2,1)S(1)} collective-permute-done((bf16[2,64,2048]{2,1,0:T(8,128)(2,1)S(1)}, bf16[2,64,2048]{2,1,0:T(8,128)(2,1)S(1)}, u32[]{:S(2)}, u32[]{:S(2)}) %collective-permute-start.4) | collective-permute-done | bytes 524320 | tf_op jit(solution)/shard_map/ppermute | solution.py:82
  23.3 2.9 %partial_hidden.1 = (bf16[256,2048]{1,0:T(8,128)(2,1)S(1)}, f32[8,128]{1,0:T(8,128)S(1)}, f32[64,2048]{1,0:T(8,128)S(1)}, f32[64,2048]{1,0:T(8,128)S(1)}, f32[64...) custom-call(s32[8]{0:T(128)S(1)} %fusion.10.offsets, ...), custom_call_target="tpu_custom_call" | custom-call | flops 2147483648 | bytes 8388608 | tf_op jit(solution)/shard_map/partial_hidden/pallas_call | solution.py:174
  26.2 1.0 copy-done.1
  27.2 5.6 %collective-permute-start.7 = (bf16[64,2048]{1,0:T(8,128)(2,1)S(1)}, bf16[64,2048]{1,0:T(8,128)(2,1)S(1)}, u32[]{:S(2)}, u32[]{:S(2)}) collective-permute-start(bf16[64,2048]{1,0:T(8,128)(2,1)S(1)} %get-tuple-element.37), channel_id=1, source_target_pairs={{0,16},{24,8},{1,17},{25,9},{2,18},{26,10},{3,19},{27,11},{4,20},{... | collective-permute-start | bytes 786440 | tf_op jit(solution)/shard_map/ppermute | solution.py:68
  33.4 1.3 %collective-permute-start.6 = (bf16[64,2048]{1,0:T(8,128)(2,1)S(1)}, bf16[64,2048]{1,0:T(8,128)(2,1)S(1)}, u32[]{:S(2)}, u32[]{:S(2)}) collective-permute-start(bf16[64,2048]{1,0:T(8,128)(2,1)S(1)} %get-tuple-element.34), channel_id=1, source_target_pairs={{0,8},{8,16},{1,9},{9,17},{2,10},{10,18},{3,11},{11,19},{4,12},{12... | collective-permute-start | bytes 786440 | tf_op jit(solution)/shard_map/ppermute | solution.py:66
  34.8 1.5 %collective-permute-start.14 = (bf16[2,64,2048]{2,1,0:T(8,128)(2,1)}, bf16[2,64,2048]{2,1,0:T(8,128)(2,1)}, u32[]{:S(2)}, u32[]{:S(2)}) collective-permute-start(bf16[2,64,2048]{2,1,0:T(8,128)(2,1)} %copy-done.6), channel_id=1, source_target_pairs={{8,16},{16,24},{9,17},{17,25},{10,18},{18,26},{11,19},{19,27},{12,... | collective-permute-start | bytes 1572872 | tf_op jit(solution)/shard_map/ppermute | solution.py:82
  36.2 1.3 %collective-permute-start.16 = (bf16[2,64,2048]{2,1,0:T(8,128)(2,1)}, bf16[2,64,2048]{2,1,0:T(8,128)(2,1)}, u32[]{:S(2)}, u32[]{:S(2)}) collective-permute-start(bf16[2,64,2048]{2,1,0:T(8,128)(2,1)} %copy-done.5), channel_id=1, source_target_pairs={{8,0},{16,8},{9,1},{17,9},{10,2},{18,10},{11,3},{19,11},{12,4},{20... | collective-permute-start | bytes 1572872 | tf_op jit(solution)/shard_map/ppermute | solution.py:82
  37.5 1.5 %collective-permute-done.7 = bf16[64,2048]{1,0:T(8,128)(2,1)S(1)} collective-permute-done((bf16[64,2048]{1,0:T(8,128)(2,1)S(1)}, bf16[64,2048]{1,0:T(8,128)(2,1)S(1)}, u32[]{:S(2)}, u32[]{:S(2)}) %collective-permute-start.7) | collective-permute-done | bytes 262176 | tf_op jit(solution)/shard_map/ppermute | solution.py:68
  39.0 2.8 %collective-permute-done.6 = bf16[64,2048]{1,0:T(8,128)(2,1)S(1)} collective-permute-done((bf16[64,2048]{1,0:T(8,128)(2,1)S(1)}, bf16[64,2048]{1,0:T(8,128)(2,1)S(1)}, u32[]{:S(2)}, u32[]{:S(2)}) %collective-permute-start.6) | collective-permute-done | bytes 262176 | tf_op jit(solution)/shard_map/ppermute | solution.py:66
  42.1 1.6 %collective-permute-start.18 = (bf16[1,32,2048]{2,1,0:T(8,128)(2,1)S(1)}, bf16[1,32,2048]{2,1,0:T(8,128)(2,1)S(1)}, u32[]{:S(2)}, u32[]{:S(2)}) collective-permute-start(bf16[1,32,2048]{2,1,0:T(8,128)(2,1)S(1)} %bitcast.4), channel_id=1, source_target_pairs={{0,2},{1,3},{2,0},{3,1},{4,6},{5,7},{6,4},{7,5},{8,10},{9,11},{10,... | collective-permute-start | bytes 393224 | tf_op jit(solution)/shard_map/ppermute | solution.py:33
  43.6 5.2 %collective-permute-start.8 = (bf16[64,2048]{1,0:T(8,128)(2,1)S(1)}, bf16[64,2048]{1,0:T(8,128)(2,1)S(1)}, u32[]{:S(2)}, u32[]{:S(2)}) collective-permute-start(bf16[64,2048]{1,0:T(8,128)(2,1)S(1)} %get-tuple-element.63), channel_id=1, source_target_pairs={{0,8},{8,16},{16,24},{1,9},{9,17},{17,25},{2,10},{10,18},{18,26},{... | collective-permute-start | bytes 786440 | tf_op jit(solution)/shard_map/ppermute | solution.py:73
  48.9 1.3 %collective-permute-start.10 = (bf16[64,2048]{1,0:T(8,128)(2,1)S(1)}, bf16[64,2048]{1,0:T(8,128)(2,1)S(1)}, u32[]{:S(2)}, u32[]{:S(2)}) collective-permute-start(bf16[64,2048]{1,0:T(8,128)(2,1)S(1)} %get-tuple-element.62), channel_id=1, source_target_pairs={{24,16},{16,8},{8,0},{25,17},{17,9},{9,1},{26,18},{18,10},{10,2},{... | collective-permute-start | bytes 786440 | tf_op jit(solution)/shard_map/ppermute | solution.py:74
  50.2 1.6 %collective-permute-start.19 = (bf16[2,32,2048]{2,1,0:T(8,128)(2,1)S(1)}, bf16[2,32,2048]{2,1,0:T(8,128)(2,1)S(1)}, u32[]{:S(2)}, u32[]{:S(2)}) collective-permute-start(bf16[2,32,2048]{2,1,0:T(8,128)(2,1)S(1)} %pad_maximum_fusion.2), channel_id=1, source_target_pairs={{0,4},{1,5},{2,6},{3,7},{4,0},{5,1},{6,2},{7,3},{8,12},{9,13},{10,... | collective-permute-start | bytes 786440 | tf_op jit(solution)/shard_map/ppermute | solution.py:33
  52.5 1.5 %collective-permute-start.17 = (bf16[2,64,2048]{2,1,0:T(8,128)(2,1)}, bf16[2,64,2048]{2,1,0:T(8,128)(2,1)S(1)}, u32[]{:S(2)}, u32[]{:S(2)}) collective-permute-start(bf16[2,64,2048]{2,1,0:T(8,128)(2,1)} %collective-permute-done.16.refs_5_), channel_id=1, source_target_pairs={{8,0},{9,1},{10,2},{11,3},{12,4},{13,5},{14,6},{15,7}} | collective-permute-start | bytes 1572872 | tf_op jit(solution)/shard_map/ppermute | solution.py:82
  54.0 3.6 %collective-permute-done.10.refs_2_ = bf16[64,2048]{1,0:T(8,128)(2,1)S(1)} collective-permute-done((bf16[64,2048]{1,0:T(8,128)(2,1)S(1)}, bf16[64,2048]{1,0:T(8,128)(2,1)S(1)}, u32[]{:S(2)}, u32[]{:S(2)}) %collective-permute-start.10) | collective-permute-done | bytes 262176 | tf_op jit(solution)/shard_map/ppermute | solution.py:74
  57.7 4.6 %collective-permute-start.12 = (bf16[64,2048]{1,0:T(8,128)(2,1)S(1)}, bf16[64,2048]{1,0:T(8,128)(2,1)S(1)}, u32[]{:S(2)}, u32[]{:S(2)}) collective-permute-start(bf16[64,2048]{1,0:T(8,128)(2,1)S(1)} %summed.1.refs_2_.refs_0_), channel_id=1, source_target_pairs={{0,16},{8,24},{16,0},{24,8},{1,17},{9,25},{17,1},{25,9},{2,18},{10... | collective-permute-start | bytes 786440 | tf_op jit(solution)/shard_map/ppermute | solution.py:33
  62.5 6.6 %fetch.3 = (bf16[2048,2048]{1,0:T(8,128)(2,1)S(1)}, bf16[2048,2048]{1,0:T(8,128)(2,1)S(1)}, f32[8,128]{1,0:T(8,128)}) custom-call(bf16[2048,2048]{1,0:T(8,128)(2,1)} %refs_0_.5, bf16[2048,2048]{1,0:T(8,128)(2,1)} %refs_1_.1, bf16[64,2048]{1,0:T(8,128)(2,1)S(1)} %summed.1.refs_2_.refs_0_), custom_call_target="tpu_custom_call" | custom-call | bytes 1024 | tf_op jit(solution)/shard_map/fetch/pallas_call | solution.py:110
  69.1 3.7 %collective-permute-done.12.refs_8_.refs_2_ = bf16[64,2048]{1,0:T(8,128)(2,1)S(1)} collective-permute-done((bf16[64,2048]{1,0:T(8,128)(2,1)S(1)}, bf16[64,2048]{1,0:T(8,128)(2,1)S(1)}, u32[]{:S(2)}, u32[]{:S(2)}) %collective-permute-start.12) | collective-permute-done | bytes 262176 | tf_op jit(solution)/shard_map/ppermute | solution.py:33
  72.9 4.2 %collective-permute-done.17.refs_6_ = bf16[2,64,2048]{2,1,0:T(8,128)(2,1)S(1)} collective-permute-done((bf16[2,64,2048]{2,1,0:T(8,128)(2,1)}, bf16[2,64,2048]{2,1,0:T(8,128)(2,1)S(1)}, u32[]{:S(2)}, u32[]{:S(2)}) %collective-permute-start.17) | collective-permute-done | bytes 524320 | tf_op jit(solution)/shard_map/ppermute | solution.py:82
  77.9 6.5 %down_gradient.1 = (bf16[2048,2048]{1,0:T(8,128)(2,1)}, f32[256,2048]{1,0:T(8,128)S(1)}, f32[256,2048]{1,0:T(8,128)S(1)}) custom-call(s32[1]{0:T(128)} %bitcast.2.place, bf16[2,64,2048]{2,1,0:T(8,128)(2,1)} %copy-done.3, bf16[2,64,2048]{2,1,0:T(8,128)(2,1)} %copy-done.6, bf16[2,64,2048]{2,1,0:T(8,128)(2,1)} %collective-permute-done.14.refs_2_, ...), custom_call_target="tpu_custom_call" | custom-call | flops 2147483648 | bytes 14680064 | tf_op jit(solution)/shard_map/down_gradient/pallas_call | solution.py:259
  84.4 1.5 %collective-permute-done.13.refs_3_ = bf16[64,2048]{1,0:T(8,128)(2,1)S(1)} collective-permute-done((bf16[64,2048]{1,0:T(8,128)(2,1)S(1)}, bf16[64,2048]{1,0:T(8,128)(2,1)S(1)}, u32[]{:S(2)}, u32[]{:S(2)}) %collective-permute-start.13) | collective-permute-done | bytes 262176 | tf_op jit(solution)/shard_map/ppermute | solution.py:33
  85.9 5.8 %partial_input.1 = (bf16[256,2048]{1,0:T(8,128)(2,1)S(1)}, bf16[256,2048]{1,0:T(8,128)(2,1)S(1)}, f32[128,2048]{1,0:T(8,128)S(1)}, f32[128,2048]{1,0:T(8,128)S(1)}, f32[8,128]{1,0:T(8,128)S(1)}) custom-call(s32[8]{0:T(128)S(1)} %fusion.11.offsets, bf16[64,2048]{1,0:T(8,128)(2,1)S(1)} %summed.1.refs_2_.refs_0_, ...), custom_call_target="tpu_custom_call" | custom-call | flops 4294967296 | bytes 16777216 | tf_op jit(solution)/shard_map/partial_input/pallas_call | solution.py:309
  92.2 2.1 %collective-permute-done.20 = f32[128,2048]{1,0:T(8,128)S(1)} collective-permute-done((f32[128,2048]{1,0:T(8,128)S(1)}, f32[128,2048]{1,0:T(8,128)S(1)}, u32[]{:S(2)}, u32[]{:S(2)}) %collective-permute-start.20) | collective-permute-done | bytes 1048608 | tf_op jit(solution)/shard_map/ppermute | solution.py:33
  95.5 1.8 %collective-permute-start.23 = (bf16[32,2048]{1,0:T(8,128)(2,1)S(1)}, bf16[32,2048]{1,0:T(8,128)(2,1)S(1)}, u32[]{:S(2)}, u32[]{:S(2)}) collective-permute-start(bf16[32,2048]{1,0:T(8,128)(2,1)S(1)} %get-tuple-element.65), channel_id=1, source_target_pairs={{0,6},{1,7},{2,4},{3,5},{4,2},{5,3},{6,0},{7,1},{8,14},{9,15},{10,... | collective-permute-start | bytes 393224 | tf_op jit(solution)/shard_map/ppermute | solution.py:33
  98.2 6.4 %weight_gradients.1 = (bf16[2048,2048]{1,0:T(8,128)(2,1)}, bf16[2048,2048]{1,0:T(8,128)(2,1)}) custom-call(bf16[4,32,2048]{2,1,0:T(8,128)(2,1)S(1)} %pad_maximum_fusion.1.refs_8_.mine, bf16[4,32,2048]{2,1,0:T(8,128)(2,1)S(1)} %collective-permute-done.24.theirs, bf16[256,2048]{1,0:T(8,128)(2,1)S(1)} %get-tuple-element.54.gate_term, ...), custom_call_target="tpu_custom_call" | custom-call | flops 4294967296 | bytes 16777216 | tf_op jit(solution)/shard_map/weight_gradients/pallas_call | solution.py:342
  (57 shorter events, 8.5 us)
Async XLA Ops:
  0.6 11.6 %collective-permute-start.1 = (bf16[32,2048]{1,0:T(8,128)(2,1)}, bf16[32,2048]{1,0:T(8,128)(2,1)S(1)}, u32[]{:S(2)}, u32[]{:S(2)}) collective-permute-start(bf16[32,2048]{1,0:T(8,128)(2,1)} %refs_0_.3), channel_id=1, source_target_pairs={{0,4},{1,5},{2,6},{3,7},{4,0},{5,1},{6,2},{7,3},{8,12},{9,13},{10,... | collective-permute-start | bytes 393224 | tf_op jit(solution)/shard_map/ppermute | solution.py:33
  3.7 8.5 %collective-permute-start = (bf16[32,2048]{1,0:T(8,128)(2,1)}, bf16[32,2048]{1,0:T(8,128)(2,1)S(1)}, u32[]{:S(2)}, u32[]{:S(2)}) collective-permute-start(bf16[32,2048]{1,0:T(8,128)(2,1)} %refs_0_.3), channel_id=1, source_target_pairs={{0,2},{1,3},{2,0},{3,1},{4,6},{5,7},{6,4},{7,5},{8,10},{9,11},{10,... | collective-permute-start | bytes 393224 | tf_op jit(solution)/shard_map/ppermute | solution.py:33
  5.2 7.1 %collective-permute-start.2 = (bf16[32,2048]{1,0:T(8,128)(2,1)}, bf16[32,2048]{1,0:T(8,128)(2,1)S(1)}, u32[]{:S(2)}, u32[]{:S(2)}) collective-permute-start(bf16[32,2048]{1,0:T(8,128)(2,1)} %refs_0_.3), channel_id=1, source_target_pairs={{0,6},{1,7},{2,4},{3,5},{4,2},{5,3},{6,0},{7,1},{8,14},{9,15},{10,... | collective-permute-start | bytes 393224 | tf_op jit(solution)/shard_map/ppermute | solution.py:33
  6.3 16.2 %copy-start.3 = (bf16[2,64,2048]{2,1,0:T(8,128)(2,1)}, bf16[2,64,2048]{2,1,0:T(8,128)(2,1)S(1)}, u32[]{:S(2)}) copy-start(bf16[2,64,2048]{2,1,0:T(8,128)(2,1)S(1)} %pad_maximum_fusion.refs_0_) | copy-start | bytes 1572868
  6.3 15.0 %collective-permute-start.5 = (bf16[2,64,2048]{2,1,0:T(8,128)(2,1)S(1)}, bf16[2,64,2048]{2,1,0:T(8,128)(2,1)S(1)}, u32[]{:S(2)}, u32[]{:S(2)}) collective-permute-start(bf16[2,64,2048]{2,1,0:T(8,128)(2,1)S(1)} %pad_maximum_fusion.refs_0_), channel_id=1, source_target_pairs={{8,0},{16,8},{24,16},{9,1},{17,9},{25,17},{10,2},{18,10},{26,18},{... | collective-permute-start | bytes 1572872 | tf_op jit(solution)/shard_map/ppermute | solution.py:82
  7.6 14.9 %collective-permute-start.4 = (bf16[2,64,2048]{2,1,0:T(8,128)(2,1)S(1)}, bf16[2,64,2048]{2,1,0:T(8,128)(2,1)S(1)}, u32[]{:S(2)}, u32[]{:S(2)}) collective-permute-start(bf16[2,64,2048]{2,1,0:T(8,128)(2,1)S(1)} %pad_maximum_fusion.refs_0_), channel_id=1, source_target_pairs={{0,8},{8,16},{16,24},{1,9},{9,17},{17,25},{2,10},{10,18},{18,26},{... | collective-permute-start | bytes 1572872 | tf_op jit(solution)/shard_map/ppermute | solution.py:82
  12.2 0.9 copy-start
  13.2 9.3 %collective-permute-start.3 = (bf16[4,32,2048]{2,1,0:T(8,128)(2,1)S(1)}, bf16[4,32,2048]{2,1,0:T(8,128)(2,1)S(1)}, u32[]{:S(2)}, u32[]{:S(2)}) collective-permute-start(bf16[4,32,2048]{2,1,0:T(8,128)(2,1)S(1)} %stacked.1.refs_1_.mine), channel_id=1, source_target_pairs={{0,1},{1,0},{2,3},{3,2},{4,5},{5,4},{6,7},{7,6},{8,9},{9,8},{10,11... | collective-permute-start | bytes 1572872 | tf_op jit(solution)/shard_map/ppermute | solution.py:33
  17.4 24.7 %copy-start.4 = (bf16[32,2048]{1,0:T(8,128)(2,1)S(1)}, bf16[32,2048]{1,0:T(8,128)(2,1)}, u32[]{:S(2)}) copy-start(bf16[32,2048]{1,0:T(8,128)(2,1)} %param.7) | copy-start | bytes 393220
  21.3 1.2 %copy-start.5 = (bf16[2,64,2048]{2,1,0:T(8,128)(2,1)}, bf16[2,64,2048]{2,1,0:T(8,128)(2,1)S(1)}, u32[]{:S(2)}) copy-start(bf16[2,64,2048]{2,1,0:T(8,128)(2,1)S(1)} %collective-permute-done.5.refs_1_.refs_4_) | copy-start | bytes 1572868
  26.2 1.0 copy-start.1
  27.2 11.9 %collective-permute-start.7 = (bf16[64,2048]{1,0:T(8,128)(2,1)S(1)}, bf16[64,2048]{1,0:T(8,128)(2,1)S(1)}, u32[]{:S(2)}, u32[]{:S(2)}) collective-permute-start(bf16[64,2048]{1,0:T(8,128)(2,1)S(1)} %get-tuple-element.37), channel_id=1, source_target_pairs={{0,16},{24,8},{1,17},{25,9},{2,18},{26,10},{3,19},{27,11},{4,20},{... | collective-permute-start | bytes 786440 | tf_op jit(solution)/shard_map/ppermute | solution.py:68
  32.7 6.3 %collective-permute-start.9 = (bf16[64,2048]{1,0:T(8,128)(2,1)S(1)}, bf16[64,2048]{1,0:T(8,128)(2,1)S(1)}, u32[]{:S(2)}, u32[]{:S(2)}) collective-permute-start(bf16[64,2048]{1,0:T(8,128)(2,1)S(1)} %get-tuple-element.34), channel_id=1, source_target_pairs={{24,16},{16,8},{25,17},{17,9},{26,18},{18,10},{27,19},{19,11},{28,... | collective-permute-start | bytes 786440 | tf_op jit(solution)/shard_map/ppermute | solution.py:67
  33.4 8.4 %collective-permute-start.6 = (bf16[64,2048]{1,0:T(8,128)(2,1)S(1)}, bf16[64,2048]{1,0:T(8,128)(2,1)S(1)}, u32[]{:S(2)}, u32[]{:S(2)}) collective-permute-start(bf16[64,2048]{1,0:T(8,128)(2,1)S(1)} %get-tuple-element.34), channel_id=1, source_target_pairs={{0,8},{8,16},{1,9},{9,17},{2,10},{10,18},{3,11},{11,19},{4,12},{12... | collective-permute-start | bytes 786440 | tf_op jit(solution)/shard_map/ppermute | solution.py:66
  34.8 17.1 %collective-permute-start.14 = (bf16[2,64,2048]{2,1,0:T(8,128)(2,1)}, bf16[2,64,2048]{2,1,0:T(8,128)(2,1)}, u32[]{:S(2)}, u32[]{:S(2)}) collective-permute-start(bf16[2,64,2048]{2,1,0:T(8,128)(2,1)} %copy-done.6), channel_id=1, source_target_pairs={{8,16},{16,24},{9,17},{17,25},{10,18},{18,26},{11,19},{19,27},{12,... | collective-permute-start | bytes 1572872 | tf_op jit(solution)/shard_map/ppermute | solution.py:82
  36.2 16.3 %collective-permute-start.16 = (bf16[2,64,2048]{2,1,0:T(8,128)(2,1)}, bf16[2,64,2048]{2,1,0:T(8,128)(2,1)}, u32[]{:S(2)}, u32[]{:S(2)}) collective-permute-start(bf16[2,64,2048]{2,1,0:T(8,128)(2,1)} %copy-done.5), channel_id=1, source_target_pairs={{8,0},{16,8},{9,1},{17,9},{10,2},{18,10},{11,3},{19,11},{12,4},{20... | collective-permute-start | bytes 1572872 | tf_op jit(solution)/shard_map/ppermute | solution.py:82
  42.1 8.1 %collective-permute-start.18 = (bf16[1,32,2048]{2,1,0:T(8,128)(2,1)S(1)}, bf16[1,32,2048]{2,1,0:T(8,128)(2,1)S(1)}, u32[]{:S(2)}, u32[]{:S(2)}) collective-permute-start(bf16[1,32,2048]{2,1,0:T(8,128)(2,1)S(1)} %bitcast.4), channel_id=1, source_target_pairs={{0,2},{1,3},{2,0},{3,1},{4,6},{5,7},{6,4},{7,5},{8,10},{9,11},{10,... | collective-permute-start | bytes 393224 | tf_op jit(solution)/shard_map/ppermute | solution.py:33
  43.6 14.0 %collective-permute-start.8 = (bf16[64,2048]{1,0:T(8,128)(2,1)S(1)}, bf16[64,2048]{1,0:T(8,128)(2,1)S(1)}, u32[]{:S(2)}, u32[]{:S(2)}) collective-permute-start(bf16[64,2048]{1,0:T(8,128)(2,1)S(1)} %get-tuple-element.63), channel_id=1, source_target_pairs={{0,8},{8,16},{16,24},{1,9},{9,17},{17,25},{2,10},{10,18},{18,26},{... | collective-permute-start | bytes 786440 | tf_op jit(solution)/shard_map/ppermute | solution.py:73
  48.9 8.7 %collective-permute-start.10 = (bf16[64,2048]{1,0:T(8,128)(2,1)S(1)}, bf16[64,2048]{1,0:T(8,128)(2,1)S(1)}, u32[]{:S(2)}, u32[]{:S(2)}) collective-permute-start(bf16[64,2048]{1,0:T(8,128)(2,1)S(1)} %get-tuple-element.62), channel_id=1, source_target_pairs={{24,16},{16,8},{8,0},{25,17},{17,9},{9,1},{26,18},{18,10},{10,2},{... | collective-permute-start | bytes 786440 | tf_op jit(solution)/shard_map/ppermute | solution.py:74
  50.2 22.6 %collective-permute-start.19 = (bf16[2,32,2048]{2,1,0:T(8,128)(2,1)S(1)}, bf16[2,32,2048]{2,1,0:T(8,128)(2,1)S(1)}, u32[]{:S(2)}, u32[]{:S(2)}) collective-permute-start(bf16[2,32,2048]{2,1,0:T(8,128)(2,1)S(1)} %pad_maximum_fusion.2), channel_id=1, source_target_pairs={{0,4},{1,5},{2,6},{3,7},{4,0},{5,1},{6,2},{7,3},{8,12},{9,13},{10,... | collective-permute-start | bytes 786440 | tf_op jit(solution)/shard_map/ppermute | solution.py:33
  51.8 21.1 %collective-permute-start.15 = (bf16[2,64,2048]{2,1,0:T(8,128)(2,1)}, bf16[2,64,2048]{2,1,0:T(8,128)(2,1)S(1)}, u32[]{:S(2)}, u32[]{:S(2)}) collective-permute-start(bf16[2,64,2048]{2,1,0:T(8,128)(2,1)} %collective-permute-done.14.refs_2_), channel_id=1, source_target_pairs={{16,24},{17,25},{18,26},{19,27},{20,28},{21,29},{22,30},{23,31}} | collective-permute-start | bytes 1572872 | tf_op jit(solution)/shard_map/ppermute | solution.py:82
  52.5 24.6 %collective-permute-start.17 = (bf16[2,64,2048]{2,1,0:T(8,128)(2,1)}, bf16[2,64,2048]{2,1,0:T(8,128)(2,1)S(1)}, u32[]{:S(2)}, u32[]{:S(2)}) collective-permute-start(bf16[2,64,2048]{2,1,0:T(8,128)(2,1)} %collective-permute-done.16.refs_5_), channel_id=1, source_target_pairs={{8,0},{9,1},{10,2},{11,3},{12,4},{13,5},{14,6},{15,7}} | collective-permute-start | bytes 1572872 | tf_op jit(solution)/shard_map/ppermute | solution.py:82
  57.7 15.1 %collective-permute-start.12 = (bf16[64,2048]{1,0:T(8,128)(2,1)S(1)}, bf16[64,2048]{1,0:T(8,128)(2,1)S(1)}, u32[]{:S(2)}, u32[]{:S(2)}) collective-permute-start(bf16[64,2048]{1,0:T(8,128)(2,1)S(1)} %summed.1.refs_2_.refs_0_), channel_id=1, source_target_pairs={{0,16},{8,24},{16,0},{24,8},{1,17},{9,25},{17,1},{25,9},{2,18},{10... | collective-permute-start | bytes 786440 | tf_op jit(solution)/shard_map/ppermute | solution.py:33
  62.4 15.5 %copy-start.2 = (bf16[256,2048]{1,0:T(8,128)(2,1)S(1)}, bf16[256,2048]{1,0:T(8,128)(2,1)}, u32[]{:S(2)}) copy-start(bf16[256,2048]{1,0:T(8,128)(2,1)} %copy-done.1) | copy-start | bytes 3145732
  62.4 22.0 %collective-permute-start.11 = (bf16[64,2048]{1,0:T(8,128)(2,1)S(1)}, bf16[64,2048]{1,0:T(8,128)(2,1)S(1)}, u32[]{:S(2)}, u32[]{:S(2)}) collective-permute-start(bf16[64,2048]{1,0:T(8,128)(2,1)S(1)} %summed.1.refs_2_.refs_0_), channel_id=1, source_target_pairs={{0,8},{8,0},{16,24},{24,16},{1,9},{9,1},{17,25},{25,17},{2,10},{10... | collective-permute-start | bytes 786440 | tf_op jit(solution)/shard_map/ppermute | solution.py:33
  72.8 13.1 %collective-permute-start.13 = (bf16[64,2048]{1,0:T(8,128)(2,1)S(1)}, bf16[64,2048]{1,0:T(8,128)(2,1)S(1)}, u32[]{:S(2)}, u32[]{:S(2)}) collective-permute-start(bf16[64,2048]{1,0:T(8,128)(2,1)S(1)} %collective-permute-done.12.refs_8_.refs_2_), channel_id=1, source_target_pairs={{0,8},{8,0},{16,24},{24,16},{1,9},{9,1},{17,25},{25,17},{2,10},{10... | collective-permute-start | bytes 786440 | tf_op jit(solution)/shard_map/ppermute | solution.py:33
  72.9 4.2 %copy-start.7 = (bf16[2,64,2048]{2,1,0:T(8,128)(2,1)}, bf16[2,64,2048]{2,1,0:T(8,128)(2,1)S(1)}, u32[]{:S(2)}) copy-start(bf16[2,64,2048]{2,1,0:T(8,128)(2,1)S(1)} %collective-permute-done.15.refs_3_) | copy-start | bytes 1572868
  91.7 2.7 %collective-permute-start.20 = (f32[128,2048]{1,0:T(8,128)S(1)}, f32[128,2048]{1,0:T(8,128)S(1)}, u32[]{:S(2)}, u32[]{:S(2)}) collective-permute-start(f32[128,2048]{1,0:T(8,128)S(1)} %get-tuple-element.51), channel_id=1, source_target_pairs={{0,1},{1,0},{2,3},{3,2},{4,5},{5,4},{6,7},{7,6},{8,9},{9,8},{10,11... | collective-permute-start | bytes 3145736 | tf_op jit(solution)/shard_map/ppermute | solution.py:33
  91.7 6.4 %collective-permute-start.24 = (bf16[4,32,2048]{2,1,0:T(8,128)(2,1)S(1)}, bf16[4,32,2048]{2,1,0:T(8,128)(2,1)S(1)}, u32[]{:S(2)}, u32[]{:S(2)}) collective-permute-start(bf16[4,32,2048]{2,1,0:T(8,128)(2,1)S(1)} %pad_maximum_fusion.1.refs_8_.mine), channel_id=1, source_target_pairs={{0,1},{1,0},{2,3},{3,2},{4,5},{5,4},{6,7},{7,6},{8,9},{9,8},{10,11... | collective-permute-start | bytes 1572872 | tf_op jit(solution)/shard_map/ppermute | solution.py:33
  94.6 10.0 %collective-permute-start.21 = (bf16[32,2048]{1,0:T(8,128)(2,1)S(1)}, bf16[32,2048]{1,0:T(8,128)(2,1)S(1)}, u32[]{:S(2)}, u32[]{:S(2)}) collective-permute-start(bf16[32,2048]{1,0:T(8,128)(2,1)S(1)} %get-tuple-element.64), channel_id=1, source_target_pairs={{0,2},{1,3},{2,0},{3,1},{4,6},{5,7},{6,4},{7,5},{8,10},{9,11},{10,... | collective-permute-start | bytes 393224 | tf_op jit(solution)/shard_map/ppermute | solution.py:33
  95.5 9.1 %collective-permute-start.23 = (bf16[32,2048]{1,0:T(8,128)(2,1)S(1)}, bf16[32,2048]{1,0:T(8,128)(2,1)S(1)}, u32[]{:S(2)}, u32[]{:S(2)}) collective-permute-start(bf16[32,2048]{1,0:T(8,128)(2,1)S(1)} %get-tuple-element.65), channel_id=1, source_target_pairs={{0,6},{1,7},{2,4},{3,5},{4,2},{5,3},{6,0},{7,1},{8,14},{9,15},{10,... | collective-permute-start | bytes 393224 | tf_op jit(solution)/shard_map/ppermute | solution.py:33
  97.3 7.8 %collective-permute-start.22 = (bf16[32,2048]{1,0:T(8,128)(2,1)S(1)}, bf16[32,2048]{1,0:T(8,128)(2,1)S(1)}, u32[]{:S(2)}, u32[]{:S(2)}) collective-permute-start(bf16[32,2048]{1,0:T(8,128)(2,1)S(1)} %get-tuple-element.66), channel_id=1, source_target_pairs={{0,4},{1,5},{2,6},{3,7},{4,0},{5,1},{6,2},{7,3},{8,12},{9,13},{10,... | collective-permute-start | bytes 393224 | tf_op jit(solution)/shard_map/ppermute | solution.py:33
  (2 other events, 1.6 us)

commit v4 on v3

--- a/solution.py
+++ b/solution.py
@@ -65,7 +65,8 @@
 def reduce_line(parts, sends, col):
     right = lax.ppermute(sends[2], "col", [(0, 1), (1, 2)]).astype(F32)
     left = lax.ppermute(sends[2], "col", [(3, 2), (2, 1)]).astype(F32)
-    over = lax.ppermute(sends[3], "col", [(0, 2), (3, 1)]).astype(F32)
+    came_over = lax.ppermute(sends[3], "col", [(0, 2), (3, 1)])
+    over = came_over.astype(F32)
     right = right + jnp.where(col == 1, parts[3], parts[1]) + jnp.where(col == 2, over, 0.0)
     left = left + jnp.where(col == 2, parts[3], parts[1]) + jnp.where(col == 1, over, 0.0)
     right, left = right.astype(BF16), left.astype(BF16)
@@ -73,7 +74,7 @@
         lax.ppermute(right, "col", [(0, 1), (1, 2), (2, 3)]),
         lax.ppermute(left, "col", [(3, 2), (2, 1), (1, 0)]),
     ]
-    return arrived, right
+    return arrived, came_over
 
 
 def relay_col(low, high, n_col, step):
@@ -152,18 +153,22 @@
 
 
 def hidden_kernel(n_row, n_col, kept, early, offsets, mine, theirs, weight, *refs):
-    grad_all, token, *parts = refs[-2 - len(kept) - len(early) :]
+    grad_out, token, *parts, grad_all, left = refs[-4 - len(kept) - len(early) :]
     token[...] = jnp.zeros_like(token)
     rows, part = mine.shape[1], parts[0].shape[0]
     kinds = [(p, F32) for p in kept] + [(p, BF16) for p in early]
     for x in range(n_row):
         grad_all[pl.ds(pl.multiple_of(offsets[x], rows), rows), :] = (theirs if x % 2 else mine)[x // 2]
+    copy = pltpu.make_async_copy(grad_all, grad_out, left)
     step = stripe(weight.shape[0])
     for i in range(weight.shape[0] // step):
         at = slice(i * step, (i + 1) * step)
         total = lax.dot_general(grad_all[...], weight[at, :], NT, preferred_element_type=F32)
+        if i == 0:
+            copy.start()
         for ref, (p, kind) in zip(parts, kinds):
             ref[:, at] = total[p * part : (p + 1) * part].astype(kind)
+    copy.wait()
 
 
 def partial_hidden(mine, theirs, weight, behind, offsets, n_col, kept, early):
@@ -174,11 +179,12 @@
     grad_all, token, *parts = pl.pallas_call(
         functools.partial(hidden_kernel, n_row, n_col, kept, early),
         in_specs=[IN_SMEM] + [IN_VMEM] * 3 + [IN_HBM] * len(behind),
-        out_specs=[IN_VMEM] * (2 + len(kept) + len(early)),
-        out_shape=[jax.ShapeDtypeStruct((tokens, width), BF16), jax.ShapeDtypeStruct((8, 128), F32)]
+        out_specs=[IN_HBM] + [IN_VMEM] * (1 + len(kept) + len(early)),
+        out_shape=[pltpu.HBM((tokens, width), BF16), jax.ShapeDtypeStruct((8, 128), F32)]
         + [jax.ShapeDtypeStruct((part, units), F32)] * len(kept)
         + [jax.ShapeDtypeStruct((part, units), BF16)] * len(early),
-        compiler_params=params(2),
+        scratch_shapes=[pltpu.VMEM((tokens, width), BF16), pltpu.SemaphoreType.DMA(())],
+        compiler_params=params(3),
         cost_estimate=pl.CostEstimate(
             flops=2 * tokens * width * units, bytes_accessed=2 * units * width, transcendentals=0
         ),
@@ -220,13 +226,13 @@
 
 
 def down_kernel(n_col, scale, place, *refs):
-    moved, grad_all = refs[: 2 * n_col - 1], refs[2 * n_col - 1]
-    down_grad, up_factor, gate_factor, saved, arrived, buffer, left = refs[-7:]
+    moved, grad_out = refs[: 2 * n_col - 1], refs[2 * n_col - 1]
+    down_grad, up_factor, gate_factor, saved, grad_all, arrived, buffer, left = refs[-8:]
     loads = [pltpu.make_async_copy(block, saved.at[k], arrived.at[k]) for k, block in enumerate(moved)]
+    loads.append(pltpu.make_async_copy(grad_out, grad_all, arrived.at[len(moved)]))
     for copy in loads:
         copy.start()
-    for copy in loads:
-        copy.wait()
+    waiting = set(range(len(moved)))
     blocks = [saved.at[k] for k in range(len(moved))]
     from_low, from_high = blocks[:n_col], blocks[:1] + blocks[n_col:]
     _, part, units = from_low[0].shape
@@ -237,12 +243,19 @@
         at = slice(i * step, (i + 1) * step)
         hidden = []
         for p in range(n_col):
+            hops = {abs((c ^ p) - c) for c in range(n_col)}
+            for k in sorted(waiting):
+                if (k if k < n_col else k - n_col + 1) in hops:
+                    loads[k].wait()
+                    waiting.remove(k)
             g, u = (pick(from_low, from_high, p, col, which, at) for which in range(2))
             s = 1.0 / (1.0 + jnp.exp(-g))
             silu = g * s
             hidden.append((silu * u).astype(BF16))
             up_factor[p * part : (p + 1) * part, at] = silu
             gate_factor[p * part : (p + 1) * part, at] = u * s * (1.0 + g * (1.0 - s))
+        if i == 0:
+            loads[-1].wait()
         product = lax.dot_general(
             jnp.concatenate(hidden, axis=0), grad_all[...], TN, preferred_element_type=F32
         )
@@ -258,23 +271,26 @@
     tokens, width = grad_all.shape
     return pl.pallas_call(
         functools.partial(down_kernel, n_col, scale),
-        in_specs=[IN_SMEM] + [IN_HBM] * (2 * n_col - 1) + [IN_VMEM] + [IN_ANY] * len(behind),
+        in_specs=[IN_SMEM] + [IN_ANY] * (2 * n_col - 1) + [IN_HBM] + [IN_ANY] * len(behind),
         out_specs=[IN_HBM] + [IN_VMEM] * 2,
         out_shape=[jax.ShapeDtypeStruct((units, width), BF16)] + [jax.ShapeDtypeStruct((tokens, units), F32)] * 2,
         scratch_shapes=[
             pltpu.VMEM((2 * n_col - 1,) + from_low[0].shape, BF16),
-            pltpu.SemaphoreType.DMA((2 * n_col - 1,)),
+            pltpu.VMEM((tokens, width), BF16),
+            pltpu.SemaphoreType.DMA((2 * n_col,)),
             pltpu.VMEM((units, width), BF16),
             pltpu.SemaphoreType.DMA((units // stripe(units),)),
         ],
-        compiler_params=params(14),
+        compiler_params=params(15),
         cost_estimate=pl.CostEstimate(
             flops=1 * 2 * tokens * width * units,
             bytes_accessed=2 * units * width + 12 * tokens * units,
             transcendentals=tokens * units,
         ),
         name="down_gradient",
-    )(place, *pinned(*from_low, *from_high[1:]), grad_all, *behind)
+    )(
+        place, *pinned(*from_low[:-1]), from_low[-1], *pinned(*from_high[1:-1]), from_high[-1], *pinned(grad_all), *behind
+    )
 
 
 def input_kernel(n_row, n_col, offsets, *refs):

time: 106 us -> 105 us (level)
  starting transfers between devices: 41.4 us -> 44 us
  local copies, waits for them, and re-layouts: 3.59 us -> 1.03 us
  waiting for transfers between devices: 25 us -> 23.3 us
    unnamed x18 -> x8, local copies, waits for them, and re-layouts: 3.47 us -> 0.91 us
    ppermute x1, waiting for transfers between devices: 3.6 us -> 1.41 us  [reduce_line(): lax.ppermute(left, 'col', [(3, 2), (2, 1), (1, 0)])]
    ppermute x1, waiting for transfers between devices: 2.81 us -> 1.31 us  [reduce_line(): right = lax.ppermute(sends[2], 'col', [(0, 1), (1, 2)]).astype(F32)]
    ppermute x14, starting transfers between devices: 16.5 us -> 17.9 us  [swap(): return lax.ppermute(block, axis, flip(lax.axis_size(axis), mask))]
    ppermute x6, waiting for transfers between devices: 9.27 us -> 10.5 us  [relay_col(): return (lax.ppermute(low, 'col', up), lax.ppermute(high, 'col', down))]
  transfers between devices with their start and end apart: 25 -> 25, of which waited for: 10 -> 11; matrix products, arithmetic and copies ran while one was open for 2% -> 2% of each run, Pallas kernels for 22% -> 23%
where the time goes in v4:
time: 105 us
  starting transfers between devices  44 us (42%)
  Pallas kernels  33.1 us (32%)
  waiting for transfers between devices  23.3 us (22%)
  other arithmetic  2.37 us (2%)
    ppermute x14, starting transfers between devices, swap(): return lax.ppermute(block, axis, flip(lax.axis_size(axis), mask))  17.9 us
    ppermute x6, starting transfers between devices, relay_col(): return (lax.ppermute(low, 'col', up), lax.ppermute(high, 'col', down))  11.3 us
    pallas_call x2, Pallas kernels, fetch(): pl.pallas_call(functools.partial(fetch_kernel, len(weights)), in_specs=[I...  10.6 us
    ppermute x6, waiting for transfers between devices, relay_col(): return (lax.ppermute(low, 'col', up), lax.ppermute(high, 'col', down))  10.5 us
    ppermute x14, waiting for transfers between devices, swap(): return lax.ppermute(block, axis, flip(lax.axis_size(axis), mask))  8.57 us
    pallas_call x1, Pallas kernels, down_gradient(): pl.pallas_call(functools.partial(down_kernel, n_col, scale), in_specs=[IN...  6.53 us
    pallas_call x1, Pallas kernels, weight_gradients(): pl.pallas_call(functools.partial(weight_kernel, scale), in_specs=[IN_VMEM...  6.43 us
    ppermute x1, starting transfers between devices, reduce_line(): lax.ppermute(right, 'col', [(0, 1), (1, 2), (2, 3)])  5.79 us
  transfers between devices with their start and end apart: 25, of which 11 were waited for; matrix products, arithmetic and copies ran while one was open for 2% of the time, Pallas kernels for 23%

profile of v4, /device:TPU:0, one launch (start us, length us, event | category | flops | bytes accessed | tf_op | source)
XLA Modules:
  0.0 104.7 jit_solution(7651668062691987900)
XLA Ops:
  0.6 3.0 %collective-permute-start.1 = (bf16[32,2048]{1,0:T(8,128)(2,1)}, bf16[32,2048]{1,0:T(8,128)(2,1)S(1)}, u32[]{:S(2)}, u32[]{:S(2)}) collective-permute-start(bf16[32,2048]{1,0:T(8,128)(2,1)} %refs_0_.3), channel_id=1, source_target_pairs={{0,4},{1,5},{2,6},{3,7},{4,0},{5,1},{6,2},{7,3},{8,12},{9,13},{10,... | collective-permute-start | bytes 393224 | tf_op jit(solution)/shard_map/ppermute | solution.py:33
  3.7 1.5 %collective-permute-start = (bf16[32,2048]{1,0:T(8,128)(2,1)}, bf16[32,2048]{1,0:T(8,128)(2,1)S(1)}, u32[]{:S(2)}, u32[]{:S(2)}) collective-permute-start(bf16[32,2048]{1,0:T(8,128)(2,1)} %refs_0_.3), channel_id=1, source_target_pairs={{0,2},{1,3},{2,0},{3,1},{4,6},{5,7},{6,4},{7,5},{8,10},{9,11},{10,... | collective-permute-start | bytes 393224 | tf_op jit(solution)/shard_map/ppermute | solution.py:33
  6.3 1.3 %collective-permute-start.5 = (bf16[2,64,2048]{2,1,0:T(8,128)(2,1)S(1)}, bf16[2,64,2048]{2,1,0:T(8,128)(2,1)S(1)}, u32[]{:S(2)}, u32[]{:S(2)}) collective-permute-start(bf16[2,64,2048]{2,1,0:T(8,128)(2,1)S(1)} %pad_maximum_fusion.refs_0_), channel_id=1, source_target_pairs={{8,0},{16,8},{24,16},{9,1},{17,9},{25,17},{10,2},{18,10},{26,18},{... | collective-permute-start | bytes 1572872 | tf_op jit(solution)/shard_map/ppermute | solution.py:83
  7.6 5.3 %collective-permute-start.4 = (bf16[2,64,2048]{2,1,0:T(8,128)(2,1)S(1)}, bf16[2,64,2048]{2,1,0:T(8,128)(2,1)}, u32[]{:S(2)}, u32[]{:S(2)}) collective-permute-start(bf16[2,64,2048]{2,1,0:T(8,128)(2,1)S(1)} %pad_maximum_fusion.refs_0_), channel_id=1, source_target_pairs={{0,8},{8,16},{16,24},{1,9},{9,17},{17,25},{2,10},{10,18},{18,26},{... | collective-permute-start | bytes 1572872 | tf_op jit(solution)/shard_map/ppermute | solution.py:83
  14.0 4.1 %fetch.2 = (bf16[2048,2048]{1,0:T(8,128)(2,1)S(1)}, f32[8,128]{1,0:T(8,128)}) custom-call(bf16[2048,2048]{1,0:T(8,128)(2,1)} %refs_0_.4, bf16[4,32,2048]{2,1,0:T(8,128)(2,1)S(1)} %stacked.1.refs_1_.mine), custom_call_target="tpu_custom_call" | custom-call | bytes 1024 | tf_op jit(solution)/shard_map/fetch/pallas_call | solution.py:111
  18.2 3.1 %collective-permute-done.5.refs_1_.refs_4_ = bf16[2,64,2048]{2,1,0:T(8,128)(2,1)S(1)} collective-permute-done((bf16[2,64,2048]{2,1,0:T(8,128)(2,1)S(1)}, bf16[2,64,2048]{2,1,0:T(8,128)(2,1)S(1)}, u32[]{:S(2)}, u32[]{:S(2)}) %collective-permute-start.5) | collective-permute-done | bytes 524320 | tf_op jit(solution)/shard_map/ppermute | solution.py:83
  21.3 1.2 %collective-permute-done.4.refs_0_.refs_1_ = bf16[2,64,2048]{2,1,0:T(8,128)(2,1)} collective-permute-done((bf16[2,64,2048]{2,1,0:T(8,128)(2,1)S(1)}, bf16[2,64,2048]{2,1,0:T(8,128)(2,1)}, u32[]{:S(2)}, u32[]{:S(2)}) %collective-permute-start.4) | collective-permute-done | bytes 524320 | tf_op jit(solution)/shard_map/ppermute | solution.py:83
  22.5 3.7 %partial_hidden.1 = (bf16[256,2048]{1,0:T(8,128)(2,1)}, f32[8,128]{1,0:T(8,128)S(1)}, f32[64,2048]{1,0:T(8,128)S(1)}, f32[64,2048]{1,0:T(8,128)S(1)}, f32[64,204...) custom-call(s32[8]{0:T(128)S(1)} %fusion.10.offsets, ...), custom_call_target="tpu_custom_call" | custom-call | flops 2147483648 | bytes 8388608 | tf_op jit(solution)/shard_map/partial_hidden/pallas_call | solution.py:179
  26.2 5.7 %collective-permute-start.7 = (bf16[64,2048]{1,0:T(8,128)(2,1)S(1)}, bf16[64,2048]{1,0:T(8,128)(2,1)S(1)}, u32[]{:S(2)}, u32[]{:S(2)}) collective-permute-start(bf16[64,2048]{1,0:T(8,128)(2,1)S(1)} %get-tuple-element.37), channel_id=1, source_target_pairs={{0,16},{24,8},{1,17},{25,9},{2,18},{26,10},{3,19},{27,11},{4,20},{... | collective-permute-start | bytes 786440 | tf_op jit(solution)/shard_map/ppermute | solution.py:68
  32.6 1.3 %collective-permute-start.6 = (bf16[64,2048]{1,0:T(8,128)(2,1)S(1)}, bf16[64,2048]{1,0:T(8,128)(2,1)S(1)}, u32[]{:S(2)}, u32[]{:S(2)}) collective-permute-start(bf16[64,2048]{1,0:T(8,128)(2,1)S(1)} %get-tuple-element.34), channel_id=1, source_target_pairs={{0,8},{8,16},{1,9},{9,17},{2,10},{10,18},{3,11},{11,19},{4,12},{12... | collective-permute-start | bytes 786440 | tf_op jit(solution)/shard_map/ppermute | solution.py:66
  33.9 1.5 %collective-permute-start.14 = (bf16[2,64,2048]{2,1,0:T(8,128)(2,1)}, bf16[2,64,2048]{2,1,0:T(8,128)(2,1)}, u32[]{:S(2)}, u32[]{:S(2)}) collective-permute-start(bf16[2,64,2048]{2,1,0:T(8,128)(2,1)} %collective-permute-done.4.refs_0_.refs_1_), channel_id=1, source_target_pairs={{8,16},{16,24},{9,17},{17,25},{10,18},{18,26},{11,19},{19,27},{12,... | collective-permute-start | bytes 1572872 | tf_op jit(solution)/shard_map/ppermute | solution.py:83
  35.3 1.3 %collective-permute-start.16 = (bf16[2,64,2048]{2,1,0:T(8,128)(2,1)}, bf16[2,64,2048]{2,1,0:T(8,128)(2,1)}, u32[]{:S(2)}, u32[]{:S(2)}) collective-permute-start(bf16[2,64,2048]{2,1,0:T(8,128)(2,1)} %copy-done.3), channel_id=1, source_target_pairs={{8,0},{16,8},{9,1},{17,9},{10,2},{18,10},{11,3},{19,11},{12,4},{20... | collective-permute-start | bytes 1572872 | tf_op jit(solution)/shard_map/ppermute | solution.py:83
  36.6 1.5 %collective-permute-done.7 = bf16[64,2048]{1,0:T(8,128)(2,1)S(1)} collective-permute-done((bf16[64,2048]{1,0:T(8,128)(2,1)S(1)}, bf16[64,2048]{1,0:T(8,128)(2,1)S(1)}, u32[]{:S(2)}, u32[]{:S(2)}) %collective-permute-start.7) | collective-permute-done | bytes 262176 | tf_op jit(solution)/shard_map/ppermute | solution.py:68
  38.2 1.5 %collective-permute-start.18 = (bf16[1,32,2048]{2,1,0:T(8,128)(2,1)S(1)}, bf16[1,32,2048]{2,1,0:T(8,128)(2,1)S(1)}, u32[]{:S(2)}, u32[]{:S(2)}) collective-permute-start(bf16[1,32,2048]{2,1,0:T(8,128)(2,1)S(1)} %bitcast.4), channel_id=1, source_target_pairs={{0,2},{1,3},{2,0},{3,1},{4,6},{5,7},{6,4},{7,5},{8,10},{9,11},{10,... | collective-permute-start | bytes 393224 | tf_op jit(solution)/shard_map/ppermute | solution.py:33
  39.7 1.3 %collective-permute-done.6 = bf16[64,2048]{1,0:T(8,128)(2,1)S(1)} collective-permute-done((bf16[64,2048]{1,0:T(8,128)(2,1)S(1)}, bf16[64,2048]{1,0:T(8,128)(2,1)S(1)}, u32[]{:S(2)}, u32[]{:S(2)}) %collective-permute-start.6) | collective-permute-done | bytes 262176 | tf_op jit(solution)/shard_map/ppermute | solution.py:66
  41.2 1.3 %collective-permute-start.10 = (bf16[64,2048]{1,0:T(8,128)(2,1)S(1)}, bf16[64,2048]{1,0:T(8,128)(2,1)S(1)}, u32[]{:S(2)}, u32[]{:S(2)}) collective-permute-start(bf16[64,2048]{1,0:T(8,128)(2,1)S(1)} %get-tuple-element.62), channel_id=1, source_target_pairs={{24,16},{16,8},{8,0},{25,17},{17,9},{9,1},{26,18},{18,10},{10,2},{... | collective-permute-start | bytes 786440 | tf_op jit(solution)/shard_map/ppermute | solution.py:75
  42.5 5.8 %collective-permute-start.8 = (bf16[64,2048]{1,0:T(8,128)(2,1)S(1)}, bf16[64,2048]{1,0:T(8,128)(2,1)S(1)}, u32[]{:S(2)}, u32[]{:S(2)}) collective-permute-start(bf16[64,2048]{1,0:T(8,128)(2,1)S(1)} %get-tuple-element.63), channel_id=1, source_target_pairs={{0,8},{8,16},{16,24},{1,9},{9,17},{17,25},{2,10},{10,18},{18,26},{... | collective-permute-start | bytes 786440 | tf_op jit(solution)/shard_map/ppermute | solution.py:74
  48.4 1.7 %collective-permute-start.19 = (bf16[2,32,2048]{2,1,0:T(8,128)(2,1)S(1)}, bf16[2,32,2048]{2,1,0:T(8,128)(2,1)S(1)}, u32[]{:S(2)}, u32[]{:S(2)}) collective-permute-start(bf16[2,32,2048]{2,1,0:T(8,128)(2,1)S(1)} %pad_maximum_fusion.2), channel_id=1, source_target_pairs={{0,4},{1,5},{2,6},{3,7},{4,0},{5,1},{6,2},{7,3},{8,12},{9,13},{10,... | collective-permute-start | bytes 786440 | tf_op jit(solution)/shard_map/ppermute | solution.py:33
  50.7 2.0 %collective-permute-done.16.refs_5_ = bf16[2,64,2048]{2,1,0:T(8,128)(2,1)} collective-permute-done((bf16[2,64,2048]{2,1,0:T(8,128)(2,1)}, bf16[2,64,2048]{2,1,0:T(8,128)(2,1)}, u32[]{:S(2)}, u32[]{:S(2)}) %collective-permute-start.16) | collective-permute-done | bytes 524320 | tf_op jit(solution)/shard_map/ppermute | solution.py:83
  52.7 1.3 %collective-permute-start.17 = (bf16[2,64,2048]{2,1,0:T(8,128)(2,1)}, bf16[2,64,2048]{2,1,0:T(8,128)(2,1)S(1)}, u32[]{:S(2)}, u32[]{:S(2)}) collective-permute-start(bf16[2,64,2048]{2,1,0:T(8,128)(2,1)} %collective-permute-done.16.refs_5_), channel_id=1, source_target_pairs={{8,0},{9,1},{10,2},{11,3},{12,4},{13,5},{14,6},{15,7}} | collective-permute-start | bytes 1572872 | tf_op jit(solution)/shard_map/ppermute | solution.py:83
  53.9 1.4 %collective-permute-done.10.refs_2_ = bf16[64,2048]{1,0:T(8,128)(2,1)S(1)} collective-permute-done((bf16[64,2048]{1,0:T(8,128)(2,1)S(1)}, bf16[64,2048]{1,0:T(8,128)(2,1)S(1)}, u32[]{:S(2)}, u32[]{:S(2)}) %collective-permute-start.10) | collective-permute-done | bytes 262176 | tf_op jit(solution)/shard_map/ppermute | solution.py:75
  55.5 5.9 %collective-permute-start.12 = (bf16[64,2048]{1,0:T(8,128)(2,1)S(1)}, bf16[64,2048]{1,0:T(8,128)(2,1)S(1)}, u32[]{:S(2)}, u32[]{:S(2)}) collective-permute-start(bf16[64,2048]{1,0:T(8,128)(2,1)S(1)} %summed.1.refs_2_.refs_0_), channel_id=1, source_target_pairs={{0,16},{8,24},{16,0},{24,8},{1,17},{9,25},{17,1},{25,9},{2,18},{10... | collective-permute-start | bytes 786440 | tf_op jit(solution)/shard_map/ppermute | solution.py:33
  61.6 6.5 %fetch.3 = (bf16[2048,2048]{1,0:T(8,128)(2,1)S(1)}, bf16[2048,2048]{1,0:T(8,128)(2,1)S(1)}, f32[8,128]{1,0:T(8,128)}) custom-call(bf16[2048,2048]{1,0:T(8,128)(2,1)} %refs_0_.5, bf16[2048,2048]{1,0:T(8,128)(2,1)} %refs_1_.1, bf16[64,2048]{1,0:T(8,128)(2,1)S(1)} %summed.1.refs_2_.refs_0_), custom_call_target="tpu_custom_call" | custom-call | bytes 1024 | tf_op jit(solution)/shard_map/fetch/pallas_call | solution.py:111
  68.1 3.8 %collective-permute-done.12.refs_8_.refs_2_ = bf16[64,2048]{1,0:T(8,128)(2,1)S(1)} collective-permute-done((bf16[64,2048]{1,0:T(8,128)(2,1)S(1)}, bf16[64,2048]{1,0:T(8,128)(2,1)S(1)}, u32[]{:S(2)}, u32[]{:S(2)}) %collective-permute-start.12) | collective-permute-done | bytes 262176 | tf_op jit(solution)/shard_map/ppermute | solution.py:33
  72.0 4.2 %collective-permute-done.17.refs_6_ = bf16[2,64,2048]{2,1,0:T(8,128)(2,1)S(1)} collective-permute-done((bf16[2,64,2048]{2,1,0:T(8,128)(2,1)}, bf16[2,64,2048]{2,1,0:T(8,128)(2,1)S(1)}, u32[]{:S(2)}, u32[]{:S(2)}) %collective-permute-start.17) | collective-permute-done | bytes 524320 | tf_op jit(solution)/shard_map/ppermute | solution.py:83
  76.2 6.5 %down_gradient.1 = (bf16[2048,2048]{1,0:T(8,128)(2,1)}, f32[256,2048]{1,0:T(8,128)S(1)}, f32[256,2048]{1,0:T(8,128)S(1)}) custom-call(s32[1]{0:T(128)} %bitcast.2.place, bf16[2,64,2048]{2,1,0:T(8,128)(2,1)} %copy-done.1, bf16[2,64,2048]{2,1,0:T(8,128)(2,1)} %collective-permute-done.4.refs_0_.refs_1_, bf16[2,64,2048]{2,1,0:T(8,128)(2,1)} %collective-permute-done.14.refs_2_, ...), custom_call_target="tpu_custom_call" | custom-call | flops 2147483648 | bytes 14680064 | tf_op jit(solution)/shard_map/down_gradient/pallas_call | solution.py:272
  82.8 2.3 %collective-permute-done.13.refs_3_ = bf16[64,2048]{1,0:T(8,128)(2,1)S(1)} collective-permute-done((bf16[64,2048]{1,0:T(8,128)(2,1)S(1)}, bf16[64,2048]{1,0:T(8,128)(2,1)S(1)}, u32[]{:S(2)}, u32[]{:S(2)}) %collective-permute-start.13) | collective-permute-done | bytes 262176 | tf_op jit(solution)/shard_map/ppermute | solution.py:33
  85.0 5.6 %partial_input.1 = (bf16[256,2048]{1,0:T(8,128)(2,1)S(1)}, bf16[256,2048]{1,0:T(8,128)(2,1)S(1)}, f32[128,2048]{1,0:T(8,128)S(1)}, f32[128,2048]{1,0:T(8,128)S(1)}, f32[8,128]{1,0:T(8,128)S(1)}) custom-call(s32[8]{0:T(128)S(1)} %fusion.11.offsets, bf16[64,2048]{1,0:T(8,128)(2,1)S(1)} %summed.1.refs_2_.refs_0_, ...), custom_call_target="tpu_custom_call" | custom-call | flops 4294967296 | bytes 16777216 | tf_op jit(solution)/shard_map/partial_input/pallas_call | solution.py:325
  91.2 2.1 %collective-permute-done.20 = f32[128,2048]{1,0:T(8,128)S(1)} collective-permute-done((f32[128,2048]{1,0:T(8,128)S(1)}, f32[128,2048]{1,0:T(8,128)S(1)}, u32[]{:S(2)}, u32[]{:S(2)}) %collective-permute-start.20) | collective-permute-done | bytes 1048608 | tf_op jit(solution)/shard_map/ppermute | solution.py:33
  93.6 1.2 %collective-permute-start.21 = (bf16[32,2048]{1,0:T(8,128)(2,1)S(1)}, bf16[32,2048]{1,0:T(8,128)(2,1)S(1)}, u32[]{:S(2)}, u32[]{:S(2)}) collective-permute-start(bf16[32,2048]{1,0:T(8,128)(2,1)S(1)} %get-tuple-element.64), channel_id=1, source_target_pairs={{0,2},{1,3},{2,0},{3,1},{4,6},{5,7},{6,4},{7,5},{8,10},{9,11},{10,... | collective-permute-start | bytes 393224 | tf_op jit(solution)/shard_map/ppermute | solution.py:33
  94.8 1.4 %collective-permute-start.23 = (bf16[32,2048]{1,0:T(8,128)(2,1)S(1)}, bf16[32,2048]{1,0:T(8,128)(2,1)S(1)}, u32[]{:S(2)}, u32[]{:S(2)}) collective-permute-start(bf16[32,2048]{1,0:T(8,128)(2,1)S(1)} %get-tuple-element.65), channel_id=1, source_target_pairs={{0,6},{1,7},{2,4},{3,5},{4,2},{5,3},{6,0},{7,1},{8,14},{9,15},{10,... | collective-permute-start | bytes 393224 | tf_op jit(solution)/shard_map/ppermute | solution.py:33
  97.2 6.4 %weight_gradients.1 = (bf16[2048,2048]{1,0:T(8,128)(2,1)}, bf16[2048,2048]{1,0:T(8,128)(2,1)}) custom-call(bf16[4,32,2048]{2,1,0:T(8,128)(2,1)S(1)} %pad_maximum_fusion.1.refs_8_.mine, bf16[4,32,2048]{2,1,0:T(8,128)(2,1)S(1)} %collective-permute-done.24.theirs, bf16[256,2048]{1,0:T(8,128)(2,1)S(1)} %get-tuple-element.54.gate_term, ...), custom_call_target="tpu_custom_call" | custom-call | flops 4294967296 | bytes 16777216 | tf_op jit(solution)/shard_map/weight_gradients/pallas_call | solution.py:358
  (47 shorter events, 7.0 us)
Async XLA Ops:
  0.6 12.3 %collective-permute-start.1 = (bf16[32,2048]{1,0:T(8,128)(2,1)}, bf16[32,2048]{1,0:T(8,128)(2,1)S(1)}, u32[]{:S(2)}, u32[]{:S(2)}) collective-permute-start(bf16[32,2048]{1,0:T(8,128)(2,1)} %refs_0_.3), channel_id=1, source_target_pairs={{0,4},{1,5},{2,6},{3,7},{4,0},{5,1},{6,2},{7,3},{8,12},{9,13},{10,... | collective-permute-start | bytes 393224 | tf_op jit(solution)/shard_map/ppermute | solution.py:33
  3.7 9.3 %collective-permute-start = (bf16[32,2048]{1,0:T(8,128)(2,1)}, bf16[32,2048]{1,0:T(8,128)(2,1)S(1)}, u32[]{:S(2)}, u32[]{:S(2)}) collective-permute-start(bf16[32,2048]{1,0:T(8,128)(2,1)} %refs_0_.3), channel_id=1, source_target_pairs={{0,2},{1,3},{2,0},{3,1},{4,6},{5,7},{6,4},{7,5},{8,10},{9,11},{10,... | collective-permute-start | bytes 393224 | tf_op jit(solution)/shard_map/ppermute | solution.py:33
  5.2 7.8 %collective-permute-start.2 = (bf16[32,2048]{1,0:T(8,128)(2,1)}, bf16[32,2048]{1,0:T(8,128)(2,1)S(1)}, u32[]{:S(2)}, u32[]{:S(2)}) collective-permute-start(bf16[32,2048]{1,0:T(8,128)(2,1)} %refs_0_.3), channel_id=1, source_target_pairs={{0,6},{1,7},{2,4},{3,5},{4,2},{5,3},{6,0},{7,1},{8,14},{9,15},{10,... | collective-permute-start | bytes 393224 | tf_op jit(solution)/shard_map/ppermute | solution.py:33
  6.3 16.2 %copy-start.1 = (bf16[2,64,2048]{2,1,0:T(8,128)(2,1)}, bf16[2,64,2048]{2,1,0:T(8,128)(2,1)S(1)}, u32[]{:S(2)}) copy-start(bf16[2,64,2048]{2,1,0:T(8,128)(2,1)S(1)} %pad_maximum_fusion.refs_0_) | copy-start | bytes 1572868
  6.3 15.0 %collective-permute-start.5 = (bf16[2,64,2048]{2,1,0:T(8,128)(2,1)S(1)}, bf16[2,64,2048]{2,1,0:T(8,128)(2,1)S(1)}, u32[]{:S(2)}, u32[]{:S(2)}) collective-permute-start(bf16[2,64,2048]{2,1,0:T(8,128)(2,1)S(1)} %pad_maximum_fusion.refs_0_), channel_id=1, source_target_pairs={{8,0},{16,8},{24,16},{9,1},{17,9},{25,17},{10,2},{18,10},{26,18},{... | collective-permute-start | bytes 1572872 | tf_op jit(solution)/shard_map/ppermute | solution.py:83
  7.6 14.9 %collective-permute-start.4 = (bf16[2,64,2048]{2,1,0:T(8,128)(2,1)S(1)}, bf16[2,64,2048]{2,1,0:T(8,128)(2,1)}, u32[]{:S(2)}, u32[]{:S(2)}) collective-permute-start(bf16[2,64,2048]{2,1,0:T(8,128)(2,1)S(1)} %pad_maximum_fusion.refs_0_), channel_id=1, source_target_pairs={{0,8},{8,16},{16,24},{1,9},{9,17},{17,25},{2,10},{10,18},{18,26},{... | collective-permute-start | bytes 1572872 | tf_op jit(solution)/shard_map/ppermute | solution.py:83
  13.0 0.9 copy-start
  13.9 8.6 %collective-permute-start.3 = (bf16[4,32,2048]{2,1,0:T(8,128)(2,1)S(1)}, bf16[4,32,2048]{2,1,0:T(8,128)(2,1)S(1)}, u32[]{:S(2)}, u32[]{:S(2)}) collective-permute-start(bf16[4,32,2048]{2,1,0:T(8,128)(2,1)S(1)} %stacked.1.refs_1_.mine), channel_id=1, source_target_pairs={{0,1},{1,0},{2,3},{3,2},{4,5},{5,4},{6,7},{7,6},{8,9},{9,8},{10,11... | collective-permute-start | bytes 1572872 | tf_op jit(solution)/shard_map/ppermute | solution.py:33
  14.0 24.2 %copy-start.2 = (bf16[32,2048]{1,0:T(8,128)(2,1)S(1)}, bf16[32,2048]{1,0:T(8,128)(2,1)}, u32[]{:S(2)}) copy-start(bf16[32,2048]{1,0:T(8,128)(2,1)} %param.7) | copy-start | bytes 393220
  21.3 1.2 %copy-start.3 = (bf16[2,64,2048]{2,1,0:T(8,128)(2,1)}, bf16[2,64,2048]{2,1,0:T(8,128)(2,1)S(1)}, u32[]{:S(2)}) copy-start(bf16[2,64,2048]{2,1,0:T(8,128)(2,1)S(1)} %collective-permute-done.5.refs_1_.refs_4_) | copy-start | bytes 1572868
  26.2 12.0 %collective-permute-start.7 = (bf16[64,2048]{1,0:T(8,128)(2,1)S(1)}, bf16[64,2048]{1,0:T(8,128)(2,1)S(1)}, u32[]{:S(2)}, u32[]{:S(2)}) collective-permute-start(bf16[64,2048]{1,0:T(8,128)(2,1)S(1)} %get-tuple-element.37), channel_id=1, source_target_pairs={{0,16},{24,8},{1,17},{25,9},{2,18},{26,10},{3,19},{27,11},{4,20},{... | collective-permute-start | bytes 786440 | tf_op jit(solution)/shard_map/ppermute | solution.py:68
  31.9 7.8 %collective-permute-start.9 = (bf16[64,2048]{1,0:T(8,128)(2,1)S(1)}, bf16[64,2048]{1,0:T(8,128)(2,1)S(1)}, u32[]{:S(2)}, u32[]{:S(2)}) collective-permute-start(bf16[64,2048]{1,0:T(8,128)(2,1)S(1)} %get-tuple-element.34), channel_id=1, source_target_pairs={{24,16},{16,8},{25,17},{17,9},{26,18},{18,10},{27,19},{19,11},{28,... | collective-permute-start | bytes 786440 | tf_op jit(solution)/shard_map/ppermute | solution.py:67
  32.6 8.4 %collective-permute-start.6 = (bf16[64,2048]{1,0:T(8,128)(2,1)S(1)}, bf16[64,2048]{1,0:T(8,128)(2,1)S(1)}, u32[]{:S(2)}, u32[]{:S(2)}) collective-permute-start(bf16[64,2048]{1,0:T(8,128)(2,1)S(1)} %get-tuple-element.34), channel_id=1, source_target_pairs={{0,8},{8,16},{1,9},{9,17},{2,10},{10,18},{3,11},{11,19},{4,12},{12... | collective-permute-start | bytes 786440 | tf_op jit(solution)/shard_map/ppermute | solution.py:66
  33.9 16.1 %collective-permute-start.14 = (bf16[2,64,2048]{2,1,0:T(8,128)(2,1)}, bf16[2,64,2048]{2,1,0:T(8,128)(2,1)}, u32[]{:S(2)}, u32[]{:S(2)}) collective-permute-start(bf16[2,64,2048]{2,1,0:T(8,128)(2,1)} %collective-permute-done.4.refs_0_.refs_1_), channel_id=1, source_target_pairs={{8,16},{16,24},{9,17},{17,25},{10,18},{18,26},{11,19},{19,27},{12,... | collective-permute-start | bytes 1572872 | tf_op jit(solution)/shard_map/ppermute | solution.py:83
  35.3 17.3 %collective-permute-start.16 = (bf16[2,64,2048]{2,1,0:T(8,128)(2,1)}, bf16[2,64,2048]{2,1,0:T(8,128)(2,1)}, u32[]{:S(2)}, u32[]{:S(2)}) collective-permute-start(bf16[2,64,2048]{2,1,0:T(8,128)(2,1)} %copy-done.3), channel_id=1, source_target_pairs={{8,0},{16,8},{9,1},{17,9},{10,2},{18,10},{11,3},{19,11},{12,4},{20... | collective-permute-start | bytes 1572872 | tf_op jit(solution)/shard_map/ppermute | solution.py:83
  38.2 10.1 %collective-permute-start.18 = (bf16[1,32,2048]{2,1,0:T(8,128)(2,1)S(1)}, bf16[1,32,2048]{2,1,0:T(8,128)(2,1)S(1)}, u32[]{:S(2)}, u32[]{:S(2)}) collective-permute-start(bf16[1,32,2048]{2,1,0:T(8,128)(2,1)S(1)} %bitcast.4), channel_id=1, source_target_pairs={{0,2},{1,3},{2,0},{3,1},{4,6},{5,7},{6,4},{7,5},{8,10},{9,11},{10,... | collective-permute-start | bytes 393224 | tf_op jit(solution)/shard_map/ppermute | solution.py:33
  41.2 14.2 %collective-permute-start.10 = (bf16[64,2048]{1,0:T(8,128)(2,1)S(1)}, bf16[64,2048]{1,0:T(8,128)(2,1)S(1)}, u32[]{:S(2)}, u32[]{:S(2)}) collective-permute-start(bf16[64,2048]{1,0:T(8,128)(2,1)S(1)} %get-tuple-element.62), channel_id=1, source_target_pairs={{24,16},{16,8},{8,0},{25,17},{17,9},{9,1},{26,18},{18,10},{10,2},{... | collective-permute-start | bytes 786440 | tf_op jit(solution)/shard_map/ppermute | solution.py:75
  42.5 12.9 %collective-permute-start.8 = (bf16[64,2048]{1,0:T(8,128)(2,1)S(1)}, bf16[64,2048]{1,0:T(8,128)(2,1)S(1)}, u32[]{:S(2)}, u32[]{:S(2)}) collective-permute-start(bf16[64,2048]{1,0:T(8,128)(2,1)S(1)} %get-tuple-element.63), channel_id=1, source_target_pairs={{0,8},{8,16},{16,24},{1,9},{9,17},{17,25},{2,10},{10,18},{18,26},{... | collective-permute-start | bytes 786440 | tf_op jit(solution)/shard_map/ppermute | solution.py:74
  48.4 23.6 %collective-permute-start.19 = (bf16[2,32,2048]{2,1,0:T(8,128)(2,1)S(1)}, bf16[2,32,2048]{2,1,0:T(8,128)(2,1)S(1)}, u32[]{:S(2)}, u32[]{:S(2)}) collective-permute-start(bf16[2,32,2048]{2,1,0:T(8,128)(2,1)S(1)} %pad_maximum_fusion.2), channel_id=1, source_target_pairs={{0,4},{1,5},{2,6},{3,7},{4,0},{5,1},{6,2},{7,3},{8,12},{9,13},{10,... | collective-permute-start | bytes 786440 | tf_op jit(solution)/shard_map/ppermute | solution.py:33
  50.0 22.0 %collective-permute-start.15 = (bf16[2,64,2048]{2,1,0:T(8,128)(2,1)}, bf16[2,64,2048]{2,1,0:T(8,128)(2,1)S(1)}, u32[]{:S(2)}, u32[]{:S(2)}) collective-permute-start(bf16[2,64,2048]{2,1,0:T(8,128)(2,1)} %collective-permute-done.14.refs_2_), channel_id=1, source_target_pairs={{16,24},{17,25},{18,26},{19,27},{20,28},{21,29},{22,30},{23,31}} | collective-permute-start | bytes 1572872 | tf_op jit(solution)/shard_map/ppermute | solution.py:83
  52.7 23.6 %collective-permute-start.17 = (bf16[2,64,2048]{2,1,0:T(8,128)(2,1)}, bf16[2,64,2048]{2,1,0:T(8,128)(2,1)S(1)}, u32[]{:S(2)}, u32[]{:S(2)}) collective-permute-start(bf16[2,64,2048]{2,1,0:T(8,128)(2,1)} %collective-permute-done.16.refs_5_), channel_id=1, source_target_pairs={{8,0},{9,1},{10,2},{11,3},{12,4},{13,5},{14,6},{15,7}} | collective-permute-start | bytes 1572872 | tf_op jit(solution)/shard_map/ppermute | solution.py:83
  55.5 16.5 %collective-permute-start.12 = (bf16[64,2048]{1,0:T(8,128)(2,1)S(1)}, bf16[64,2048]{1,0:T(8,128)(2,1)S(1)}, u32[]{:S(2)}, u32[]{:S(2)}) collective-permute-start(bf16[64,2048]{1,0:T(8,128)(2,1)S(1)} %summed.1.refs_2_.refs_0_), channel_id=1, source_target_pairs={{0,16},{8,24},{16,0},{24,8},{1,17},{9,25},{17,1},{25,9},{2,18},{10... | collective-permute-start | bytes 786440 | tf_op jit(solution)/shard_map/ppermute | solution.py:33
  61.5 21.2 %collective-permute-start.11 = (bf16[64,2048]{1,0:T(8,128)(2,1)S(1)}, bf16[64,2048]{1,0:T(8,128)(2,1)S(1)}, u32[]{:S(2)}, u32[]{:S(2)}) collective-permute-start(bf16[64,2048]{1,0:T(8,128)(2,1)S(1)} %summed.1.refs_2_.refs_0_), channel_id=1, source_target_pairs={{0,8},{8,0},{16,24},{24,16},{1,9},{9,1},{17,25},{25,17},{2,10},{10... | collective-permute-start | bytes 786440 | tf_op jit(solution)/shard_map/ppermute | solution.py:33
  71.9 13.1 %collective-permute-start.13 = (bf16[64,2048]{1,0:T(8,128)(2,1)S(1)}, bf16[64,2048]{1,0:T(8,128)(2,1)S(1)}, u32[]{:S(2)}, u32[]{:S(2)}) collective-permute-start(bf16[64,2048]{1,0:T(8,128)(2,1)S(1)} %collective-permute-done.12.refs_8_.refs_2_), channel_id=1, source_target_pairs={{0,8},{8,0},{16,24},{24,16},{1,9},{9,1},{17,25},{25,17},{2,10},{10... | collective-permute-start | bytes 786440 | tf_op jit(solution)/shard_map/ppermute | solution.py:33
  90.7 2.7 %collective-permute-start.20 = (f32[128,2048]{1,0:T(8,128)S(1)}, f32[128,2048]{1,0:T(8,128)S(1)}, u32[]{:S(2)}, u32[]{:S(2)}) collective-permute-start(f32[128,2048]{1,0:T(8,128)S(1)} %get-tuple-element.51), channel_id=1, source_target_pairs={{0,1},{1,0},{2,3},{3,2},{4,5},{5,4},{6,7},{7,6},{8,9},{9,8},{10,11... | collective-permute-start | bytes 3145736 | tf_op jit(solution)/shard_map/ppermute | solution.py:33
  90.7 6.4 %collective-permute-start.24 = (bf16[4,32,2048]{2,1,0:T(8,128)(2,1)S(1)}, bf16[4,32,2048]{2,1,0:T(8,128)(2,1)S(1)}, u32[]{:S(2)}, u32[]{:S(2)}) collective-permute-start(bf16[4,32,2048]{2,1,0:T(8,128)(2,1)S(1)} %pad_maximum_fusion.1.refs_8_.mine), channel_id=1, source_target_pairs={{0,1},{1,0},{2,3},{3,2},{4,5},{5,4},{6,7},{7,6},{8,9},{9,8},{10,11... | collective-permute-start | bytes 1572872 | tf_op jit(solution)/shard_map/ppermute | solution.py:33
  93.6 10.0 %collective-permute-start.21 = (bf16[32,2048]{1,0:T(8,128)(2,1)S(1)}, bf16[32,2048]{1,0:T(8,128)(2,1)S(1)}, u32[]{:S(2)}, u32[]{:S(2)}) collective-permute-start(bf16[32,2048]{1,0:T(8,128)(2,1)S(1)} %get-tuple-element.64), channel_id=1, source_target_pairs={{0,2},{1,3},{2,0},{3,1},{4,6},{5,7},{6,4},{7,5},{8,10},{9,11},{10,... | collective-permute-start | bytes 393224 | tf_op jit(solution)/shard_map/ppermute | solution.py:33
  94.8 8.8 %collective-permute-start.23 = (bf16[32,2048]{1,0:T(8,128)(2,1)S(1)}, bf16[32,2048]{1,0:T(8,128)(2,1)S(1)}, u32[]{:S(2)}, u32[]{:S(2)}) collective-permute-start(bf16[32,2048]{1,0:T(8,128)(2,1)S(1)} %get-tuple-element.65), channel_id=1, source_target_pairs={{0,6},{1,7},{2,4},{3,5},{4,2},{5,3},{6,0},{7,1},{8,14},{9,15},{10,... | collective-permute-start | bytes 393224 | tf_op jit(solution)/shard_map/ppermute | solution.py:33
  96.2 7.8 %collective-permute-start.22 = (bf16[32,2048]{1,0:T(8,128)(2,1)S(1)}, bf16[32,2048]{1,0:T(8,128)(2,1)S(1)}, u32[]{:S(2)}, u32[]{:S(2)}) collective-permute-start(bf16[32,2048]{1,0:T(8,128)(2,1)S(1)} %get-tuple-element.66), channel_id=1, source_target_pairs={{0,4},{1,5},{2,6},{3,7},{4,0},{5,1},{6,2},{7,3},{8,12},{9,13},{10,... | collective-permute-start | bytes 393224 | tf_op jit(solution)/shard_map/ppermute | solution.py:33
